TPU v7x, 512 devices: a whole 4x4x16 slice. The times are simulated.
512 devices in a mesh: dp: 32 (over z_hi, x, y), code: 16 (over z_lo, core).
Axes of the slice: x: 4, y: 4, z: 16 (z_hi: 2, z_lo: 8; z = z_hi * 8 + z_lo), core: 2. Of those that a mesh axis runs over, the one named last changes fastest.
Arguments:
- latents: bfloat16 [524288, 256], P(('dp', 'code')), may hold values from -6 to 6
- batch_order: int32 [512, 1024], P(('dp', 'code')), may hold values from 0 to 1023, each once within a row
- code_block: int32 [524288, 1], P(('dp', 'code')), may hold values from 0 to 511; in each aligned block of 512 rows (0 to 511, 512 to 1023, ...) at most 2 rows name the same one
- code_offset: int32 [524288], P(('dp', 'code')), may hold values from 0 to 255
- ema_counts: float32 [131072], P(('dp', 'code')), may hold values from 0.5 to 8
- ema_sums: float32 [131072, 256], P(('dp', 'code')), may hold values from -6 to 6
- queries: bfloat16 [32768, 256], P('dp'), may hold values from -6 to 6
Outputs:
- codebook: float32 [131072, 256], P(('dp', 'code'))
- new_counts: float32 [131072], P(('dp', 'code'))
- new_sums: float32 [131072, 256], P(('dp', 'code'))
- nearest: float32 [32768], P('dp')
Inputs may be any that keep to these rules, and one draw needn't show every extreme that they name: `code_block`: in each aligned block of 512 rows (one device's batch of one step) no code block is named more than 2 times, and in every draw some block names one code block exactly 2 times. Each row of batch_order names every number of 0 to 1023 once.
All inputs are finite; a program needn't handle non-finite values.
Results may differ from a plain program's by a relative error of at most 0.0009.
Values may be sent and summed in bfloat16 or wider, within the bound.
No kernel may reach another device: no remote copies, remote signals or barrier semaphores. Data moves between devices by JAX's collectives and lax.ppermute only.
A program may use at most 64 MiB of HBM per device.

v0:
```python
import math

import jax
import jax.numpy as jnp
from jax import lax
from jax.sharding import PartitionSpec as P

E = 256
CPD = 256
STEPS = 2


ema_decay = 0.9


def closest_codes(query_rows, code_rows):
    total_rows = query_rows.shape[0]
    block_rows = math.gcd(total_rows, 512)
    code_norms = jnp.sum(jnp.square(code_rows.astype(jnp.float32)), axis=1)

    def block_minimum(query_block):
        products = lax.dot_general(
            query_block, code_rows, (((1,), (1,)), ((), ())), preferred_element_type=jnp.float32
        )
        own_norms = jnp.sum(jnp.square(query_block.astype(jnp.float32)), axis=1)
        distance = (own_norms[:, None] + code_norms[None, :] - 2.0 * products) / E
        return jnp.min(distance, axis=1)

    blocks = query_rows.reshape(total_rows // block_rows, block_rows, E)
    return lax.map(block_minimum, blocks).reshape(total_rows)


def body(latents, batch_order, code_block, code_offset, ema_counts, ema_sums, queries):
    dp_size = lax.axis_size("dp")
    code_size = lax.axis_size("code")
    devices = dp_size * code_size
    tok_rows = latents.shape[0] // STEPS
    capacity = max(2, 2 * tok_rows // devices)
    batched = latents[batch_order.reshape(-1)]
    owners = code_block.reshape(STEPS, tok_rows)
    owner_table = (
        owners[:, :, None] == jnp.arange(devices, dtype=jnp.int32)[None, None, :]
    ).astype(jnp.bfloat16)
    positions = jnp.arange(tok_rows, dtype=jnp.int32)
    lower_mask = (positions[:, None] > positions[None, :]).astype(jnp.bfloat16)
    earlier = jnp.einsum("pq,sqd->spd", lower_mask, owner_table, preferred_element_type=jnp.float32)
    slot_rank = jnp.sum(earlier * owner_table, axis=2).astype(jnp.int32)
    step_ids = jnp.arange(STEPS, dtype=jnp.int32)[:, None]
    destination = ((owners * STEPS + step_ids) * capacity + slot_rank).reshape(-1)
    slot_total = devices * STEPS * capacity
    send_rows = jnp.zeros((slot_total, E), jnp.bfloat16).at[destination].set(batched)
    send_offsets = jnp.full((slot_total,), -1, jnp.int32).at[destination].set(code_offset)
    send_rows = send_rows.reshape(dp_size, code_size, STEPS, capacity, E)
    send_offsets = send_offsets.reshape(dp_size, code_size, STEPS, capacity)
    got_rows, got_offsets = (
        lax.all_to_all(
            lax.all_to_all(send_rows, "dp", split_axis=0, concat_axis=0, tiled=True),
            "code",
            split_axis=1,
            concat_axis=1,
            tiled=True,
        ),
        lax.all_to_all(
            lax.all_to_all(send_offsets, "dp", split_axis=0, concat_axis=0, tiled=True),
            "code",
            split_axis=1,
            concat_axis=1,
            tiled=True,
        ),
    )
    local_codes = jnp.arange(CPD, dtype=jnp.int32)
    counts_now = ema_counts
    sums_now = ema_sums
    for step_index in range(STEPS):
        step_rows = got_rows[:, :, step_index].reshape(-1, E)
        step_offsets = got_offsets[:, :, step_index].reshape(-1)
        hit_table = (step_offsets[:, None] == local_codes[None, :]).astype(jnp.bfloat16)
        step_sums = jnp.einsum(
            "rk,re->ke", hit_table, step_rows, preferred_element_type=jnp.float32
        )
        step_counts = jnp.sum(hit_table.astype(jnp.float32), axis=0)
        counts_now = ema_decay * counts_now + (1.0 - ema_decay) * step_counts
        sums_now = ema_decay * sums_now + (1.0 - ema_decay) * step_sums
    codebook = sums_now / counts_now[:, None]
    rounded = codebook.astype(jnp.bfloat16)
    start_min = jnp.full((queries.shape[0],), 3e38, jnp.float32)
    partial_value = jnp.minimum(
        start_min, closest_codes(queries, lax.all_gather(rounded, "dp", axis=0, tiled=True))
    )
    nearest = lax.pmin(partial_value, "code")
    return (codebook, counts_now, sums_now, nearest)


def solution(mesh):
    placed = (
        P(("dp", "code"), None),
        P(("dp", "code"), None),
        P(("dp", "code"), None),
        P(("dp", "code")),
        P(("dp", "code")),
        P(("dp", "code"), None),
        P("dp", None),
    )
    return jax.shard_map(
        body,
        mesh=mesh,
        in_specs=placed,
        out_specs=(P(("dp", "code"), None), P(("dp", "code")), P(("dp", "code"), None), P("dp")),
        check_vma=False,
    )
```

profile of v0, /device:TPU:1, one launch (start us, length us, event | category | flops | bytes accessed | tf_op | source)
XLA Modules:
  0.0 421.1 jit_solution(5931519551796506416)
XLA Ops:
  7.2 0.0 copy-start
  7.2 0.0 copy-start.2
  7.2 0.5 broadcast.79
  7.7 1.3 reduce.3
  9.1 0.9 fusion.3
  10.0 0.7 compare_select_fusion.1
  10.7 4.5 %scatter_custom_fusion = s32[2048]{0:T(1024)S(1)} fusion(s32[1024]{0:T(1024)S(1)} %bitcast.64, s32[1024]{0:T(1024)} %param.12, s32[]{:T(128)} %constant.6.clone.1), kind=kCustom, calls=%fused_computation.39 | custom fusion | bytes 8704 | tf_op jit(solution)/shard_map/scatter | solution.py:52
  15.2 0.8 reshape.74
  16.0 1.1 copy.22
  17.1 21.1 %all-to-all-start = ((s32[32,16,2,2]{1,3,2,0:T(2,128)}), s32[32,16,2,2]{1,3,2,0:T(2,128)S(1)}, u32[]{:S(2)}, u32[]{:S(2)}) async-start(s32[32,16,2,2]{1,3,2,0:T(2,128)} %copy.22), calls=%async_computation | async-start | bytes 131072 | tf_op jit(solution)/shard_map/all_to_all | solution.py:64
  38.2 0.0 copy-done.2
  38.2 0.0 copy-done
  38.2 8.5 %scatter_custom_fusion.1 = bf16[2048,256]{1,0:T(8,128)(2,1)S(1)} fusion(s32[1024]{0:T(1024)S(1)} %bitcast.65, bf16[1024,256]{1,0:T(8,128)(2,1)S(1)} %copy-done, s32[1024]{0:T(1024)S(1)} %broadcast_clamp_fusion, bf16[]{:T(256)} %constant.10.clone.1), kind=kCustom, calls=%fused_computation.28 | custom fusion | bytes 1048578 | tf_op jit(solution)/shard_map/scatter | solution.py:51
  46.8 1.2 reshape.76
  48.0 0.0 copy-start.3
  48.0 6.1 %all-to-all-done = s32[32,16,2,2]{1,3,2,0:T(2,128)S(1)} async-done(((s32[32,16,2,2]{1,3,2,0:T(2,128)}), s32[32,16,2,2]{1,3,2,0:T(2,128)S(1)}, u32[]{:S(2)}, u32[]{:S(2)}) %all-to-all-start) | async-done | bytes 8224 | tf_op jit(solution)/shard_map/all_to_all | solution.py:64
  54.1 10.5 %all-to-all-start.2 = ((bf16[32,16,2,2,256]{4,3,2,1,0:T(2,128)(2,1)}), bf16[32,16,2,2,256]{4,3,2,1,0:T(2,128)(2,1)S(1)}, u32[]{:S(2)}, u32[]{:S(2)}) async-start(bf16[32,16,2,2,256]{4,3,2,1,0:T(2,128)(2,1)} %reshape.76), calls=%async_computation.2 | async-start | bytes 2097152 | tf_op jit(solution)/shard_map/all_to_all | solution.py:57
  64.6 0.1 copy.23
  64.7 0.7 reshape.120
  65.4 27.0 %all-to-all-done.2 = bf16[32,16,2,2,256]{4,3,2,1,0:T(2,128)(2,1)S(1)} async-done(((bf16[32,16,2,2,256]{4,3,2,1,0:T(2,128)(2,1)}), bf16[32,16,2,2,256]{4,3,2,1,0:T(2,128)(2,1)S(1)}, u32[]{:S(2)}, u32[]{:S(2)}) %all-to-all-start.2) | async-done | bytes 1048608 | tf_op jit(solution)/shard_map/all_to_all | solution.py:57
  92.5 36.4 %all-to-all-start.1 = ((s32[16,1,128]{2,1,0:T(1,128)}), s32[16,1,128]{2,1,0:T(1,128)S(1)}, u32[]{:S(2)}, u32[]{:S(2)}) async-start(s32[16,1,128]{2,1,0:T(1,128)} %reshape.120), calls=%async_computation.1 | async-start | bytes 16384 | tf_op jit(solution)/shard_map/all_to_all | solution.py:63
  128.9 2.0 copy.25
  130.9 7.6 %all-to-all-done.1 = s32[16,1,128]{2,1,0:T(1,128)S(1)} async-done(((s32[16,1,128]{2,1,0:T(1,128)}), s32[16,1,128]{2,1,0:T(1,128)S(1)}, u32[]{:S(2)}, u32[]{:S(2)}) %all-to-all-start.1) | async-done | bytes 8224 | tf_op jit(solution)/shard_map/all_to_all | solution.py:63
  138.5 4.2 all-to-all-start.3
  142.7 0.2 all-gather.2.cloned.1.call-start
  142.9 0.5 broadcast.80
  143.5 0.7 reduce.4
  144.1 0.1 reshape.121
  144.2 0.0 copy-start.5
  144.3 0.2 copy.24
  144.5 0.2 eq.49
  144.6 0.2 copy.27
  144.8 0.2 eq.53
  145.0 0.4 convert_reduce_fusion
  145.4 0.0 copy-done.3
  145.4 0.0 copy-start.4
  145.4 41.8 %all-to-all-done.3 = bf16[32,16,2,2,256]{4,3,2,0,1:T(2,128)(2,1)S(1)} async-done(((bf16[32,16,2,2,256]{4,3,2,0,1:T(2,128)(2,1)}), bf16[32,16,2,2,256]{4,3,2,0,1:T(2,128)(2,1)S(1)}, u32[]{:S(2)}, u32[]{:S(2)}) %all-to-all-start.3) | async-done | bytes 1048608 | tf_op jit(solution)/shard_map/all_to_all | solution.py:56
  187.2 0.7 fusion.22
  187.9 0.5 copy.28
  188.5 0.2 reshape_squeeze.7
  188.7 0.6 convolution_multiply_fusion
  189.3 0.0 copy-start.1
  189.3 0.5 copy.26
  189.9 0.2 reshape_squeeze.6
  190.1 0.0 copy-done.5
  190.1 1.4 fusion.21
  191.5 0.0 copy-done.4
  191.5 0.0 all-gather.2.cloned.1.call-update
  191.6 157.3 %all-gather.2.cloned.1.call-done = bf16[8192,256]{1,0:T(8,128)(2,1)} async-done(((bf16[256,256]{1,0:T(8,128)(2,1)}), bf16[8192,256]{1,0:T(8,128)(2,1)}) %all-gather.2.cloned.1.call-update) | async-done | bytes 4194320 | tf_op jit(solution)/shard_map/all_gather | solution.py:88
  348.9 3.3 multiply_reduce_fusion.2
  352.2 0.0 copy-done.1
  352.3 11.7 %while.10 = (s32[]{:T(128)}, f32[2,512]{1,0:T(2,128)S(1)}, bf16[2,512,256]{2,1,0:T(8,128)(2,1)S(1)}, f32[8192]{0:T(1024)S(1)}, bf16[8192,256]{1,0:T(8,128)(2,1)}, /*index=5*/s32[]{:T(128)}, s32[]{:T(128)}) while((s32[]{:T(128)}, f32[2,512]{1,0:T(2,128)S(1)}, bf16[2,512,256]{2,1,0:T(8,128)(2,1)S(1)}, f32[8192]{0:T(1024)S(1)}, ...), condition=%wide.region_9.10_spmd, body=%wide.region_6.9_spmd.sunk | while | flops 2168847360 | bytes 4761689 | solution.py:30
  352.3 0.2 multiply_reduce_fusion.5
  352.4 5.6 %multiply_reduce_fusion.6 = f32[512]{0:T(512)S(1)} fusion(bf16[8192,256]{1,0:T(8,128)(2,1)} %get-tuple-element.100, f32[8192]{0:T(1024)S(1)} %get-tuple-element.99, f32[512]{0:T(512)S(1)} %multiply_reduce_fusion.5, bf16[2,512,256]{2,1,0:T(8,128)(2,1)S(1)} %get-tuple-element.98, s32[]{:T(128)} %get-tuple-element.89), kind=kOutput, calls=%fused_computation.3.clone.1 | convolution fusion | flops 2168454656 | bytes 4493316 | tf_op jit(solution)/shard_map/while/body/eval_jaxpr/dot_general | solution.py:22
  358.1 0.2 multiply_reduce_fusion.5
  358.3 5.6 %multiply_reduce_fusion.6 = f32[512]{0:T(512)S(1)} fusion(bf16[8192,256]{1,0:T(8,128)(2,1)} %get-tuple-element.100, f32[8192]{0:T(1024)S(1)} %get-tuple-element.99, f32[512]{0:T(512)S(1)} %multiply_reduce_fusion.5, bf16[2,512,256]{2,1,0:T(8,128)(2,1)S(1)} %get-tuple-element.98, s32[]{:T(128)} %get-tuple-element.89), kind=kOutput, calls=%fused_computation.3.clone.1 | convolution fusion | flops 2168454656 | bytes 4493316 | tf_op jit(solution)/shard_map/while/body/eval_jaxpr/dot_general | solution.py:22
  364.0 50.3 %pmin.7 = f32[1024]{0:T(1024)} all-reduce(f32[1024]{0:T(1024)S(1)} %bitcast.60), channel_id=1, replica_groups=mesh['dp'=32,'code'=16] {'code'}, use_global_device_ids=true, to_apply=%region_10.11 | all-reduce | flops 1024 | bytes 8192 | tf_op jit(solution)/shard_map/pmin | solution.py:90
  (14 shorter events, 0.2 us)
Async XLA Ops:
  7.2 31.1 %copy-start = (bf16[1024,256]{1,0:T(8,128)(2,1)S(1)}, bf16[1024,256]{1,0:T(8,128)(2,1)}, u32[]{:S(2)}) copy-start(bf16[1024,256]{1,0:T(8,128)(2,1)} %param.9) | copy-start | bytes 1572868
  7.2 31.0 %copy-start.2 = (s32[1,1024]{1,0:T(1,128)S(1)}, s32[1,1024]{1,0:T(1,128)}, u32[]{:S(2)}) copy-start(s32[1,1024]{1,0:T(1,128)} %param.10) | copy-start | bytes 12292
  17.1 37.0 %all-to-all-start = ((s32[32,16,2,2]{1,3,2,0:T(2,128)}), s32[32,16,2,2]{1,3,2,0:T(2,128)S(1)}, u32[]{:S(2)}, u32[]{:S(2)}) async-start(s32[32,16,2,2]{1,3,2,0:T(2,128)} %copy.22), calls=%async_computation | async-start | bytes 131072 | tf_op jit(solution)/shard_map/all_to_all | solution.py:64
  48.0 97.4 %copy-start.3 = (f32[256]{0:T(256)S(1)}, f32[256]{0:T(256)}, u32[]{:S(2)}) copy-start(f32[256]{0:T(256)} %param.13) | copy-start | bytes 3076
  54.1 38.4 %all-to-all-start.2 = ((bf16[32,16,2,2,256]{4,3,2,1,0:T(2,128)(2,1)}), bf16[32,16,2,2,256]{4,3,2,1,0:T(2,128)(2,1)S(1)}, u32[]{:S(2)}, u32[]{:S(2)}) async-start(bf16[32,16,2,2,256]{4,3,2,1,0:T(2,128)(2,1)} %reshape.76), calls=%async_computation.2 | async-start | bytes 2097152 | tf_op jit(solution)/shard_map/all_to_all | solution.py:57
  92.5 46.1 %all-to-all-start.1 = ((s32[16,1,128]{2,1,0:T(1,128)}), s32[16,1,128]{2,1,0:T(1,128)S(1)}, u32[]{:S(2)}, u32[]{:S(2)}) async-start(s32[16,1,128]{2,1,0:T(1,128)} %reshape.120), calls=%async_computation.1 | async-start | bytes 16384 | tf_op jit(solution)/shard_map/all_to_all | solution.py:63
  138.5 48.7 %all-to-all-start.3 = ((bf16[32,16,2,2,256]{4,3,2,0,1:T(2,128)(2,1)}), bf16[32,16,2,2,256]{4,3,2,0,1:T(2,128)(2,1)S(1)}, u32[]{:S(2)}, u32[]{:S(2)}) async-start(bf16[32,16,2,2,256]{4,3,2,0,1:T(2,128)(2,1)} %copy.25), calls=%async_computation.3 | async-start | bytes 2097152 | tf_op jit(solution)/shard_map/all_to_all | solution.py:56
  142.7 206.2 %all-gather.2.cloned.1.call-start = ((), (), s32[]{:S(2)}) async-start(), calls=%async_computation.4 | async-start | bytes 4325376 | tf_op jit(solution)/shard_map/all_gather | solution.py:88
  144.2 45.8 %copy-start.5 = (f32[256,256]{1,0:T(8,128)S(1)}, f32[256,256]{1,0:T(8,128)}, u32[]{:S(2)}) copy-start(f32[256,256]{1,0:T(8,128)} %param.14) | copy-start | bytes 786436
  145.4 46.1 %copy-start.4 = (f32[256]{0:T(256)}, f32[256]{0:T(256)S(1)}, u32[]{:S(2)}) copy-start(f32[256]{0:T(256)S(1)} %multiply_add_fusion) | copy-start | bytes 3076
  189.3 162.9 %copy-start.1 = (bf16[1024,256]{1,0:T(8,128)(2,1)S(1)}, bf16[1024,256]{1,0:T(8,128)(2,1)}, u32[]{:S(2)}) copy-start(bf16[1024,256]{1,0:T(8,128)(2,1)} %param.15) | copy-start | bytes 1572868
Sparse Core Ops, SparseCore 0:
  191.7 157.1 all-gather.1
where the time goes:
time: 423 us; the launch traced here: 421 us
  waiting for transfers between devices  240 us (57%)
  starting transfers between devices  72.5 us (17%)
  blocking collectives  50.3 us (12%)
  local copies, waits for them, and re-layouts  23.1 us (5%)
  between operations  14.4 us (3%)
  matrix products  14.2 us (3%)
  other arithmetic  6.75 us (2%)
    all_gather x1, waiting for transfers between devices, body(): lax.all_gather(rounded, 'dp', axis=0, tiled=True)  157 us
    pmin x1, blocking collectives, body(): nearest = lax.pmin(partial_value, 'code')  50.3 us
    all_to_all x1, waiting for transfers between devices, body(): lax.all_to_all(lax.all_to_all(send_rows, 'dp', split_axis=0, concat_axis=...  41.8 us
    all_to_all x1, starting transfers between devices, body(): lax.all_to_all(lax.all_to_all(send_offsets, 'dp', split_axis=0, concat_ax...  36.4 us
    all_to_all x1, waiting for transfers between devices, body(): lax.all_to_all(send_rows, 'dp', split_axis=0, concat_axis=0, tiled=True)  27 us
    all_to_all x1, starting transfers between devices, body(): lax.all_to_all(send_offsets, 'dp', split_axis=0, concat_axis=0, tiled=True)  21.1 us
    dot_general x2, matrix products, block_minimum(): lax.dot_general(query_block, code_rows, (((1,), (1,)), ((), ())), preferr...  11.3 us
    all_to_all x1, starting transfers between devices, body(): lax.all_to_all(send_rows, 'dp', split_axis=0, concat_axis=0, tiled=True)  10.5 us
  transfers between devices with their start and end apart: 5, of which 5 were waited for; matrix products, arithmetic and copies ran while one was open for 4% of the time, Pallas kernels for 0%

commit v1 on v0

v1 whole, which is shorter than its diff:
```python
import jax
import jax.numpy as jnp
from jax import lax
from jax.experimental import pallas as pl
from jax.experimental.pallas import tpu as pltpu
from jax.sharding import Mesh, PartitionSpec as P

E = 256
CPD = 256
STEPS = 2
CAP = 2
SLOTS = STEPS * CAP
ema_decay = 0.9

AXES = ("zh", "x", "y", "zl", "core")
SIZES = (2, 4, 4, 8, 2)
PARTNERS = ("x", "y", "core", "zh", "zl")
NT = (((1,), (1,)), ((), ()))

f32 = jnp.float32
bf16 = jnp.bfloat16
i32 = jnp.int32


def iota(shape, dim):
    return lax.broadcasted_iota(i32, shape, dim)


def one_hot(hit):
    return jnp.where(hit, 1.0, 0.0).astype(bf16)


def build_kernel(latents_ref, order_ref, block_ref, offset_ref, rows_ref, table_ref):
    tokens = latents_ref.shape[0]
    step = tokens // STEPS
    block = block_ref[...]
    earlier = one_hot(iota((step, step), 0) < iota((step, step), 1))
    ranks = []
    for t in range(STEPS):
        own = iota((512, step), 0) == block[:, t * step : (t + 1) * step]
        counts = jnp.dot(one_hot(own), earlier, preferred_element_type=f32)
        ranks.append(jnp.sum(jnp.where(own, counts, 0.0), axis=0, keepdims=True))
    rank = jnp.concatenate(ranks, axis=1).astype(i32)
    position = iota((1, tokens), 1)
    slot = jnp.where(position >= step, CAP, 0) + rank
    z_row = ((block >> 8) << 3) | ((block >> 1) & 7)
    plane = (((block >> 4) & 15) << 1) | (block & 1)
    place = (plane * 16 + z_row) * SLOTS + slot
    code = (offset_ref[...] + 1).astype(f32)
    rows_hit = jnp.where(iota((16, tokens), 0) == z_row, code, 0.0).astype(bf16)
    lanes_hit = one_hot(iota((128, tokens), 0) == plane * SLOTS + slot)
    table_ref[...] = lax.dot_general(rows_hit, lanes_hit, NT, preferred_element_type=f32)
    digits = jnp.where(iota((8, tokens), 0) == 0, place >> 6, place & 63).astype(f32).astype(bf16)
    stored = one_hot(iota((tokens, tokens), 0) == order_ref[...])
    pair = lax.dot_general(digits, stored, NT, preferred_element_type=f32).astype(i32)
    place = pair[0:1] * 64 + pair[1:2]
    latents = latents_ref[...]
    chunk = 512
    low = iota((chunk // 8, 8, 128), 1) < 4
    for c in range(512 * SLOTS // chunk):
        pick = one_hot(iota((chunk, tokens), 0) + c * chunk == place)
        got = jnp.dot(pick, latents, preferred_element_type=f32)
        a = got[:, :128].reshape(chunk // 8, 8, 128)
        b = got[:, 128:].reshape(chunk // 8, 8, 128)
        first = jnp.where(low, a, pltpu.roll(b, 4, 1))
        second = jnp.where(low, pltpu.roll(a, 4, 1), b)
        both = jnp.stack([first, second], axis=1).reshape(chunk // 4, 8, 128)
        rows_ref[c * (chunk // 4) : (c + 1) * (chunk // 4)] = both.astype(bf16)


def build(latents, order, block, offset):
    return pl.pallas_call(
        build_kernel,
        out_shape=(
            jax.ShapeDtypeStruct((512, 8, 128), bf16),
            jax.ShapeDtypeStruct((16, 128), f32),
        ),
        compiler_params=pltpu.CompilerParams(vmem_limit_bytes=48 << 20),
        cost_estimate=pl.CostEstimate(flops=3 << 30, bytes_accessed=2 << 20, transcendentals=0),
        name="build",
    )(latents, order, block, offset)


def update_kernel(mine_ref, rows_ref, table_ref, count_col_ref, count_row_ref, sums_ref,
                  codebook_ref, counts_ref, new_sums_ref, rounded_ref, hit_ref):
    mine = mine_ref[0]
    lane = iota((512, 128), 1)
    table = jnp.where((lane >> 2) == mine, table_ref[...], 0.0).astype(bf16)
    spread = one_hot((iota((128, 128), 0) & 3) == (iota((128, 128), 1) & 3))
    spread = jnp.dot(table, spread, preferred_element_type=f32)
    keep = (iota((512, 128), 0) & 31) == (lane >> 2)
    code = jnp.sum(jnp.where(keep, spread, 0.0).reshape(16, 32, 128), axis=1).astype(i32)
    local = iota((2 * CPD, 128), 0)
    step = ((iota((2 * CPD, 128), 1) & 3) >> 1) == (local >> 8)
    local = jnp.where(step, (local & 255) + 1, -1)
    for i in range(16):
        hit_ref[:, i * 128 : (i + 1) * 128] = one_hot(local == code[i : i + 1])
    pairs = rows_ref[...].astype(f32).reshape(256, 2, 8, 128)
    first, second = pairs[:, 0], pairs[:, 1]
    low = iota((256, 8, 128), 1) < 4
    left = jnp.where(low, first, pltpu.roll(second, 4, 1)).reshape(2048, 128)
    right = jnp.where(low, pltpu.roll(first, 4, 1), second).reshape(2048, 128)
    hits = hit_ref[...]
    sums_left = jnp.dot(hits, left.astype(bf16), preferred_element_type=f32)
    sums_right = jnp.dot(hits, right.astype(bf16), preferred_element_type=f32)
    step_sums = jnp.concatenate([sums_left, sums_right], axis=1)
    step_cols = jnp.dot(hits, jnp.ones((2048, 128), bf16), preferred_element_type=f32)
    step_rows = lax.dot_general(jnp.ones((8, 2048), bf16), hits, NT, preferred_element_type=f32)
    sums = sums_ref[...]
    cols = count_col_ref[...]
    rows = count_row_ref[...]
    for t in range(STEPS):
        part = slice(t * CPD, (t + 1) * CPD)
        sums = ema_decay * sums + (1.0 - ema_decay) * step_sums[part]
        cols = ema_decay * cols + (1.0 - ema_decay) * step_cols[part, 0:1]
        rows = ema_decay * rows + (1.0 - ema_decay) * step_rows[0:1, part]
    book = sums / cols
    codebook_ref[...] = book
    rounded_ref[...] = book.astype(bf16)
    new_sums_ref[...] = sums
    counts_ref[...] = rows


def update(mine, rows, table, counts, sums):
    vmem = pl.BlockSpec(memory_space=pltpu.VMEM)
    return pl.pallas_call(
        update_kernel,
        out_shape=(
            jax.ShapeDtypeStruct((CPD, E), f32),
            jax.ShapeDtypeStruct((1, CPD), f32),
            jax.ShapeDtypeStruct((CPD, E), f32),
            jax.ShapeDtypeStruct((CPD, E), bf16),
        ),
        in_specs=[pl.BlockSpec(memory_space=pltpu.SMEM)] + [vmem] * 5,
        out_specs=(vmem,) * 4,
        scratch_shapes=[pltpu.VMEM((2 * CPD, 2048), bf16)],
        compiler_params=pltpu.CompilerParams(vmem_limit_bytes=48 << 20),
        cost_estimate=pl.CostEstimate(flops=1 << 30, bytes_accessed=3 << 20, transcendentals=0),
        name="update",
    )(mine, rows, table, counts.reshape(CPD, 1), counts.reshape(1, CPD), sums)


def nearest_kernel(codes_ref, queries_ref, out_ref, best_ref):
    groups, width = out_ref.shape
    tile = 256
    for c in range(codes_ref.shape[0] // tile):
        codes = codes_ref[c * tile : (c + 1) * tile].astype(f32)
        norms = jnp.sum(codes * codes, axis=1, keepdims=True)
        scaled = (-2.0 * codes).astype(bf16)
        for g in range(groups):
            part = queries_ref[g * width : (g + 1) * width]
            value = lax.dot_general(scaled, part, NT, preferred_element_type=f32) + norms
            value = jnp.min(value.reshape(tile // 8, 8, width), axis=0)
            best_ref[g] = value if c == 0 else jnp.minimum(best_ref[g], value)
    for g in range(groups):
        out_ref[g : g + 1] = jnp.min(best_ref[g], axis=0, keepdims=True)


def nearest_codes(codes, queries):
    return pl.pallas_call(
        nearest_kernel,
        out_shape=jax.ShapeDtypeStruct((8, 512), f32),
        scratch_shapes=[pltpu.VMEM((8, 8, 512), f32)],
        compiler_params=pltpu.CompilerParams(vmem_limit_bytes=48 << 20),
        cost_estimate=pl.CostEstimate(flops=5 << 30, bytes_accessed=3 << 20, transcendentals=0),
        name="nearest",
    )(codes, queries)


def gather_queries(queries):
    share = queries.shape[0] // 8
    slice_ = lax.dynamic_slice_in_dim(queries, lax.axis_index("zl") * share, share, 0)
    both = lax.all_gather(slice_, ("zh", "zl"), axis=0, tiled=True)
    half = queries.shape[0] // 2
    both = both.reshape(2, 2 * half, E)
    mine = lax.dynamic_slice_in_dim(both, lax.axis_index("core") * half, half, 1)
    return lax.all_gather(mine.reshape(2 * half, E), "y", axis=0, tiled=True)


def body(latents, batch_order, code_block, code_offset, ema_counts, ema_sums, queries):
    batch_queries = gather_queries(queries)
    own = jnp.sum(jnp.square(queries.astype(f32)), axis=1)
    rows, table = build(
        latents, batch_order, code_block.reshape(1, -1), code_offset.reshape(1, -1)
    )
    got = lax.all_to_all(rows, PARTNERS, 0, 0, tiled=True)
    z_table = lax.all_to_all(table, ("zh", "zl"), 0, 0, tiled=True)
    tables = lax.all_gather(z_table, ("x", "y", "core"), axis=0, tiled=True)
    mine = lax.axis_index(("x", "y", "core")).astype(i32).reshape(1)
    codebook, counts, sums, rounded = update(mine, got, tables, ema_counts, ema_sums)
    codes = lax.all_gather(rounded, "x", axis=0, tiled=True)
    other = lax.ppermute(codes, "core", [(0, 1), (1, 0)])
    codes = jnp.concatenate([codes, other], axis=0)
    best = nearest_codes(codes, batch_queries)
    sent = jnp.broadcast_to(best[:, None, :], (8, 8, 512)).reshape(64, 4, 128)
    found = jnp.min(lax.all_to_all(sent, ("y", "zh", "zl"), 0, 0, tiled=True), axis=0)
    found = lax.all_gather(found, "core", axis=0, tiled=True).reshape(-1)
    nearest = (own + found) / E
    return (codebook, counts.reshape(-1), sums, nearest)


def solution(mesh):
    fine = Mesh(mesh.devices.reshape(SIZES), AXES)
    placed = (
        P(AXES, None),
        P(AXES, None),
        P(AXES, None),
        P(AXES),
        P(AXES),
        P(AXES, None),
        P(("zh", "x", "y"), None),
    )
    return jax.shard_map(
        body,
        mesh=fine,
        in_specs=placed,
        out_specs=(P(AXES, None), P(AXES), P(AXES, None), P(("zh", "x", "y"))),
        check_vma=False,
    )
```

time: 423 us -> 227 us (0.54)
  waiting for transfers between devices: 240 us -> 103 us
  starting transfers between devices: 72.5 us -> 42.5 us
  local copies, waits for them, and re-layouts: 23.1 us -> 8.04 us
  matrix products: 14.2 us -> 0 us
  Pallas kernels: 0 us -> 11.6 us
  other arithmetic: 6.75 us -> 0.95 us
    all_gather x1 -> x2, waiting for transfers between devices: 157 us -> 76 us  [the longest x1 76 us: gather_queries(): both = lax.all_gather(slice_, ('zh', 'zl'), axis=0, tiled=True)]
    all_to_all x4 -> x3, waiting for transfers between devices: 82.5 us -> 25.5 us  [the longest x1 14.3 us: body(): lax.all_to_all(sent, ('y', 'zh', 'zl'), 0, 0, tiled=True)]
    pmin x1 -> x0, blocking collectives: 50.3 us -> none  [body(): nearest = lax.pmin(partial_value, 'code')]
    all_gather x0 -> x3, blocking collectives: none -> 46.2 us  [the longest x1 32 us: body(): tables = lax.all_gather(z_table, ('x', 'y', 'core'), axis=0, tiled=True)]
    all_to_all x4 -> x3, starting transfers between devices: 72.3 us -> 37.9 us  [the longest x1 15.9 us: body(): z_table = lax.all_to_all(table, ('zh', 'zl'), 0, 0, tiled=True)]
    dot_general x5 -> x0, matrix products: 14.2 us -> none  [the longest x2 11.3 us: block_minimum(): lax.dot_general(query_block, code_rows, (((1,), (1,)), ((), ())), preferr...]
    scatter x2 -> x0, local copies, waits for them, and re-layouts: 13 us -> none  [the longest x1 8.52 us: body(): jnp.zeros((slot_total, E), jnp.bfloat16).at[destination].set(batched)]
    pallas_call x0 -> x3, Pallas kernels: none -> 11.6 us  [the longest x1 4.59 us: nearest_codes(): pl.pallas_call(nearest_kernel, out_shape=jax.ShapeDtypeStruct((8, 512), f...]
  transfers between devices with their start and end apart: 5 -> 6, of which waited for: 5 -> 4; matrix products, arithmetic and copies ran while one was open for 4% -> 1% of each run, Pallas kernels for 0% -> 1%
where the time goes in v1:
time: 227 us; the launch traced here: 226 us
  waiting for transfers between devices  103 us (45%)
  blocking collectives  46.2 us (20%)
  starting transfers between devices  42.5 us (19%)
  between operations  14.2 us (6%)
  Pallas kernels  11.6 us (5%)
  local copies, waits for them, and re-layouts  8.04 us (4%)
    all_gather x1, waiting for transfers between devices, gather_queries(): both = lax.all_gather(slice_, ('zh', 'zl'), axis=0, tiled=True)  76 us
    all_gather x1, blocking collectives, body(): tables = lax.all_gather(z_table, ('x', 'y', 'core'), axis=0, tiled=True)  32 us
    all_to_all x1, starting transfers between devices, body(): z_table = lax.all_to_all(table, ('zh', 'zl'), 0, 0, tiled=True)  15.9 us
    all_to_all x1, waiting for transfers between devices, body(): lax.all_to_all(sent, ('y', 'zh', 'zl'), 0, 0, tiled=True)  14.3 us
    all_to_all x1, starting transfers between devices, body(): got = lax.all_to_all(rows, PARTNERS, 0, 0, tiled=True)  11.7 us
    all_to_all x1, waiting for transfers between devices, body(): z_table = lax.all_to_all(table, ('zh', 'zl'), 0, 0, tiled=True)  11.2 us
    all_gather x1, blocking collectives, body(): codes = lax.all_gather(rounded, 'x', axis=0, tiled=True)  10.5 us
    all_to_all x1, starting transfers between devices, body(): lax.all_to_all(sent, ('y', 'zh', 'zl'), 0, 0, tiled=True)  10.3 us
  transfers between devices with their start and end apart: 6, of which 4 were waited for; matrix products, arithmetic and copies ran while one was open for 1% of the time, Pallas kernels for 1%

profile of v1, /device:TPU:1, one launch (start us, length us, event | category | flops | bytes accessed | tf_op | source)
XLA Modules:
  0.0 226.5 jit_solution(5751958659809355737)
XLA Ops:
  7.2 0.0 copy-start.2
  7.2 1.0 copy-done.2
  8.2 0.0 copy-start.4
  8.2 0.7 copy-done.4
  8.9 0.0 copy-start.5
  8.9 0.7 copy-done.5
  9.6 0.0 copy-start.6
  9.6 0.7 copy-done.6
  10.3 3.7 %build.1 = (bf16[512,8,128]{2,1,0:T(8,128)(2,1)}, f32[16,128]{1,0:T(8,128)}) custom-call(bf16[1024,256]{1,0:T(8,128)(2,1)S(1)} %copy-done.2, s32[1,1024]{1,0:T(1,128)S(1)} %copy-done.4, s32[1,1024]{1,0:T(1,128)S(1)} %bitcast.18, s32[1,1024]{1,0:T(1,128)S(1)} %bitcast.19), custom_call_target="tpu_custom_call" | custom-call | flops 3221225472 | bytes 2097152 | tf_op jit(solution)/shard_map/build/pallas_call | solution.py:72
  14.0 0.0 copy-start.7
  14.0 0.0 copy-start
  14.0 15.9 %all-to-all-start.1 = ((f32[16,1,128]{2,1,0:T(1,128)}), f32[16,1,128]{2,1,0:T(1,128)S(1)}, u32[]{:S(2)}, u32[]{:S(2)}) async-start(f32[16,1,128]{2,1,0:T(1,128)} %bitcast.4), calls=%async_computation.1 | async-start | bytes 16384 | tf_op jit(solution)/shard_map/all_to_all | solution.py:187
  29.9 11.2 %all-to-all-done.1 = f32[16,1,128]{2,1,0:T(1,128)S(1)} async-done(((f32[16,1,128]{2,1,0:T(1,128)}), f32[16,1,128]{2,1,0:T(1,128)S(1)}, u32[]{:S(2)}, u32[]{:S(2)}) %all-to-all-start.1) | async-done | bytes 8224 | tf_op jit(solution)/shard_map/all_to_all | solution.py:187
  41.1 0.0 copy-start.3
  41.1 11.7 %all-to-all-start = ((bf16[512,8,128]{2,1,0:T(8,128)(2,1)}), bf16[512,8,128]{2,1,0:T(8,128)(2,1)S(1)}, u32[]{:S(2)}, u32[]{:S(2)}) async-start(bf16[512,8,128]{2,1,0:T(8,128)(2,1)} %get-tuple-element.10), calls=%async_computation | async-start | bytes 2097152 | tf_op jit(solution)/shard_map/all_to_all | solution.py:186
  52.9 0.0 all-gather.5.cloned.1.call-start
  52.9 0.0 copy-done.7
  52.9 0.6 constant_dynamic-slice_fusion.1
  53.6 0.0 all-gather.5.cloned.1.call-update
  53.6 0.0 all-gather.7.cloned.1.call-start
  53.6 76.0 %all-gather.5.cloned.1.call-done = bf16[2048,256]{1,0:T(8,128)(2,1)} async-done(((bf16[128,256]{1,0:T(8,128)(2,1)}), bf16[2048,256]{1,0:T(8,128)(2,1)}) %all-gather.5.cloned.1.call-update) | async-done | bytes 1048592 | tf_op jit(solution)/shard_map/all_gather | solution.py:173
  129.6 1.9 constant_dynamic-slice_fusion
  131.5 0.0 all-gather.7.cloned.1.call-update
  131.5 0.0 copy-done
  131.5 0.1 copy.20.count_col_ref
  131.7 32.0 %all-gather = f32[512,1,128]{2,0,1:T(8,128)S(1)} all-gather(f32[16,1,128]{2,0,1:T(8,128)S(1)} %bitcast.22), channel_id=2, replica_groups=mesh['zh'=2,'x'=4,'y'=4,'zl'=8,'core'=2] {'x','y','core'}, dimensions={0}, use_global_device_ids=true | all-gather | bytes 270336 | tf_op jit(solution)/shard_map/all_gather | solution.py:188
  163.7 0.0 all-to-all-done.rows_ref
  163.7 0.0 copy-done.3
  163.7 3.3 %update.1 = (f32[256,256]{1,0:T(8,128)}, f32[1,256]{1,0:T(1,128)}, f32[256,256]{1,0:T(8,128)}, bf16[256,256]{1,0:T(8,128)(2,1)S(1)}) custom-call(s32[1]{0:T(128)} %bitcast.mine_ref, bf16[512,8,128]{2,1,0:T(8,128)(2,1)S(1)} %all-to-all-done.rows_ref, f32[512,128]{1,0:T(8,128)S(1)} %bitcast.15, f32[256,1]{1,0:T(8,128)S(1)} %copy.20.count_col_ref, ...), custom_call_target="tpu_custom_call" | custom-call | flops 1073741824 | bytes 3145728 | tf_op jit(solution)/shard_map/update/pallas_call | solution.py:126
  167.1 10.5 %all_gather.16 = bf16[1024,256]{1,0:T(8,128)(2,1)S(1)} all-gather(bf16[256,256]{1,0:T(8,128)(2,1)S(1)} %get-tuple-element.15), channel_id=1, replica_groups=mesh['zh'=2,'x'=4,'y'=4,'zl'=8,'core'=2] {'x'}, dimensions={0}, use_global_device_ids=true | all-gather | bytes 655360 | tf_op jit(solution)/shard_map/all_gather | solution.py:191
  177.6 4.6 %collective-permute-start = (bf16[1024,256]{1,0:T(8,128)(2,1)S(1)}, bf16[1024,256]{1,0:T(8,128)(2,1)S(1)}, u32[]{:S(2)}, u32[]{:S(2)}) collective-permute-start(bf16[1024,256]{1,0:T(8,128)(2,1)S(1)} %all_gather.16), channel_id=1, source_target_pairs={{0,1},{1,0},{2,3},{3,2},{4,5},{5,4},{6,7},{7,6},{8,9},{9,8},{10,11... | collective-permute-start | bytes 1572872 | tf_op jit(solution)/shard_map/ppermute | solution.py:192
  182.2 1.3 collective-permute-done
  183.5 0.1 pad_maximum_fusion.codes_ref
  183.6 0.0 all-gather.7.cloned.1.call-done.queries_ref
  183.6 0.0 copy-start.1
  183.6 1.6 copy-done.1
  185.2 4.6 %nearest.1 = f32[8,512]{1,0:T(8,128)S(1)} custom-call(bf16[2048,256]{1,0:T(8,128)(2,1)S(1)} %pad_maximum_fusion.codes_ref, bf16[4096,256]{1,0:T(8,128)(2,1)S(1)} %copy-done.1), custom_call_target="tpu_custom_call" | custom-call | flops 5368709120 | bytes 3145728 | tf_op jit(solution)/shard_map/nearest/pallas_call | solution.py:160
  189.8 0.7 reshape.49
  190.5 10.3 %all-to-all-start.2 = ((f32[64,4,128]{2,1,0:T(4,128)}), f32[64,4,128]{2,1,0:T(4,128)S(1)}, u32[]{:S(2)}, u32[]{:S(2)}) async-start(f32[64,4,128]{2,1,0:T(4,128)} %reshape.49), calls=%async_computation.2 | async-start | bytes 262144 | tf_op jit(solution)/shard_map/all_to_all | solution.py:196
  200.8 0.2 multiply_reduce_fusion
  201.0 14.3 %all-to-all-done.2 = f32[64,4,128]{2,1,0:T(4,128)S(1)} async-done(((f32[64,4,128]{2,1,0:T(4,128)}), f32[64,4,128]{2,1,0:T(4,128)S(1)}, u32[]{:S(2)}, u32[]{:S(2)}) %all-to-all-start.2) | async-done | bytes 131104 | tf_op jit(solution)/shard_map/all_to_all | solution.py:196
  215.3 0.1 reduce_min.9
  215.4 3.7 %all-gather.1 = f32[2,4,128]{2,1,0:T(4,128)S(1)} all-gather(f32[1,4,128]{2,1,0:T(4,128)S(1)} %bitcast.24), channel_id=1, replica_groups=mesh['zh'=2,'x'=4,'y'=4,'zl'=8,'core'=2] {'core'}, dimensions={0}, use_global_device_ids=true | all-gather | bytes 6144 | tf_op jit(solution)/shard_map/all_gather | solution.py:197
  219.0 0.6 add_multiply_fusion
  (1 shorter events, 0.0 us)
Async XLA Ops:
  7.2 1.0 copy-start.2
  8.2 0.7 copy-start.4
  8.9 0.7 copy-start.5
  9.6 0.7 copy-start.6
  14.0 38.9 %copy-start.7 = (bf16[1024,256]{1,0:T(8,128)(2,1)S(1)}, bf16[1024,256]{1,0:T(8,128)(2,1)}, u32[]{:S(2)}) copy-start(bf16[1024,256]{1,0:T(8,128)(2,1)} %param.13) | copy-start | bytes 1572868
  14.0 117.5 %copy-start = (f32[256]{0:T(256)S(1)}, f32[256]{0:T(256)}, u32[]{:S(2)}) copy-start(f32[256]{0:T(256)} %param.11) | copy-start | bytes 3076
  14.0 27.1 %all-to-all-start.1 = ((f32[16,1,128]{2,1,0:T(1,128)}), f32[16,1,128]{2,1,0:T(1,128)S(1)}, u32[]{:S(2)}, u32[]{:S(2)}) async-start(f32[16,1,128]{2,1,0:T(1,128)} %bitcast.4), calls=%async_computation.1 | async-start | bytes 16384 | tf_op jit(solution)/shard_map/all_to_all | solution.py:187
  41.1 122.6 %copy-start.3 = (f32[256,256]{1,0:T(8,128)S(1)}, f32[256,256]{1,0:T(8,128)}, u32[]{:S(2)}) copy-start(f32[256,256]{1,0:T(8,128)} %sums_ref.1) | copy-start | bytes 786436
  41.1 122.6 %all-to-all-start = ((bf16[512,8,128]{2,1,0:T(8,128)(2,1)}), bf16[512,8,128]{2,1,0:T(8,128)(2,1)S(1)}, u32[]{:S(2)}, u32[]{:S(2)}) async-start(bf16[512,8,128]{2,1,0:T(8,128)(2,1)} %get-tuple-element.10), calls=%async_computation | async-start | bytes 2097152 | tf_op jit(solution)/shard_map/all_to_all | solution.py:186
  52.9 76.8 %all-gather.5.cloned.1.call-start = ((), (), s32[]{:S(2)}) async-start(), calls=%async_computation.3 | async-start | bytes 1114112 | tf_op jit(solution)/shard_map/all_gather | solution.py:173
  53.6 130.0 %all-gather.7.cloned.1.call-start = ((), (), s32[]{:S(2)}) async-start(), calls=%async_computation.4 | async-start | bytes 2621440 | tf_op jit(solution)/shard_map/all_gather | solution.py:177
  177.6 5.9 %collective-permute-start = (bf16[1024,256]{1,0:T(8,128)(2,1)S(1)}, bf16[1024,256]{1,0:T(8,128)(2,1)S(1)}, u32[]{:S(2)}, u32[]{:S(2)}) collective-permute-start(bf16[1024,256]{1,0:T(8,128)(2,1)S(1)} %all_gather.16), channel_id=1, source_target_pairs={{0,1},{1,0},{2,3},{3,2},{4,5},{5,4},{6,7},{7,6},{8,9},{9,8},{10,11... | collective-permute-start | bytes 1572872 | tf_op jit(solution)/shard_map/ppermute | solution.py:192
  183.6 1.6 copy-start.1
  190.5 24.8 %all-to-all-start.2 = ((f32[64,4,128]{2,1,0:T(4,128)}), f32[64,4,128]{2,1,0:T(4,128)S(1)}, u32[]{:S(2)}, u32[]{:S(2)}) async-start(f32[64,4,128]{2,1,0:T(4,128)} %reshape.49), calls=%async_computation.2 | async-start | bytes 262144 | tf_op jit(solution)/shard_map/all_to_all | solution.py:196
Sparse Core Ops, SparseCore 0:
  56.3 73.2 all-gather.4
  131.7 41.7 all-gather.6

commit v2 on v1

--- a/solution.py
+++ b/solution.py
@@ -30,9 +30,19 @@
     return jnp.where(hit, 1.0, 0.0).astype(bf16)
 
 
-def build_kernel(latents_ref, order_ref, block_ref, offset_ref, rows_ref, table_ref):
+def build_kernel(latents_hbm, order_hbm, block_hbm, offset_hbm, rows_ref, table_ref,
+                 latents_ref, order_ref, block_ref, offset_ref, sems):
     tokens = latents_ref.shape[0]
     step = tokens // STEPS
+    copies = [
+        pltpu.make_async_copy(block_hbm, block_ref, sems.at[0]),
+        pltpu.make_async_copy(offset_hbm, offset_ref, sems.at[1]),
+        pltpu.make_async_copy(order_hbm, order_ref, sems.at[2]),
+        pltpu.make_async_copy(latents_hbm, latents_ref, sems.at[3]),
+    ]
+    for copy in copies:
+        copy.start()
+    copies[0].wait()
     block = block_ref[...]
     earlier = one_hot(iota((step, step), 0) < iota((step, step), 1))
     ranks = []
@@ -46,14 +56,17 @@
     z_row = ((block >> 8) << 3) | ((block >> 1) & 7)
     plane = (((block >> 4) & 15) << 1) | (block & 1)
     place = (plane * 16 + z_row) * SLOTS + slot
+    copies[1].wait()
     code = (offset_ref[...] + 1).astype(f32)
     rows_hit = jnp.where(iota((16, tokens), 0) == z_row, code, 0.0).astype(bf16)
     lanes_hit = one_hot(iota((128, tokens), 0) == plane * SLOTS + slot)
     table_ref[...] = lax.dot_general(rows_hit, lanes_hit, NT, preferred_element_type=f32)
     digits = jnp.where(iota((8, tokens), 0) == 0, place >> 6, place & 63).astype(f32).astype(bf16)
+    copies[2].wait()
     stored = one_hot(iota((tokens, tokens), 0) == order_ref[...])
     pair = lax.dot_general(digits, stored, NT, preferred_element_type=f32).astype(i32)
     place = pair[0:1] * 64 + pair[1:2]
+    copies[3].wait()
     latents = latents_ref[...]
     chunk = 512
     low = iota((chunk // 8, 8, 128), 1) < 4
@@ -75,7 +88,15 @@
             jax.ShapeDtypeStruct((512, 8, 128), bf16),
             jax.ShapeDtypeStruct((16, 128), f32),
         ),
-        compiler_params=pltpu.CompilerParams(vmem_limit_bytes=48 << 20),
+        in_specs=[pl.BlockSpec(memory_space=pltpu.HBM)] * 4,
+        scratch_shapes=[
+            pltpu.VMEM((1024, E), bf16),
+            pltpu.VMEM((1, 1024), i32),
+            pltpu.VMEM((1, 1024), i32),
+            pltpu.VMEM((1, 1024), i32),
+            pltpu.SemaphoreType.DMA((4,)),
+        ],
+        compiler_params=pltpu.CompilerParams(vmem_limit_bytes=60 << 20),
         cost_estimate=pl.CostEstimate(flops=3 << 30, bytes_accessed=2 << 20, transcendentals=0),
         name="build",
     )(latents, order, block, offset)
@@ -140,62 +161,59 @@
     )(mine, rows, table, counts.reshape(CPD, 1), counts.reshape(1, CPD), sums)
 
 
-def nearest_kernel(codes_ref, queries_ref, out_ref, best_ref):
-    groups, width = out_ref.shape
+def nearest_kernel(near_ref, far_ref, queries_ref, out_ref, best_ref):
+    groups, _, width = best_ref.shape
     tile = 256
-    for c in range(codes_ref.shape[0] // tile):
-        codes = codes_ref[c * tile : (c + 1) * tile].astype(f32)
-        norms = jnp.sum(codes * codes, axis=1, keepdims=True)
-        scaled = (-2.0 * codes).astype(bf16)
-        for g in range(groups):
-            part = queries_ref[g * width : (g + 1) * width]
-            value = lax.dot_general(scaled, part, NT, preferred_element_type=f32) + norms
-            value = jnp.min(value.reshape(tile // 8, 8, width), axis=0)
-            best_ref[g] = value if c == 0 else jnp.minimum(best_ref[g], value)
-    for g in range(groups):
-        out_ref[g : g + 1] = jnp.min(best_ref[g], axis=0, keepdims=True)
-
-
-def nearest_codes(codes, queries):
+    first = True
+    for codes_ref in (near_ref, far_ref):
+        for c in range(codes_ref.shape[0] // tile):
+            codes = codes_ref[c * tile : (c + 1) * tile].astype(f32)
+            norms = jnp.sum(codes * codes, axis=1, keepdims=True)
+            scaled = (-2.0 * codes).astype(bf16)
+            for g in range(groups):
+                part = queries_ref[g * width : (g + 1) * width]
+                value = lax.dot_general(scaled, part, NT, preferred_element_type=f32) + norms
+                value = jnp.min(value.reshape(tile // 8, 8, width), axis=0)
+                best_ref[g] = value if first else jnp.minimum(best_ref[g], value)
+            first = False
+    for y in range(4):
+        lines = []
+        for g in (2 * y, 2 * y + 1):
+            line = jnp.min(best_ref[g], axis=0, keepdims=True)
+            lines += [line[:, j * 128 : (j + 1) * 128] for j in range(4)]
+        tile_ = jnp.concatenate(lines, axis=0)
+        out_ref[y * 16 : (y + 1) * 16] = jnp.broadcast_to(tile_[None], (16, 8, 128))
+
+
+def nearest_codes(near, far, queries):
     return pl.pallas_call(
         nearest_kernel,
-        out_shape=jax.ShapeDtypeStruct((8, 512), f32),
+        out_shape=jax.ShapeDtypeStruct((64, 8, 128), f32),
         scratch_shapes=[pltpu.VMEM((8, 8, 512), f32)],
         compiler_params=pltpu.CompilerParams(vmem_limit_bytes=48 << 20),
         cost_estimate=pl.CostEstimate(flops=5 << 30, bytes_accessed=3 << 20, transcendentals=0),
         name="nearest",
-    )(codes, queries)
-
-
-def gather_queries(queries):
-    share = queries.shape[0] // 8
-    slice_ = lax.dynamic_slice_in_dim(queries, lax.axis_index("zl") * share, share, 0)
-    both = lax.all_gather(slice_, ("zh", "zl"), axis=0, tiled=True)
-    half = queries.shape[0] // 2
-    both = both.reshape(2, 2 * half, E)
-    mine = lax.dynamic_slice_in_dim(both, lax.axis_index("core") * half, half, 1)
-    return lax.all_gather(mine.reshape(2 * half, E), "y", axis=0, tiled=True)
+    )(near, far, queries)
 
 
 def body(latents, batch_order, code_block, code_offset, ema_counts, ema_sums, queries):
-    batch_queries = gather_queries(queries)
+    row_queries = lax.all_gather(queries, "y", axis=0, tiled=True)
     own = jnp.sum(jnp.square(queries.astype(f32)), axis=1)
     rows, table = build(
         latents, batch_order, code_block.reshape(1, -1), code_offset.reshape(1, -1)
     )
     got = lax.all_to_all(rows, PARTNERS, 0, 0, tiled=True)
-    z_table = lax.all_to_all(table, ("zh", "zl"), 0, 0, tiled=True)
+    z_tables = lax.all_gather(table, ("zh", "zl"), axis=0)
+    z_table = lax.dynamic_index_in_dim(z_tables, lax.axis_index(("zh", "zl")), 1, keepdims=False)
     tables = lax.all_gather(z_table, ("x", "y", "core"), axis=0, tiled=True)
     mine = lax.axis_index(("x", "y", "core")).astype(i32).reshape(1)
     codebook, counts, sums, rounded = update(mine, got, tables, ema_counts, ema_sums)
-    codes = lax.all_gather(rounded, "x", axis=0, tiled=True)
-    other = lax.ppermute(codes, "core", [(0, 1), (1, 0)])
-    codes = jnp.concatenate([codes, other], axis=0)
-    best = nearest_codes(codes, batch_queries)
-    sent = jnp.broadcast_to(best[:, None, :], (8, 8, 512)).reshape(64, 4, 128)
-    found = jnp.min(lax.all_to_all(sent, ("y", "zh", "zl"), 0, 0, tiled=True), axis=0)
-    found = lax.all_gather(found, "core", axis=0, tiled=True).reshape(-1)
-    nearest = (own + found) / E
+    mirrored = lax.ppermute(rounded, ("zh", "zl"), [(z, 15 - z) for z in range(16)])
+    near = lax.all_gather(rounded, "x", axis=0, tiled=True)
+    far = lax.all_gather(mirrored, "x", axis=0, tiled=True)
+    best = nearest_codes(near, far, row_queries)
+    found = jnp.min(lax.all_to_all(best, ("y", "zl", "core"), 0, 0, tiled=True), axis=0)
+    nearest = (own + found.reshape(-1)) / E
     return (codebook, counts.reshape(-1), sums, nearest)
 
 

time: 227 us -> 210 us (0.925)
  waiting for transfers between devices: 103 us -> 22.3 us
  blocking collectives: 46.2 us -> 117 us
  local copies, waits for them, and re-layouts: 8.04 us -> 1.76 us
  starting transfers between devices: 42.5 us -> 40.1 us
    all_gather x2 -> x1, waiting for transfers between devices: 76 us -> 0.01 us  [body(): row_queries = lax.all_gather(queries, 'y', axis=0, tiled=True)]
    all_gather x2 -> x3, blocking collectives: 14.2 us -> 86.2 us  [the longest x1 63.7 us: body(): z_tables = lax.all_gather(table, ('zh', 'zl'), axis=0)]
    all_to_all x2 -> x1, starting transfers between devices: 26.2 us -> 12.9 us  [body(): lax.all_to_all(best, ('y', 'zl', 'core'), 0, 0, tiled=True)]
    all_to_all x1, starting transfers between devices: 11.7 us -> 24.3 us  [body(): got = lax.all_to_all(rows, PARTNERS, 0, 0, tiled=True)]
    all_to_all x2 -> x1, waiting for transfers between devices: 25.5 us -> 19.1 us  [body(): lax.all_to_all(best, ('y', 'zl', 'core'), 0, 0, tiled=True)]
    unnamed x16 -> x10, local copies, waits for them, and re-layouts: 4.69 us -> 1.61 us
    dynamic_slice x2 -> x1, local copies, waits for them, and re-layouts: 2.51 us -> 0.01 us  [body(): lax.dynamic_index_in_dim(z_tables, lax.axis_index(('zh', 'zl')), 1, keepd...]
  transfers between devices with their start and end apart: 6 -> 4, of which waited for: 4 -> 2; matrix products, arithmetic and copies ran while one was open for 1% -> 0% of each run, Pallas kernels for 1% -> 2%
where the time goes in v2:
time: 210 us
  blocking collectives  117 us (56%)
  starting transfers between devices  40.1 us (19%)
  waiting for transfers between devices  22.3 us (11%)
  between operations  14.2 us (7%)
  Pallas kernels  13.5 us (6%)
    all_gather x1, blocking collectives, body(): z_tables = lax.all_gather(table, ('zh', 'zl'), axis=0)  63.7 us
    all_gather x1, blocking collectives, body(): tables = lax.all_gather(z_table, ('x', 'y', 'core'), axis=0, tiled=True)  30.7 us
    all_to_all x1, starting transfers between devices, body(): got = lax.all_to_all(rows, PARTNERS, 0, 0, tiled=True)  24.3 us
    all_to_all x1, waiting for transfers between devices, body(): lax.all_to_all(best, ('y', 'zl', 'core'), 0, 0, tiled=True)  19.1 us
    all_to_all x1, starting transfers between devices, body(): lax.all_to_all(best, ('y', 'zl', 'core'), 0, 0, tiled=True)  12.9 us
    all_gather x1, blocking collectives, body(): far = lax.all_gather(mirrored, 'x', axis=0, tiled=True)  11.5 us
    all_gather x1, blocking collectives, body(): near = lax.all_gather(rounded, 'x', axis=0, tiled=True)  11 us
    pallas_call x1, Pallas kernels, nearest_codes(): pl.pallas_call(nearest_kernel, out_shape=jax.ShapeDtypeStruct((64, 8, 128...  5.39 us
  transfers between devices with their start and end apart: 4, of which 2 were waited for; matrix products, arithmetic and copies ran while one was open for 0% of the time, Pallas kernels for 2%

profile of v2, /device:TPU:1, one launch (start us, length us, event | category | flops | bytes accessed | tf_op | source)
XLA Modules:
  0.0 209.6 jit_solution(7447526043942994449)
XLA Ops:
  7.2 4.7 %build.1 = (bf16[512,8,128]{2,1,0:T(8,128)(2,1)}, f32[16,128]{1,0:T(8,128)}) custom-call(bf16[1024,256]{1,0:T(8,128)(2,1)} %latents_hbm.1, s32[1,1024]{1,0:T(1,128)} %order_hbm.1, s32[1,1024]{1,0:T(1,128)} %bitcast.18, s32[1,1024]{1,0:T(1,128)} %bitcast.19), custom_call_target="tpu_custom_call" | custom-call | flops 3221225472 | bytes 2097152 | tf_op jit(solution)/shard_map/build/pallas_call | solution.py:85
  11.9 0.0 copy-start
  11.9 0.0 copy-start.4
  11.9 0.0 copy-start.2
  11.9 24.3 %all-to-all-start = ((bf16[512,8,128]{2,1,0:T(8,128)(2,1)}), bf16[512,8,128]{2,1,0:T(8,128)(2,1)S(1)}, u32[]{:S(2)}, u32[]{:S(2)}) async-start(bf16[512,8,128]{2,1,0:T(8,128)(2,1)} %get-tuple-element.10), calls=%async_computation | async-start | bytes 2097152 | tf_op jit(solution)/shard_map/all_to_all | solution.py:205
  36.3 0.0 all-gather.4.cloned.1.call-start
  36.3 0.7 all-gather.4.cloned.1.call-update
  37.0 0.0 copy-done
  37.0 0.1 copy.12.count_col_ref
  37.2 0.0 copy-done.4
  37.2 63.7 %all-gather = f32[256,128]{1,0:T(8,128)S(1)} all-gather(f32[16,128]{1,0:T(8,128)S(1)} %copy-done.4), channel_id=2, replica_groups=mesh['zh'=2,'x'=4,'y'=4,'zl'=8,'core'=2] {'zh','zl'}, dimensions={0}, use_global_device_ids=true | all-gather | bytes 139264 | tf_op jit(solution)/shard_map/all_gather | solution.py:206
  100.9 30.7 %all-gather.1 = f32[512,1,128]{2,0,1:T(8,128)S(1)} all-gather(f32[16,1,128]{2,0,1:T(8,128)S(1)} %bitcast.17), channel_id=3, replica_groups=mesh['zh'=2,'x'=4,'y'=4,'zl'=8,'core'=2] {'x','y','core'}, dimensions={0}, use_global_device_ids=true | all-gather | bytes 270336 | tf_op jit(solution)/shard_map/all_gather | solution.py:208
  131.6 0.0 all-to-all-done.rows_ref
  131.6 0.0 copy-done.2
  131.6 3.3 %update.1 = (f32[256,256]{1,0:T(8,128)}, f32[1,256]{1,0:T(1,128)}, f32[256,256]{1,0:T(8,128)}, bf16[256,256]{1,0:T(8,128)(2,1)S(1)}) custom-call(s32[1]{0:T(128)} %bitcast.mine_ref, bf16[512,8,128]{2,1,0:T(8,128)(2,1)S(1)} %all-to-all-done.rows_ref, f32[512,128]{1,0:T(8,128)S(1)} %bitcast.13, f32[256,1]{1,0:T(8,128)S(1)} %copy.12.count_col_ref, ...), custom_call_target="tpu_custom_call" | custom-call | flops 1073741824 | bytes 3145728 | tf_op jit(solution)/shard_map/update/pallas_call | solution.py:147
  135.0 2.9 %collective-permute-start = (bf16[256,256]{1,0:T(8,128)(2,1)S(1)}, bf16[256,256]{1,0:T(8,128)(2,1)S(1)}, u32[]{:S(2)}, u32[]{:S(2)}) collective-permute-start(bf16[256,256]{1,0:T(8,128)(2,1)S(1)} %get-tuple-element.15), channel_id=1, source_target_pairs={{0,270},{2,268},{4,266},{6,264},{8,262},{10,260},{12,258},{14,256}... | collective-permute-start | bytes 393224 | tf_op jit(solution)/shard_map/ppermute | solution.py:211
  137.8 11.0 %all_gather.21.near_ref = bf16[1024,256]{1,0:T(8,128)(2,1)S(1)} all-gather(bf16[256,256]{1,0:T(8,128)(2,1)S(1)} %get-tuple-element.15), channel_id=1, replica_groups=mesh['zh'=2,'x'=4,'y'=4,'zl'=8,'core'=2] {'x'}, dimensions={0}, use_global_device_ids=true | all-gather | bytes 655360 | tf_op jit(solution)/shard_map/all_gather | solution.py:212
  148.8 2.6 %collective-permute-done = bf16[256,256]{1,0:T(8,128)(2,1)S(1)} collective-permute-done((bf16[256,256]{1,0:T(8,128)(2,1)S(1)}, bf16[256,256]{1,0:T(8,128)(2,1)S(1)}, u32[]{:S(2)}, u32[]{:S(2)}) %collective-permute-start) | collective-permute-done | bytes 131104 | tf_op jit(solution)/shard_map/ppermute | solution.py:211
  151.4 11.5 %all_gather.22.far_ref = bf16[1024,256]{1,0:T(8,128)(2,1)S(1)} all-gather(bf16[256,256]{1,0:T(8,128)(2,1)S(1)} %collective-permute-done), channel_id=1, replica_groups=mesh['zh'=2,'x'=4,'y'=4,'zl'=8,'core'=2] {'x'}, dimensions={0}, use_global_device_ids=true | all-gather | bytes 655360 | tf_op jit(solution)/shard_map/all_gather | solution.py:213
  162.9 0.0 all-gather.4.cloned.1.call-done.queries_ref
  162.9 0.0 copy-start.1
  162.9 1.6 copy-done.1
  164.5 0.0 copy-start.3
  164.5 5.4 %nearest.1 = f32[64,8,128]{2,1,0:T(8,128)} custom-call(bf16[1024,256]{1,0:T(8,128)(2,1)S(1)} %all_gather.21.near_ref, bf16[1024,256]{1,0:T(8,128)(2,1)S(1)} %all_gather.22.far_ref, bf16[4096,256]{1,0:T(8,128)(2,1)S(1)} %copy-done.1), custom_call_target="tpu_custom_call" | custom-call | flops 5368709120 | bytes 3145728 | tf_op jit(solution)/shard_map/nearest/pallas_call | solution.py:189
  169.9 12.9 %all-to-all-start.1 = ((f32[64,8,128]{2,1,0:T(8,128)}), f32[64,8,128]{2,1,0:T(8,128)S(1)}, u32[]{:S(2)}, u32[]{:S(2)}) async-start(f32[64,8,128]{2,1,0:T(8,128)} %nearest.1), calls=%async_computation.1 | async-start | bytes 524288 | tf_op jit(solution)/shard_map/all_to_all | solution.py:215
  182.9 0.0 copy-done.3
  182.9 0.2 multiply_reduce_fusion
  183.1 19.1 %all-to-all-done.1 = f32[64,8,128]{2,1,0:T(8,128)S(1)} async-done(((f32[64,8,128]{2,1,0:T(8,128)}), f32[64,8,128]{2,1,0:T(8,128)S(1)}, u32[]{:S(2)}, u32[]{:S(2)}) %all-to-all-start.1) | async-done | bytes 262176 | tf_op jit(solution)/shard_map/all_to_all | solution.py:215
  202.1 0.1 reduce_min.9
  202.2 0.6 fusion
  (1 shorter events, 0.0 us)
Async XLA Ops:
  11.9 25.1 %copy-start = (f32[256]{0:T(256)S(1)}, f32[256]{0:T(256)}, u32[]{:S(2)}) copy-start(f32[256]{0:T(256)} %param.11) | copy-start | bytes 3076
  11.9 25.3 %copy-start.4 = (f32[16,128]{1,0:T(8,128)S(1)}, f32[16,128]{1,0:T(8,128)}, u32[]{:S(2)}) copy-start(f32[16,128]{1,0:T(8,128)} %get-tuple-element.11) | copy-start | bytes 24580
  11.9 119.7 %copy-start.2 = (f32[256,256]{1,0:T(8,128)S(1)}, f32[256,256]{1,0:T(8,128)}, u32[]{:S(2)}) copy-start(f32[256,256]{1,0:T(8,128)} %sums_ref.1) | copy-start | bytes 786436
  11.9 119.7 %all-to-all-start = ((bf16[512,8,128]{2,1,0:T(8,128)(2,1)}), bf16[512,8,128]{2,1,0:T(8,128)(2,1)S(1)}, u32[]{:S(2)}, u32[]{:S(2)}) async-start(bf16[512,8,128]{2,1,0:T(8,128)(2,1)} %get-tuple-element.10), calls=%async_computation | async-start | bytes 2097152 | tf_op jit(solution)/shard_map/all_to_all | solution.py:205
  36.3 126.7 %all-gather.4.cloned.1.call-start = ((), (), s32[]{:S(2)}) async-start(), calls=%async_computation.2 | async-start | bytes 2621440 | tf_op jit(solution)/shard_map/all_gather | solution.py:200
  135.0 16.5 %collective-permute-start = (bf16[256,256]{1,0:T(8,128)(2,1)S(1)}, bf16[256,256]{1,0:T(8,128)(2,1)S(1)}, u32[]{:S(2)}, u32[]{:S(2)}) collective-permute-start(bf16[256,256]{1,0:T(8,128)(2,1)S(1)} %get-tuple-element.15), channel_id=1, source_target_pairs={{0,270},{2,268},{4,266},{6,264},{8,262},{10,260},{12,258},{14,256}... | collective-permute-start | bytes 393224 | tf_op jit(solution)/shard_map/ppermute | solution.py:211
  162.9 1.6 copy-start.1
  164.5 18.3 %copy-start.3 = (bf16[1024,256]{1,0:T(8,128)(2,1)S(1)}, bf16[1024,256]{1,0:T(8,128)(2,1)}, u32[]{:S(2)}) copy-start(bf16[1024,256]{1,0:T(8,128)(2,1)} %param.13) | copy-start | bytes 1572868
  169.9 32.2 %all-to-all-start.1 = ((f32[64,8,128]{2,1,0:T(8,128)}), f32[64,8,128]{2,1,0:T(8,128)S(1)}, u32[]{:S(2)}, u32[]{:S(2)}) async-start(f32[64,8,128]{2,1,0:T(8,128)} %nearest.1), calls=%async_computation.1 | async-start | bytes 524288 | tf_op jit(solution)/shard_map/all_to_all | solution.py:215
Sparse Core Ops, SparseCore 0:
  39.2 46.3 all-gather.3

commit v3 on v2

--- a/solution.py
+++ b/solution.py
@@ -14,7 +14,6 @@
 
 AXES = ("zh", "x", "y", "zl", "core")
 SIZES = (2, 4, 4, 8, 2)
-PARTNERS = ("x", "y", "core", "zh", "zl")
 NT = (((1,), (1,)), ((), ()))
 
 f32 = jnp.float32
@@ -30,7 +29,7 @@
     return jnp.where(hit, 1.0, 0.0).astype(bf16)
 
 
-def build_kernel(latents_hbm, order_hbm, block_hbm, offset_hbm, rows_ref, table_ref,
+def build_kernel(latents_hbm, order_hbm, block_hbm, offset_hbm, rows_ref,
                  latents_ref, order_ref, block_ref, offset_ref, sems):
     tokens = latents_ref.shape[0]
     step = tokens // STEPS
@@ -53,14 +52,12 @@
     rank = jnp.concatenate(ranks, axis=1).astype(i32)
     position = iota((1, tokens), 1)
     slot = jnp.where(position >= step, CAP, 0) + rank
-    z_row = ((block >> 8) << 3) | ((block >> 1) & 7)
-    plane = (((block >> 4) & 15) << 1) | (block & 1)
-    place = (plane * 16 + z_row) * SLOTS + slot
+    place = block * SLOTS + slot
     copies[1].wait()
     code = (offset_ref[...] + 1).astype(f32)
-    rows_hit = jnp.where(iota((16, tokens), 0) == z_row, code, 0.0).astype(bf16)
-    lanes_hit = one_hot(iota((128, tokens), 0) == plane * SLOTS + slot)
-    table_ref[...] = lax.dot_general(rows_hit, lanes_hit, NT, preferred_element_type=f32)
+    lanes = jnp.where((iota((128, tokens), 0) & 3) == slot, code, 0.0).astype(bf16)
+    named = one_hot((iota((1024, tokens), 0) >> 1) == block)
+    labels = lax.dot_general(named, lanes, NT, preferred_element_type=f32).reshape(128, 8, 128)
     digits = jnp.where(iota((8, tokens), 0) == 0, place >> 6, place & 63).astype(f32).astype(bf16)
     copies[2].wait()
     stored = one_hot(iota((tokens, tokens), 0) == order_ref[...])
@@ -70,6 +67,7 @@
     latents = latents_ref[...]
     chunk = 512
     low = iota((chunk // 8, 8, 128), 1) < 4
+    row = iota((chunk // 16, 8, 128), 1)
     for c in range(512 * SLOTS // chunk):
         pick = one_hot(iota((chunk, tokens), 0) + c * chunk == place)
         got = jnp.dot(pick, latents, preferred_element_type=f32)
@@ -77,17 +75,28 @@
         b = got[:, 128:].reshape(chunk // 8, 8, 128)
         first = jnp.where(low, a, pltpu.roll(b, 4, 1))
         second = jnp.where(low, pltpu.roll(a, 4, 1), b)
-        both = jnp.stack([first, second], axis=1).reshape(chunk // 4, 8, 128)
-        rows_ref[c * (chunk // 4) : (c + 1) * (chunk // 4)] = both.astype(bf16)
+        m = jnp.stack([first, second], axis=1).reshape(chunk // 16, 4, 8, 128)
+        label = labels[c * (chunk // 16) : (c + 1) * (chunk // 16)]
+        m1 = pltpu.roll(m[:, 1], 2, 1)
+        m2 = pltpu.roll(m[:, 2], 4, 1)
+        m3 = pltpu.roll(m[:, 3], 6, 1)
+        tiles = [
+            m[:, 0],
+            jnp.where(row < 2, label, m1),
+            jnp.where(row < 2, m1, jnp.where(row < 4, label, m2)),
+            jnp.where(row < 4, m2, jnp.where(row < 6, label, m3)),
+            jnp.where(row < 6, m3, label),
+        ]
+        count = chunk // 16 * 40
+        rows_ref[c * count : (c + 1) * count] = (
+            jnp.stack(tiles, axis=1).reshape(count, 128).astype(bf16)
+        )
 
 
 def build(latents, order, block, offset):
     return pl.pallas_call(
         build_kernel,
-        out_shape=(
-            jax.ShapeDtypeStruct((512, 8, 128), bf16),
-            jax.ShapeDtypeStruct((16, 128), f32),
-        ),
+        out_shape=jax.ShapeDtypeStruct((512 * 10, 128), bf16),
         in_specs=[pl.BlockSpec(memory_space=pltpu.HBM)] * 4,
         scratch_shapes=[
             pltpu.VMEM((1024, E), bf16),
@@ -102,22 +111,24 @@
     )(latents, order, block, offset)
 
 
-def update_kernel(mine_ref, rows_ref, table_ref, count_col_ref, count_row_ref, sums_ref,
+def update_kernel(rows_ref, count_col_ref, count_row_ref, sums_ref,
                   codebook_ref, counts_ref, new_sums_ref, rounded_ref, hit_ref):
-    mine = mine_ref[0]
-    lane = iota((512, 128), 1)
-    table = jnp.where((lane >> 2) == mine, table_ref[...], 0.0).astype(bf16)
-    spread = one_hot((iota((128, 128), 0) & 3) == (iota((128, 128), 1) & 3))
-    spread = jnp.dot(table, spread, preferred_element_type=f32)
-    keep = (iota((512, 128), 0) & 31) == (lane >> 2)
-    code = jnp.sum(jnp.where(keep, spread, 0.0).reshape(16, 32, 128), axis=1).astype(i32)
+    t0, t1, t2, t3, t4 = jnp.split(rows_ref[...].astype(f32).reshape(128, 5, 8, 128), 5, axis=1)
+    t0, t1, t2, t3, t4 = t0[:, 0], t1[:, 0], t2[:, 0], t3[:, 0], t4[:, 0]
+    row = iota((128, 8, 128), 1)
+    label = jnp.where(row < 2, t1, jnp.where(row < 4, t2, jnp.where(row < 6, t3, t4)))
+    keep = iota((64, 128), 0) == 2 * (iota((64, 128), 1) >> 2)
+    code = jnp.sum(jnp.where(keep, label.reshape(16, 64, 128), 0.0), axis=1).astype(i32)
     local = iota((2 * CPD, 128), 0)
     step = ((iota((2 * CPD, 128), 1) & 3) >> 1) == (local >> 8)
     local = jnp.where(step, (local & 255) + 1, -1)
     for i in range(16):
         hit_ref[:, i * 128 : (i + 1) * 128] = one_hot(local == code[i : i + 1])
-    pairs = rows_ref[...].astype(f32).reshape(256, 2, 8, 128)
-    first, second = pairs[:, 0], pairs[:, 1]
+    m1 = jnp.where(row < 6, pltpu.roll(t1, 6, 1), pltpu.roll(t2, 6, 1))
+    m2 = jnp.where(row < 4, pltpu.roll(t2, 4, 1), pltpu.roll(t3, 4, 1))
+    m3 = jnp.where(row < 2, pltpu.roll(t3, 2, 1), pltpu.roll(t4, 2, 1))
+    first = jnp.stack([t0, m2], axis=1).reshape(256, 8, 128)
+    second = jnp.stack([m1, m3], axis=1).reshape(256, 8, 128)
     low = iota((256, 8, 128), 1) < 4
     left = jnp.where(low, first, pltpu.roll(second, 4, 1)).reshape(2048, 128)
     right = jnp.where(low, pltpu.roll(first, 4, 1), second).reshape(2048, 128)
@@ -142,7 +153,7 @@
     counts_ref[...] = rows
 
 
-def update(mine, rows, table, counts, sums):
+def update(rows, counts, sums):
     vmem = pl.BlockSpec(memory_space=pltpu.VMEM)
     return pl.pallas_call(
         update_kernel,
@@ -152,13 +163,13 @@
             jax.ShapeDtypeStruct((CPD, E), f32),
             jax.ShapeDtypeStruct((CPD, E), bf16),
         ),
-        in_specs=[pl.BlockSpec(memory_space=pltpu.SMEM)] + [vmem] * 5,
+        in_specs=[vmem] * 4,
         out_specs=(vmem,) * 4,
         scratch_shapes=[pltpu.VMEM((2 * CPD, 2048), bf16)],
         compiler_params=pltpu.CompilerParams(vmem_limit_bytes=48 << 20),
         cost_estimate=pl.CostEstimate(flops=1 << 30, bytes_accessed=3 << 20, transcendentals=0),
         name="update",
-    )(mine, rows, table, counts.reshape(CPD, 1), counts.reshape(1, CPD), sums)
+    )(rows, counts.reshape(CPD, 1), counts.reshape(1, CPD), sums)
 
 
 def nearest_kernel(near_ref, far_ref, queries_ref, out_ref, best_ref):
@@ -176,19 +187,18 @@
                 value = jnp.min(value.reshape(tile // 8, 8, width), axis=0)
                 best_ref[g] = value if first else jnp.minimum(best_ref[g], value)
             first = False
-    for y in range(4):
-        lines = []
-        for g in (2 * y, 2 * y + 1):
-            line = jnp.min(best_ref[g], axis=0, keepdims=True)
-            lines += [line[:, j * 128 : (j + 1) * 128] for j in range(4)]
-        tile_ = jnp.concatenate(lines, axis=0)
-        out_ref[y * 16 : (y + 1) * 16] = jnp.broadcast_to(tile_[None], (16, 8, 128))
+    for g in range(groups):
+        line = jnp.min(best_ref[g], axis=0, keepdims=True)
+        part = jnp.concatenate([line[:, j * 128 : (j + 1) * 128] for j in range(4)], axis=0)
+        y, core = g // 2, g % 2
+        for zl in range(8):
+            out_ref[y * 16 + zl * 2 + core] = part
 
 
 def nearest_codes(near, far, queries):
     return pl.pallas_call(
         nearest_kernel,
-        out_shape=jax.ShapeDtypeStruct((64, 8, 128), f32),
+        out_shape=jax.ShapeDtypeStruct((64, 4, 128), f32),
         scratch_shapes=[pltpu.VMEM((8, 8, 512), f32)],
         compiler_params=pltpu.CompilerParams(vmem_limit_bytes=48 << 20),
         cost_estimate=pl.CostEstimate(flops=5 << 30, bytes_accessed=3 << 20, transcendentals=0),
@@ -199,21 +209,18 @@
 def body(latents, batch_order, code_block, code_offset, ema_counts, ema_sums, queries):
     row_queries = lax.all_gather(queries, "y", axis=0, tiled=True)
     own = jnp.sum(jnp.square(queries.astype(f32)), axis=1)
-    rows, table = build(
+    rows = build(
         latents, batch_order, code_block.reshape(1, -1), code_offset.reshape(1, -1)
     )
-    got = lax.all_to_all(rows, PARTNERS, 0, 0, tiled=True)
-    z_tables = lax.all_gather(table, ("zh", "zl"), axis=0)
-    z_table = lax.dynamic_index_in_dim(z_tables, lax.axis_index(("zh", "zl")), 1, keepdims=False)
-    tables = lax.all_gather(z_table, ("x", "y", "core"), axis=0, tiled=True)
-    mine = lax.axis_index(("x", "y", "core")).astype(i32).reshape(1)
-    codebook, counts, sums, rounded = update(mine, got, tables, ema_counts, ema_sums)
+    got = lax.all_to_all(rows.reshape(512, 5, 2, 128), AXES, 0, 0, tiled=True)
+    codebook, counts, sums, rounded = update(got.reshape(5120, 128), ema_counts, ema_sums)
     mirrored = lax.ppermute(rounded, ("zh", "zl"), [(z, 15 - z) for z in range(16)])
     near = lax.all_gather(rounded, "x", axis=0, tiled=True)
     far = lax.all_gather(mirrored, "x", axis=0, tiled=True)
     best = nearest_codes(near, far, row_queries)
     found = jnp.min(lax.all_to_all(best, ("y", "zl", "core"), 0, 0, tiled=True), axis=0)
-    nearest = (own + found.reshape(-1)) / E
+    found = lax.all_gather(found, "core", axis=0, tiled=True).reshape(-1)
+    nearest = (own + found) / E
     return (codebook, counts.reshape(-1), sums, nearest)
 
 

time: 210 us -> 179 us (0.85)
  blocking collectives: 117 us -> 25.5 us
  waiting for transfers between devices: 22.3 us -> 81.6 us
    all_gather x2 -> x1, blocking collectives: 94.4 us -> 2.18 us  [body(): found = lax.all_gather(found, 'core', axis=0, tiled=True).reshape(-1)]
    all_to_all x1, waiting for transfers between devices: 0.01 us -> 66.6 us  [body(): got = lax.all_to_all(rows.reshape(512, 5, 2, 128), AXES, 0, 0, tiled=True)]
    all_to_all x1, waiting for transfers between devices: 19.1 us -> 14.3 us  [body(): lax.all_to_all(best, ('y', 'zl', 'core'), 0, 0, tiled=True)]
    ppermute x1, waiting for transfers between devices: 2.61 us -> 0.01 us  [body(): lax.ppermute(rounded, ('zh', 'zl'), [(z, 15 - z) for z in range(16)])]
    all_to_all x1, starting transfers between devices: 12.9 us -> 10.4 us  [body(): lax.all_to_all(best, ('y', 'zl', 'core'), 0, 0, tiled=True)]
where the time goes in v3:
time: 179 us; the launch traced here: 178 us
  waiting for transfers between devices  81.6 us (46%)
  starting transfers between devices  39.1 us (22%)
  blocking collectives  25.5 us (14%)
  Pallas kernels  15.2 us (8%)
  between operations  14.1 us (8%)
    all_to_all x1, waiting for transfers between devices, body(): got = lax.all_to_all(rows.reshape(512, 5, 2, 128), AXES, 0, 0, tiled=True)  66.6 us
    all_to_all x1, starting transfers between devices, body(): got = lax.all_to_all(rows.reshape(512, 5, 2, 128), AXES, 0, 0, tiled=True)  24.3 us
    all_to_all x1, waiting for transfers between devices, body(): lax.all_to_all(best, ('y', 'zl', 'core'), 0, 0, tiled=True)  14.3 us
    all_gather x1, blocking collectives, body(): near = lax.all_gather(rounded, 'x', axis=0, tiled=True)  11.7 us
    all_gather x1, blocking collectives, body(): far = lax.all_gather(mirrored, 'x', axis=0, tiled=True)  11.6 us
    all_to_all x1, starting transfers between devices, body(): lax.all_to_all(best, ('y', 'zl', 'core'), 0, 0, tiled=True)  10.4 us
    pallas_call x1, Pallas kernels, build(): pl.pallas_call(build_kernel, out_shape=jax.ShapeDtypeStruct((512 * 10, 12...  6.63 us
    pallas_call x1, Pallas kernels, nearest_codes(): pl.pallas_call(nearest_kernel, out_shape=jax.ShapeDtypeStruct((64, 4, 128...  5.25 us
  transfers between devices with their start and end apart: 4, of which 2 were waited for; matrix products, arithmetic and copies ran while one was open for 0% of the time, Pallas kernels for 2%

profile of v3, /device:TPU:1, one launch (start us, length us, event | category | flops | bytes accessed | tf_op | source)
XLA Modules:
  0.0 178.2 jit_solution(14154951965790262210)
XLA Ops:
  7.2 6.6 %build.1 = bf16[5120,128]{1,0:T(8,128)(2,1)} custom-call(bf16[1024,256]{1,0:T(8,128)(2,1)} %latents_hbm.1, s32[1,1024]{1,0:T(1,128)} %order_hbm.1, s32[1,1024]{1,0:T(1,128)} %bitcast.15, s32[1,1024]{1,0:T(1,128)} %bitcast.16), custom_call_target="tpu_custom_call" | custom-call | flops 3221225472 | bytes 2097152 | tf_op jit(solution)/shard_map/build/pallas_call | solution.py:97
  13.8 0.0 copy-start
  13.8 0.0 copy-start.2
  13.8 24.3 %all-to-all-start = ((bf16[512,5,2,128]{3,2,1,0:T(2,128)(2,1)}), bf16[512,5,2,128]{3,2,1,0:T(2,128)(2,1)S(1)}, u32[]{:S(2)}, u32[]{:S(2)}) async-start(bf16[512,5,2,128]{3,2,1,0:T(2,128)(2,1)} %bitcast.12), calls=%async_computation | async-start | bytes 2621440 | tf_op jit(solution)/shard_map/all_to_all | solution.py:215
  38.1 0.0 all-gather.3.cloned.1.call-start
  38.2 0.7 all-gather.3.cloned.1.call-update
  38.9 0.0 copy-done
  38.9 0.1 copy.12.count_col_ref
  39.0 66.6 %all-to-all-done = bf16[512,5,2,128]{3,2,1,0:T(2,128)(2,1)S(1)} async-done(((bf16[512,5,2,128]{3,2,1,0:T(2,128)(2,1)}), bf16[512,5,2,128]{3,2,1,0:T(2,128)(2,1)S(1)}, u32[]{:S(2)}, u32[]{:S(2)}) %all-to-all-start) | async-done | bytes 1310752 | tf_op jit(solution)/shard_map/all_to_all | solution.py:215
  105.6 0.0 copy-done.2
  105.6 3.3 %update.1 = (f32[256,256]{1,0:T(8,128)}, f32[1,256]{1,0:T(1,128)}, f32[256,256]{1,0:T(8,128)}, bf16[256,256]{1,0:T(8,128)(2,1)S(1)}) custom-call(bf16[5120,128]{1,0:T(8,128)(2,1)S(1)} %bitcast.9, f32[256,1]{1,0:T(8,128)S(1)} %copy.12.count_col_ref, f32[1,256]{1,0:T(1,128)S(1)} %bitcast.11, f32[256,256]{1,0:T(8,128)S(1)} %copy-done.2), custom_call_target="tpu_custom_call" | custom-call | flops 1073741824 | bytes 3145728 | tf_op jit(solution)/shard_map/update/pallas_call | solution.py:158
  109.0 4.3 %collective-permute-start = (bf16[256,256]{1,0:T(8,128)(2,1)S(1)}, bf16[256,256]{1,0:T(8,128)(2,1)S(1)}, u32[]{:S(2)}, u32[]{:S(2)}) collective-permute-start(bf16[256,256]{1,0:T(8,128)(2,1)S(1)} %get-tuple-element.11), channel_id=1, source_target_pairs={{0,270},{2,268},{4,266},{6,264},{8,262},{10,260},{12,258},{14,256}... | collective-permute-start | bytes 393224 | tf_op jit(solution)/shard_map/ppermute | solution.py:217
  113.3 11.7 %all_gather.12.near_ref = bf16[1024,256]{1,0:T(8,128)(2,1)S(1)} all-gather(bf16[256,256]{1,0:T(8,128)(2,1)S(1)} %get-tuple-element.11), channel_id=1, replica_groups=mesh['zh'=2,'x'=4,'y'=4,'zl'=8,'core'=2] {'x'}, dimensions={0}, use_global_device_ids=true | all-gather | bytes 655360 | tf_op jit(solution)/shard_map/all_gather | solution.py:218
  125.0 0.0 collective-permute-done
  125.0 11.6 %all_gather.13.far_ref = bf16[1024,256]{1,0:T(8,128)(2,1)S(1)} all-gather(bf16[256,256]{1,0:T(8,128)(2,1)S(1)} %collective-permute-done), channel_id=1, replica_groups=mesh['zh'=2,'x'=4,'y'=4,'zl'=8,'core'=2] {'x'}, dimensions={0}, use_global_device_ids=true | all-gather | bytes 655360 | tf_op jit(solution)/shard_map/all_gather | solution.py:219
  136.6 0.0 all-gather.3.cloned.1.call-done.queries_ref
  136.6 0.0 copy-start.1
  136.7 1.6 copy-done.1
  138.2 0.0 copy-start.3
  138.2 5.2 %nearest.1 = f32[64,4,128]{2,1,0:T(4,128)} custom-call(bf16[1024,256]{1,0:T(8,128)(2,1)S(1)} %all_gather.12.near_ref, bf16[1024,256]{1,0:T(8,128)(2,1)S(1)} %all_gather.13.far_ref, bf16[4096,256]{1,0:T(8,128)(2,1)S(1)} %copy-done.1), custom_call_target="tpu_custom_call" | custom-call | flops 5368709120 | bytes 3145728 | tf_op jit(solution)/shard_map/nearest/pallas_call | solution.py:199
  143.5 10.4 %all-to-all-start.1 = ((f32[64,4,128]{2,1,0:T(4,128)}), f32[64,4,128]{2,1,0:T(4,128)S(1)}, u32[]{:S(2)}, u32[]{:S(2)}) async-start(f32[64,4,128]{2,1,0:T(4,128)} %nearest.1), calls=%async_computation.1 | async-start | bytes 262144 | tf_op jit(solution)/shard_map/all_to_all | solution.py:221
  153.9 0.0 copy-done.3
  154.0 0.2 multiply_reduce_fusion
  154.2 14.3 %all-to-all-done.1 = f32[64,4,128]{2,1,0:T(4,128)S(1)} async-done(((f32[64,4,128]{2,1,0:T(4,128)}), f32[64,4,128]{2,1,0:T(4,128)S(1)}, u32[]{:S(2)}, u32[]{:S(2)}) %all-to-all-start.1) | async-done | bytes 131104 | tf_op jit(solution)/shard_map/all_to_all | solution.py:221
  168.5 0.1 reduce_min.9
  168.6 2.2 %all-gather = f32[2,4,128]{2,1,0:T(4,128)S(1)} all-gather(f32[1,4,128]{2,1,0:T(4,128)S(1)} %bitcast.14), channel_id=1, replica_groups=mesh['zh'=2,'x'=4,'y'=4,'zl'=8,'core'=2] {'core'}, dimensions={0}, use_global_device_ids=true | all-gather | bytes 6144 | tf_op jit(solution)/shard_map/all_gather | solution.py:222
  170.8 0.6 add_multiply_fusion
Async XLA Ops:
  13.8 25.1 %copy-start = (f32[256]{0:T(256)S(1)}, f32[256]{0:T(256)}, u32[]{:S(2)}) copy-start(f32[256]{0:T(256)} %param.11) | copy-start | bytes 3076
  13.8 91.8 %copy-start.2 = (f32[256,256]{1,0:T(8,128)S(1)}, f32[256,256]{1,0:T(8,128)}, u32[]{:S(2)}) copy-start(f32[256,256]{1,0:T(8,128)} %sums_ref.1) | copy-start | bytes 786436
  13.8 91.8 %all-to-all-start = ((bf16[512,5,2,128]{3,2,1,0:T(2,128)(2,1)}), bf16[512,5,2,128]{3,2,1,0:T(2,128)(2,1)S(1)}, u32[]{:S(2)}, u32[]{:S(2)}) async-start(bf16[512,5,2,128]{3,2,1,0:T(2,128)(2,1)} %bitcast.12), calls=%async_computation | async-start | bytes 2621440 | tf_op jit(solution)/shard_map/all_to_all | solution.py:215
  38.1 98.5 %all-gather.3.cloned.1.call-start = ((), (), s32[]{:S(2)}) async-start(), calls=%async_computation.2 | async-start | bytes 2621440 | tf_op jit(solution)/shard_map/all_gather | solution.py:210
  109.0 16.0 %collective-permute-start = (bf16[256,256]{1,0:T(8,128)(2,1)S(1)}, bf16[256,256]{1,0:T(8,128)(2,1)S(1)}, u32[]{:S(2)}, u32[]{:S(2)}) collective-permute-start(bf16[256,256]{1,0:T(8,128)(2,1)S(1)} %get-tuple-element.11), channel_id=1, source_target_pairs={{0,270},{2,268},{4,266},{6,264},{8,262},{10,260},{12,258},{14,256}... | collective-permute-start | bytes 393224 | tf_op jit(solution)/shard_map/ppermute | solution.py:217
  136.6 1.6 copy-start.1
  138.2 15.7 %copy-start.3 = (bf16[1024,256]{1,0:T(8,128)(2,1)S(1)}, bf16[1024,256]{1,0:T(8,128)(2,1)}, u32[]{:S(2)}) copy-start(bf16[1024,256]{1,0:T(8,128)(2,1)} %param.13) | copy-start | bytes 1572868
  143.5 25.0 %all-to-all-start.1 = ((f32[64,4,128]{2,1,0:T(4,128)}), f32[64,4,128]{2,1,0:T(4,128)S(1)}, u32[]{:S(2)}, u32[]{:S(2)}) async-start(f32[64,4,128]{2,1,0:T(4,128)} %nearest.1), calls=%async_computation.1 | async-start | bytes 262144 | tf_op jit(solution)/shard_map/all_to_all | solution.py:221
Sparse Core Ops, SparseCore 0:
  41.1 46.2 all-gather.2

commit v4 on v3

v4 whole, which is shorter than its diff:
```python
import functools

import jax
import jax.numpy as jnp
from jax import lax
from jax.experimental import pallas as pl
from jax.experimental.pallas import tpu as pltpu
from jax.sharding import Mesh, PartitionSpec as P

E = 256
CPD = 256
STEPS = 2
CAP = 2
SLOTS = STEPS * CAP
ema_decay = 0.9

AXES = ("zh", "x", "y", "zl", "core")
SIZES = (2, 4, 4, 8, 2)
NT = (((1,), (1,)), ((), ()))

f32 = jnp.float32
bf16 = jnp.bfloat16
i32 = jnp.int32


def iota(shape, dim):
    return lax.broadcasted_iota(i32, shape, dim)


def one_hot(hit):
    return jnp.where(hit, 1.0, 0.0).astype(bf16)


def build_kernel(core_ref, latents_hbm, order_hbm, block_hbm, offset_hbm, rows_ref,
                 latents_ref, order_ref, block_ref, offset_ref, sems):
    tokens = latents_ref.shape[0]
    step = tokens // STEPS
    copies = [
        pltpu.make_async_copy(block_hbm, block_ref, sems.at[0]),
        pltpu.make_async_copy(offset_hbm, offset_ref, sems.at[1]),
        pltpu.make_async_copy(order_hbm, order_ref, sems.at[2]),
        pltpu.make_async_copy(latents_hbm, latents_ref, sems.at[3]),
    ]
    for copy in copies:
        copy.start()
    copies[0].wait()
    block = block_ref[...] ^ core_ref[0]
    earlier = one_hot(iota((step, step), 0) < iota((step, step), 1))
    ranks = []
    for t in range(STEPS):
        own = iota((512, step), 0) == block[:, t * step : (t + 1) * step]
        counts = jnp.dot(one_hot(own), earlier, preferred_element_type=f32)
        ranks.append(jnp.sum(jnp.where(own, counts, 0.0), axis=0, keepdims=True))
    rank = jnp.concatenate(ranks, axis=1).astype(i32)
    position = iota((1, tokens), 1)
    slot = jnp.where(position >= step, CAP, 0) + rank
    place = block * SLOTS + slot
    copies[1].wait()
    code = (offset_ref[...] + 1).astype(f32)
    lanes = jnp.where((iota((128, tokens), 0) & 7) == (place & 7), code, 0.0).astype(bf16)
    named = one_hot((iota((512, tokens), 0) >> 1) == (block >> 1))
    labels = lax.dot_general(named, lanes, NT, preferred_element_type=f32)
    labels = jnp.where((iota((512, 128), 0) & 1) == 1, pltpu.roll(labels, 4, 1), labels)
    labels = labels.reshape(64, 8, 128)
    digits = jnp.where(iota((8, tokens), 0) == 0, place >> 6, place & 63).astype(f32).astype(bf16)
    copies[2].wait()
    stored = one_hot(iota((tokens, tokens), 0) == order_ref[...])
    pair = lax.dot_general(digits, stored, NT, preferred_element_type=f32).astype(i32)
    place = pair[0:1] * 64 + pair[1:2]
    copies[3].wait()
    latents = latents_ref[...]
    chunk = 512
    low = iota((chunk // 8, 8, 128), 1) < 4
    groups = chunk // 32
    row = iota((groups, 8, 128), 1)
    for c in range(512 * SLOTS // chunk):
        pick = one_hot(iota((chunk, tokens), 0) + c * chunk == place)
        got = jnp.dot(pick, latents, preferred_element_type=f32)
        a = got[:, :128].reshape(chunk // 8, 8, 128)
        b = got[:, 128:].reshape(chunk // 8, 8, 128)
        first = jnp.where(low, a, pltpu.roll(b, 4, 1))
        second = jnp.where(low, pltpu.roll(a, 4, 1), b)
        m = jnp.stack([first, second], axis=1).reshape(groups, 4, 2, 8, 128)
        label = labels[c * groups : (c + 1) * groups]
        a1, b1 = pltpu.roll(m[:, 1, 0], 2, 1), pltpu.roll(m[:, 1, 1], 2, 1)
        a2, b2 = pltpu.roll(m[:, 2, 0], 4, 1), pltpu.roll(m[:, 2, 1], 4, 1)
        a3, b3 = pltpu.roll(m[:, 3, 0], 6, 1), pltpu.roll(m[:, 3, 1], 6, 1)
        tiles = [
            m[:, 0, 0],
            m[:, 0, 1],
            jnp.where(row < 2, label, a1),
            jnp.where(row < 2, a1, b1),
            jnp.where(row < 2, b1, jnp.where(row < 4, label, a2)),
            jnp.where(row < 4, a2, b2),
            jnp.where(row < 4, b2, jnp.where(row < 6, label, a3)),
            jnp.where(row < 6, a3, b3),
            jnp.where(row < 6, b3, label),
        ]
        count = groups * 72
        rows_ref[c * count : (c + 1) * count] = (
            jnp.stack(tiles, axis=1).reshape(count, 128).astype(bf16)
        )


def build(core, latents, order, block, offset):
    return pl.pallas_call(
        build_kernel,
        out_shape=jax.ShapeDtypeStruct((256 * 18, 128), bf16),
        in_specs=[pl.BlockSpec(memory_space=pltpu.SMEM)] + [pl.BlockSpec(memory_space=pltpu.HBM)] * 4,
        scratch_shapes=[
            pltpu.VMEM((1024, E), bf16),
            pltpu.VMEM((1, 1024), i32),
            pltpu.VMEM((1, 1024), i32),
            pltpu.VMEM((1, 1024), i32),
            pltpu.SemaphoreType.DMA((4,)),
        ],
        compiler_params=pltpu.CompilerParams(vmem_limit_bytes=60 << 20),
        cost_estimate=pl.CostEstimate(flops=3 << 30, bytes_accessed=2 << 20, transcendentals=0),
        name="build",
    )(core, latents, order, block, offset)


def partial_kernel(side, rows_ref, queries_ref, out_ref, hit_ref):
    del queries_ref
    tiles = rows_ref[...].astype(f32).reshape(64, 9, 8, 128)
    row = iota((64, 8, 128), 1)
    label = jnp.where(row < 6, tiles[:, 6], tiles[:, 8])
    label = jnp.where(row < 2, tiles[:, 2], jnp.where(row < 4, tiles[:, 4], label))
    line, lane = iota((64, 128), 0), iota((64, 128), 1)
    keep = line == 2 * (lane >> 2) + (((lane >> 2) & 1) ^ side)
    code = jnp.sum(jnp.where(keep, label.reshape(8, 64, 128), 0.0), axis=1).astype(i32)
    local = iota((2 * CPD, 128), 0)
    step = ((iota((2 * CPD, 128), 1) & 3) >> 1) == (local >> 8)
    local = jnp.where(step, (local & 255) + 1, -1)
    for i in range(8):
        hit_ref[:, i * 128 : (i + 1) * 128] = one_hot(local == code[i : i + 1])
    messages = []
    for i in range(4):
        at, shift = (18 * i + 8 * side) // 8, (18 * i) % 8
        if shift:
            low = pltpu.roll(tiles[:, at], 8 - shift, 1)
            high = pltpu.roll(tiles[:, at + 1], 8 - shift, 1)
            messages.append(jnp.where(row < 8 - shift, low, high))
        else:
            messages.append(tiles[:, at])
    first = jnp.stack(messages[0::2], axis=1).reshape(128, 8, 128)
    second = jnp.stack(messages[1::2], axis=1).reshape(128, 8, 128)
    low = iota((128, 8, 128), 1) < 4
    left = jnp.where(low, first, pltpu.roll(second, 4, 1)).reshape(1024, 128)
    right = jnp.where(low, pltpu.roll(first, 4, 1), second).reshape(1024, 128)
    rows = jnp.concatenate([left, right], axis=1).astype(bf16)
    hits = hit_ref[...]
    sums = jnp.dot(hits, rows, preferred_element_type=f32)
    counts = lax.dot_general(jnp.ones((8, 1024), bf16), hits, NT, preferred_element_type=f32)
    keep_rate, add_rate = ema_decay, 1.0 - ema_decay
    out_ref[:CPD] = keep_rate * (add_rate * sums[:CPD]) + add_rate * sums[CPD:]
    out_ref[CPD:] = keep_rate * (add_rate * counts[:, :CPD]) + add_rate * counts[:, CPD:]


def partial_update(side, rows, queries):
    return pl.pallas_call(
        functools.partial(partial_kernel, side),
        out_shape=jax.ShapeDtypeStruct((CPD + 8, E), f32),
        in_specs=[pl.BlockSpec(memory_space=pltpu.VMEM), pl.BlockSpec(memory_space=pl.ANY)],
        scratch_shapes=[pltpu.VMEM((2 * CPD, 1024), bf16)],
        compiler_params=pltpu.CompilerParams(vmem_limit_bytes=32 << 20),
        cost_estimate=pl.CostEstimate(flops=1 << 29, bytes_accessed=2 << 20, transcendentals=0),
        name="partial",
    )(rows, queries)


def merge_kernel(own_ref, other_ref, counts_ref, sums_ref, codebook_ref, new_counts_ref, new_sums_ref, rounded_ref):
    rows = own_ref[CPD:] + other_ref[CPD:]
    rows = ema_decay * (ema_decay * counts_ref[...]) + rows
    sums = ema_decay * (ema_decay * sums_ref[...]) + (own_ref[:CPD] + other_ref[:CPD])
    cols = jnp.transpose(jnp.broadcast_to(rows[0:1], (128, CPD)))
    book = jnp.concatenate([sums[:, :128] / cols, sums[:, 128:] / cols], axis=1)
    codebook_ref[...] = book
    rounded_ref[...] = book.astype(bf16)
    new_sums_ref[...] = sums
    new_counts_ref[...] = rows[0:1]


def merge(own, other, counts, sums):
    return pl.pallas_call(
        merge_kernel,
        out_shape=(
            jax.ShapeDtypeStruct((CPD, E), f32),
            jax.ShapeDtypeStruct((1, CPD), f32),
            jax.ShapeDtypeStruct((CPD, E), f32),
            jax.ShapeDtypeStruct((CPD, E), bf16),
        ),
        compiler_params=pltpu.CompilerParams(vmem_limit_bytes=32 << 20),
        cost_estimate=pl.CostEstimate(flops=1 << 20, bytes_accessed=2 << 20, transcendentals=0),
        name="merge",
    )(own, other, counts.reshape(1, CPD), sums)


def nearest_kernel(codes, *refs):
    groups, width = 16, 512
    codes_refs, queries_ref, rest = refs[:codes], refs[codes], refs[codes + 1 :]
    out_ref = rest[-1]
    last = out_ref.shape == (groups, 4, 128)
    scaled, norms = [], []
    for codes_ref in codes_refs:
        part = codes_ref[...].astype(f32)
        norms.append(jnp.sum(part * part, axis=1, keepdims=True))
        scaled.append((-2.0 * part).astype(bf16))
    for g in range(groups):
        part = queries_ref[g * width : (g + 1) * width]
        best = rest[0][g] if len(rest) > 1 else None
        for m, n in zip(scaled, norms):
            value = lax.dot_general(m, part, NT, preferred_element_type=f32) + n
            value = jnp.min(value.reshape(CPD // 8, 8, width), axis=0)
            best = value if best is None else jnp.minimum(best, value)
        if last:
            line = jnp.min(best, axis=0, keepdims=True)
            out_ref[g] = jnp.concatenate([line[:, j * 128 : (j + 1) * 128] for j in range(4)], axis=0)
        else:
            out_ref[g] = best


def nearest_codes(codes, queries, best=None, last=False):
    shape = (16, 4, 128) if last else (16, 8, 512)
    operands = (*codes, queries) if best is None else (*codes, queries, best)
    return pl.pallas_call(
        functools.partial(nearest_kernel, len(codes)),
        out_shape=jax.ShapeDtypeStruct(shape, f32),
        compiler_params=pltpu.CompilerParams(vmem_limit_bytes=32 << 20),
        cost_estimate=pl.CostEstimate(
            flops=len(codes) << 30, bytes_accessed=5 << 20, transcendentals=0
        ),
        name="nearest",
    )(*operands)


def swap_cores(x):
    return lax.ppermute(x, "core", [(0, 1), (1, 0)])


def body(latents, batch_order, code_block, code_offset, ema_counts, ema_sums, queries):
    core = lax.axis_index("core").astype(i32)
    half = queries.shape[0] // 2
    mine = lax.dynamic_slice_in_dim(queries, core * half, half, 0)
    plane_queries = lax.all_gather(mine, ("x", "y"), axis=0, tiled=True)
    own = jnp.sum(jnp.square(queries.astype(f32)), axis=1)
    rows = build(
        core.reshape(1), latents, batch_order, code_block.reshape(1, -1), code_offset.reshape(1, -1)
    )
    got = lax.all_to_all(rows.reshape(256, 9, 2, 128), ("zh", "x", "y", "zl"), 0, 0, tiled=True)
    got = got.reshape(256 * 18, 128)
    arrived = plane_queries[:16]
    other_part = swap_cores(partial_update(1, got, arrived))
    own_part = partial_update(0, got, arrived)
    codebook, counts, sums, rounded = merge(own_part, other_part, ema_counts, ema_sums)
    far = lax.ppermute(rounded, ("zh", "zl"), [(z, 15 - z) for z in range(16)])
    near_other = swap_cores(rounded)
    best = nearest_codes((rounded, near_other), plane_queries)
    far, best = lax.optimization_barrier((far, best))
    far_other = swap_cores(far)
    best = nearest_codes((far,), plane_queries, best)
    best = nearest_codes((far_other,), plane_queries, best, last=True)
    found = jnp.min(lax.all_to_all(best, ("x", "y"), 0, 0, tiled=True), axis=0)
    found = jnp.broadcast_to(found[None], (16, 4, 128))
    found = lax.all_to_all(found, ("zl", "core"), 0, 0, tiled=True)
    found = jnp.min(found.reshape(8, 2, 4, 128), axis=0).reshape(-1)
    nearest = (own + found) / E
    return (codebook, counts.reshape(-1), sums, nearest)


def solution(mesh):
    fine = Mesh(mesh.devices.reshape(SIZES), AXES)
    placed = (
        P(AXES, None),
        P(AXES, None),
        P(AXES, None),
        P(AXES),
        P(AXES),
        P(AXES, None),
        P(("zh", "x", "y"), None),
    )
    return jax.shard_map(
        body,
        mesh=fine,
        in_specs=placed,
        out_specs=(P(AXES, None), P(AXES), P(AXES, None), P(("zh", "x", "y"))),
        check_vma=False,
    )
```

time: 179 us -> 166 us (0.927)
  blocking collectives: 25.5 us -> 12.8 us
  waiting for transfers between devices: 81.6 us -> 72.5 us
  starting transfers between devices: 39.1 us -> 48.1 us
    all_to_all x2, waiting for transfers between devices: 81 us -> 13.3 us  [the longest x1 9.62 us: body(): found = lax.all_to_all(found, ('zl', 'core'), 0, 0, tiled=True)]
    all_gather x1, waiting for transfers between devices: 0.01 us -> 49.8 us  [body(): plane_queries = lax.all_gather(mine, ('x', 'y'), axis=0, tiled=True)]
    all_gather x3 -> x0, blocking collectives: 25.5 us -> none  [the longest x1 11.7 us: body(): near = lax.all_gather(rounded, 'x', axis=0, tiled=True)]
    ppermute x1 -> x4, starting transfers between devices: 4.33 us -> 17.7 us  [the longest x3 12.7 us: swap_cores(): return lax.ppermute(x, 'core', [(0, 1), (1, 0)])]
    all_to_all x0 -> x1, blocking collectives: none -> 12.8 us  [body(): found = jnp.min(lax.all_to_all(best, ('x', 'y'), 0, 0, tiled=True), axis=0)]
    ppermute x1 -> x4, waiting for transfers between devices: 0.01 us -> 9.3 us  [the longest x1 9.15 us: body(): far = lax.ppermute(rounded, ('zh', 'zl'), [(z, 15 - z) for z in range(16)])]
    all_to_all x2, starting transfers between devices: 34.8 us -> 30.4 us  [the longest x1 25.5 us: body(): lax.all_to_all(rows.reshape(256, 9, 2, 128), ('zh', 'x', 'y', 'zl'), 0, 0...]
    pallas_call x3 -> x7, Pallas kernels: 15.2 us -> 13.6 us  [the longest x1 5.77 us: build(): pl.pallas_call(build_kernel, out_shape=jax.ShapeDtypeStruct((256 * 18, 12...]
  transfers between devices with their start and end apart: 4 -> 7, of which waited for: 2 -> 5; matrix products, arithmetic and copies ran while one was open for 0% -> 1% of each run, Pallas kernels for 2% -> 6%
where the time goes in v4:
time: 166 us; the launch traced here: 165 us
  waiting for transfers between devices  72.5 us (44%)
  starting transfers between devices  48.1 us (29%)
  between operations  14.2 us (9%)
  Pallas kernels  13.6 us (8%)
  blocking collectives  12.8 us (8%)
  local copies, waits for them, and re-layouts  3 us (2%)
    all_gather x1, waiting for transfers between devices, body(): plane_queries = lax.all_gather(mine, ('x', 'y'), axis=0, tiled=True)  49.8 us
    all_to_all x1, starting transfers between devices, body(): lax.all_to_all(rows.reshape(256, 9, 2, 128), ('zh', 'x', 'y', 'zl'), 0, 0...  25.5 us
    all_to_all x1, blocking collectives, body(): found = jnp.min(lax.all_to_all(best, ('x', 'y'), 0, 0, tiled=True), axis=0)  12.8 us
    ppermute x3, starting transfers between devices, swap_cores(): return lax.ppermute(x, 'core', [(0, 1), (1, 0)])  12.7 us
    all_to_all x1, waiting for transfers between devices, body(): found = lax.all_to_all(found, ('zl', 'core'), 0, 0, tiled=True)  9.62 us
    ppermute x1, waiting for transfers between devices, body(): far = lax.ppermute(rounded, ('zh', 'zl'), [(z, 15 - z) for z in range(16)])  9.15 us
    pallas_call x1, Pallas kernels, build(): pl.pallas_call(build_kernel, out_shape=jax.ShapeDtypeStruct((256 * 18, 12...  5.77 us
    pallas_call x3, Pallas kernels, nearest_codes(): pl.pallas_call(functools.partial(nearest_kernel, len(codes)), out_shape=j...  5.01 us
  transfers between devices with their start and end apart: 7, of which 5 were waited for; matrix products, arithmetic and copies ran while one was open for 1% of the time, Pallas kernels for 6%

profile of v4, /device:TPU:1, one launch (start us, length us, event | category | flops | bytes accessed | tf_op | source)
XLA Modules:
  0.0 165.1 jit_solution(9577453799442868218)
XLA Ops:
  7.2 0.0 all-gather.2.cloned.1.call-start
  7.2 1.7 %constant_dynamic-slice_fusion = bf16[512,256]{1,0:T(8,128)(2,1)} fusion(bf16[1024,256]{1,0:T(8,128)(2,1)} %param.13, s32[]{:T(128)S(6)} %select_n.3), kind=kLoop, calls=%fused_computation.2 | loop fusion | bytes 524292 | tf_op jit(solution)/shard_map/dynamic_slice | solution.py:244
  8.9 0.0 all-gather.2.cloned.1.call-update
  8.9 5.8 %build.1 = bf16[4608,128]{1,0:T(8,128)(2,1)} custom-call(s32[1]{0:T(128)} %bitcast.core_ref, bf16[1024,256]{1,0:T(8,128)(2,1)} %latents_hbm.1, s32[1,1024]{1,0:T(1,128)} %order_hbm.1, s32[1,1024]{1,0:T(1,128)} %bitcast.15, s32[1,1024]{1,0:T(1,128)} %bitcast.16), custom_call_target="tpu_custom_call" | custom-call | flops 3221225472 | bytes 2097152 | tf_op jit(solution)/shard_map/build/pallas_call | solution.py:106
  14.7 0.0 copy-start.1
  14.7 0.0 copy-start.2
  14.7 25.5 %all-to-all-start = ((bf16[256,9,2,128]{3,2,1,0:T(2,128)(2,1)}), bf16[256,9,2,128]{3,2,1,0:T(2,128)(2,1)S(1)}, u32[]{:S(2)}, u32[]{:S(2)}) async-start(bf16[256,9,2,128]{3,2,1,0:T(2,128)(2,1)} %bitcast.12), calls=%async_computation | async-start | bytes 2359296 | tf_op jit(solution)/shard_map/all_to_all | solution.py:250
  40.2 49.8 %all-gather.2.cloned.1.call-done.refs_2_.refs_1_ = bf16[8192,256]{1,0:T(8,128)(2,1)} async-done(((bf16[512,256]{1,0:T(8,128)(2,1)}), bf16[8192,256]{1,0:T(8,128)(2,1)}) %all-gather.2.cloned.1.call-update) | async-done | bytes 4194320 | tf_op jit(solution)/shard_map/all_gather | solution.py:245
  90.1 0.7 slice.4.queries_ref
  90.8 3.7 %all-to-all-done = bf16[256,9,2,128]{3,2,1,0:T(2,128)(2,1)S(1)} async-done(((bf16[256,9,2,128]{3,2,1,0:T(2,128)(2,1)}), bf16[256,9,2,128]{3,2,1,0:T(2,128)(2,1)S(1)}, u32[]{:S(2)}, u32[]{:S(2)}) %all-to-all-start) | async-done | bytes 1179680 | tf_op jit(solution)/shard_map/all_to_all | solution.py:250
  94.5 0.0 copy-start
  94.5 1.0 partial.3
  95.5 7.8 %collective-permute-start = (f32[264,256]{1,0:T(8,128)S(1)}, f32[264,256]{1,0:T(8,128)S(1)}, u32[]{:S(2)}, u32[]{:S(2)}) collective-permute-start(f32[264,256]{1,0:T(8,128)S(1)} %partial.3), channel_id=1, source_target_pairs={{0,1},{1,0},{2,3},{3,2},{4,5},{5,4},{6,7},{7,6},{8,9},{9,8},{10,11... | collective-permute-start | bytes 811016 | tf_op jit(solution)/shard_map/ppermute | solution.py:238
  103.3 1.0 partial.2.own_ref
  104.4 0.1 collective-permute-done.other_ref
  104.5 0.0 copy-done.1
  104.5 0.0 copy-done.2
  104.5 0.9 merge.1
  105.4 2.3 %collective-permute-start.2 = (bf16[256,256]{1,0:T(8,128)(2,1)S(1)}, bf16[256,256]{1,0:T(8,128)(2,1)S(1)}, u32[]{:S(2)}, u32[]{:S(2)}) collective-permute-start(bf16[256,256]{1,0:T(8,128)(2,1)S(1)} %get-tuple-element.13.refs_0_), channel_id=1, source_target_pairs={{0,1},{1,0},{2,3},{3,2},{4,5},{5,4},{6,7},{7,6},{8,9},{9,8},{10,11... | collective-permute-start | bytes 393224 | tf_op jit(solution)/shard_map/ppermute | solution.py:238
  107.6 5.0 %collective-permute-start.1 = (bf16[256,256]{1,0:T(8,128)(2,1)S(1)}, bf16[256,256]{1,0:T(8,128)(2,1)S(1)}, u32[]{:S(2)}, u32[]{:S(2)}) collective-permute-start(bf16[256,256]{1,0:T(8,128)(2,1)S(1)} %get-tuple-element.13.refs_0_), channel_id=1, source_target_pairs={{0,270},{2,268},{4,266},{6,264},{8,262},{10,260},{12,258},{14,256}... | collective-permute-start | bytes 393224 | tf_op jit(solution)/shard_map/ppermute | solution.py:256
  112.6 0.0 collective-permute-done.2.refs_1_
  112.7 0.0 copy-done
  112.7 2.4 %nearest.3.refs_2_ = f32[16,8,512]{2,1,0:T(8,128)S(1)} custom-call(bf16[256,256]{1,0:T(8,128)(2,1)S(1)} %get-tuple-element.13.refs_0_, bf16[256,256]{1,0:T(8,128)(2,1)S(1)} %collective-permute-done.2.refs_1_, bf16[8192,256]{1,0:T(8,128)(2,1)S(1)} %copy-done), custom_call_target="tpu_custom_call" | custom-call | flops 2147483648 | bytes 5242880 | tf_op jit(solution)/shard_map/nearest/pallas_call | solution.py:226
  115.1 9.2 %collective-permute-done.1.refs_0_ = bf16[256,256]{1,0:T(8,128)(2,1)S(1)} collective-permute-done((bf16[256,256]{1,0:T(8,128)(2,1)S(1)}, bf16[256,256]{1,0:T(8,128)(2,1)S(1)}, u32[]{:S(2)}, u32[]{:S(2)}) %collective-permute-start.1) | collective-permute-done | bytes 131104 | tf_op jit(solution)/shard_map/ppermute | solution.py:256
  124.2 2.6 %collective-permute-start.3 = (bf16[256,256]{1,0:T(8,128)(2,1)S(1)}, bf16[256,256]{1,0:T(8,128)(2,1)S(1)}, u32[]{:S(2)}, u32[]{:S(2)}) collective-permute-start(bf16[256,256]{1,0:T(8,128)(2,1)S(1)} %collective-permute-done.1.refs_0_), channel_id=1, source_target_pairs={{0,1},{1,0},{2,3},{3,2},{4,5},{5,4},{6,7},{7,6},{8,9},{9,8},{10,11... | collective-permute-start | bytes 393224 | tf_op jit(solution)/shard_map/ppermute | solution.py:238
  126.8 1.3 nearest.4.refs_2_
  128.1 0.0 copy-start.3
  128.1 0.0 collective-permute-done.3.refs_0_
  128.1 1.3 nearest.5
  129.4 12.8 %all_to_all.15 = f32[16,4,128]{2,1,0:T(4,128)S(1)} all-to-all(f32[16,4,128]{2,1,0:T(4,128)S(1)} %nearest.5), channel_id=1, replica_groups=mesh['zh'=2,'x'=4,'y'=4,'zl'=8,'core'=2] {'x','y'}, dimensions={0} | all-to-all | bytes 65536 | tf_op jit(solution)/shard_map/all_to_all | solution.py:263
  142.3 0.6 broadcast_in_dim.2
  142.9 4.9 %all-to-all-start.2 = ((f32[16,4,128]{2,1,0:T(4,128)}), f32[16,4,128]{2,1,0:T(4,128)S(1)}, u32[]{:S(2)}, u32[]{:S(2)}) async-start(f32[16,4,128]{2,1,0:T(4,128)} %broadcast_in_dim.2), calls=%async_computation.2 | async-start | bytes 65536 | tf_op jit(solution)/shard_map/all_to_all | solution.py:265
  147.8 0.0 copy-done.3
  147.8 0.2 multiply_reduce_fusion
  148.0 9.6 %all-to-all-done.2 = f32[16,4,128]{2,1,0:T(4,128)S(1)} async-done(((f32[16,4,128]{2,1,0:T(4,128)}), f32[16,4,128]{2,1,0:T(4,128)S(1)}, u32[]{:S(2)}, u32[]{:S(2)}) %all-to-all-start.2) | async-done | bytes 32800 | tf_op jit(solution)/shard_map/all_to_all | solution.py:265
  157.7 0.6 add_multiply_fusion
  (2 shorter events, 0.0 us)
Async XLA Ops:
  7.2 82.9 %all-gather.2.cloned.1.call-start = ((), (), s32[]{:S(2)}) async-start(), calls=%async_computation.3 | async-start | bytes 4456448 | tf_op jit(solution)/shard_map/all_gather | solution.py:245
  14.7 89.8 %copy-start.1 = (f32[256,256]{1,0:T(8,128)S(1)}, f32[256,256]{1,0:T(8,128)}, u32[]{:S(2)}) copy-start(f32[256,256]{1,0:T(8,128)} %sums_ref.1) | copy-start | bytes 786436
  14.7 89.8 %copy-start.2 = (f32[256]{0:T(256)S(1)}, f32[256]{0:T(256)}, u32[]{:S(2)}) copy-start(f32[256]{0:T(256)} %param.11) | copy-start | bytes 3076
  14.7 79.8 %all-to-all-start = ((bf16[256,9,2,128]{3,2,1,0:T(2,128)(2,1)}), bf16[256,9,2,128]{3,2,1,0:T(2,128)(2,1)S(1)}, u32[]{:S(2)}, u32[]{:S(2)}) async-start(bf16[256,9,2,128]{3,2,1,0:T(2,128)(2,1)} %bitcast.12), calls=%async_computation | async-start | bytes 2359296 | tf_op jit(solution)/shard_map/all_to_all | solution.py:250
  94.5 18.2 %copy-start = (bf16[8192,256]{1,0:T(8,128)(2,1)S(1)}, bf16[8192,256]{1,0:T(8,128)(2,1)}, u32[]{:S(2)}) copy-start(bf16[8192,256]{1,0:T(8,128)(2,1)} %all-gather.2.cloned.1.call-done.refs_2_.refs_1_) | copy-start | bytes 12582916
  95.5 9.0 %collective-permute-start = (f32[264,256]{1,0:T(8,128)S(1)}, f32[264,256]{1,0:T(8,128)S(1)}, u32[]{:S(2)}, u32[]{:S(2)}) collective-permute-start(f32[264,256]{1,0:T(8,128)S(1)} %partial.3), channel_id=1, source_target_pairs={{0,1},{1,0},{2,3},{3,2},{4,5},{5,4},{6,7},{7,6},{8,9},{9,8},{10,11... | collective-permute-start | bytes 811016 | tf_op jit(solution)/shard_map/ppermute | solution.py:238
  105.4 7.3 %collective-permute-start.2 = (bf16[256,256]{1,0:T(8,128)(2,1)S(1)}, bf16[256,256]{1,0:T(8,128)(2,1)S(1)}, u32[]{:S(2)}, u32[]{:S(2)}) collective-permute-start(bf16[256,256]{1,0:T(8,128)(2,1)S(1)} %get-tuple-element.13.refs_0_), channel_id=1, source_target_pairs={{0,1},{1,0},{2,3},{3,2},{4,5},{5,4},{6,7},{7,6},{8,9},{9,8},{10,11... | collective-permute-start | bytes 393224 | tf_op jit(solution)/shard_map/ppermute | solution.py:238
  107.6 16.6 %collective-permute-start.1 = (bf16[256,256]{1,0:T(8,128)(2,1)S(1)}, bf16[256,256]{1,0:T(8,128)(2,1)S(1)}, u32[]{:S(2)}, u32[]{:S(2)}) collective-permute-start(bf16[256,256]{1,0:T(8,128)(2,1)S(1)} %get-tuple-element.13.refs_0_), channel_id=1, source_target_pairs={{0,270},{2,268},{4,266},{6,264},{8,262},{10,260},{12,258},{14,256}... | collective-permute-start | bytes 393224 | tf_op jit(solution)/shard_map/ppermute | solution.py:256
  124.2 3.9 %collective-permute-start.3 = (bf16[256,256]{1,0:T(8,128)(2,1)S(1)}, bf16[256,256]{1,0:T(8,128)(2,1)S(1)}, u32[]{:S(2)}, u32[]{:S(2)}) collective-permute-start(bf16[256,256]{1,0:T(8,128)(2,1)S(1)} %collective-permute-done.1.refs_0_), channel_id=1, source_target_pairs={{0,1},{1,0},{2,3},{3,2},{4,5},{5,4},{6,7},{7,6},{8,9},{9,8},{10,11... | collective-permute-start | bytes 393224 | tf_op jit(solution)/shard_map/ppermute | solution.py:238
  128.1 19.7 %copy-start.3 = (bf16[1024,256]{1,0:T(8,128)(2,1)S(1)}, bf16[1024,256]{1,0:T(8,128)(2,1)}, u32[]{:S(2)}) copy-start(bf16[1024,256]{1,0:T(8,128)(2,1)} %param.13) | copy-start | bytes 1572868
  142.9 14.7 %all-to-all-start.2 = ((f32[16,4,128]{2,1,0:T(4,128)}), f32[16,4,128]{2,1,0:T(4,128)S(1)}, u32[]{:S(2)}, u32[]{:S(2)}) async-start(f32[16,4,128]{2,1,0:T(4,128)} %broadcast_in_dim.2), calls=%async_computation.2 | async-start | bytes 65536 | tf_op jit(solution)/shard_map/all_to_all | solution.py:265
Sparse Core Ops, SparseCore 0:
  11.6 78.4 all-gather.1

commit v5 on v4

--- a/solution.py
+++ b/solution.py
@@ -31,8 +31,8 @@
     return jnp.where(hit, 1.0, 0.0).astype(bf16)
 
 
-def build_kernel(core_ref, latents_hbm, order_hbm, block_hbm, offset_hbm, rows_ref,
-                 latents_ref, order_ref, block_ref, offset_ref, sems):
+def build_kernel(core_ref, latents_hbm, order_hbm, block_hbm, offset_hbm, queries_hbm,
+                 rows_ref, half_hbm, latents_ref, order_ref, block_ref, offset_ref, sems):
     tokens = latents_ref.shape[0]
     step = tokens // STEPS
     copies = [
@@ -43,6 +43,10 @@
     ]
     for copy in copies:
         copy.start()
+    half = half_hbm.shape[0]
+    side = pl.multiple_of(core_ref[0] * half, half)
+    half_copy = pltpu.make_async_copy(queries_hbm.at[pl.ds(side, half)], half_hbm, sems.at[4])
+    half_copy.start()
     copies[0].wait()
     block = block_ref[...] ^ core_ref[0]
     earlier = one_hot(iota((step, step), 0) < iota((step, step), 1))
@@ -100,24 +104,32 @@
         rows_ref[c * count : (c + 1) * count] = (
             jnp.stack(tiles, axis=1).reshape(count, 128).astype(bf16)
         )
-
-
-def build(core, latents, order, block, offset):
+    half_copy.wait()
+
+
+def build(core, latents, order, block, offset, queries):
     return pl.pallas_call(
         build_kernel,
-        out_shape=jax.ShapeDtypeStruct((256 * 18, 128), bf16),
-        in_specs=[pl.BlockSpec(memory_space=pltpu.SMEM)] + [pl.BlockSpec(memory_space=pltpu.HBM)] * 4,
+        out_shape=(
+            jax.ShapeDtypeStruct((256 * 18, 128), bf16),
+            jax.ShapeDtypeStruct((512, E), bf16),
+        ),
+        in_specs=[pl.BlockSpec(memory_space=pltpu.SMEM)] + [pl.BlockSpec(memory_space=pltpu.HBM)] * 5,
+        out_specs=(
+            pl.BlockSpec(memory_space=pltpu.VMEM),
+            pl.BlockSpec(memory_space=pltpu.HBM),
+        ),
         scratch_shapes=[
             pltpu.VMEM((1024, E), bf16),
             pltpu.VMEM((1, 1024), i32),
             pltpu.VMEM((1, 1024), i32),
             pltpu.VMEM((1, 1024), i32),
-            pltpu.SemaphoreType.DMA((4,)),
+            pltpu.SemaphoreType.DMA((5,)),
         ],
         compiler_params=pltpu.CompilerParams(vmem_limit_bytes=60 << 20),
         cost_estimate=pl.CostEstimate(flops=3 << 30, bytes_accessed=2 << 20, transcendentals=0),
         name="build",
-    )(core, latents, order, block, offset)
+    )(core, latents, order, block, offset, queries)
 
 
 def partial_kernel(side, rows_ref, queries_ref, out_ref, hit_ref):
@@ -211,7 +223,7 @@
         best = rest[0][g] if len(rest) > 1 else None
         for m, n in zip(scaled, norms):
             value = lax.dot_general(m, part, NT, preferred_element_type=f32) + n
-            value = jnp.min(value.reshape(CPD // 8, 8, width), axis=0)
+            value = jnp.min(value.reshape(-1, 8, width), axis=0)
             best = value if best is None else jnp.minimum(best, value)
         if last:
             line = jnp.min(best, axis=0, keepdims=True)
@@ -240,13 +252,16 @@
 
 def body(latents, batch_order, code_block, code_offset, ema_counts, ema_sums, queries):
     core = lax.axis_index("core").astype(i32)
-    half = queries.shape[0] // 2
-    mine = lax.dynamic_slice_in_dim(queries, core * half, half, 0)
+    own = jnp.sum(jnp.square(queries.astype(f32)), axis=1)
+    rows, mine = build(
+        core.reshape(1),
+        latents,
+        batch_order,
+        code_block.reshape(1, -1),
+        code_offset.reshape(1, -1),
+        queries,
+    )
     plane_queries = lax.all_gather(mine, ("x", "y"), axis=0, tiled=True)
-    own = jnp.sum(jnp.square(queries.astype(f32)), axis=1)
-    rows = build(
-        core.reshape(1), latents, batch_order, code_block.reshape(1, -1), code_offset.reshape(1, -1)
-    )
     got = lax.all_to_all(rows.reshape(256, 9, 2, 128), ("zh", "x", "y", "zl"), 0, 0, tiled=True)
     got = got.reshape(256 * 18, 128)
     arrived = plane_queries[:16]
@@ -254,8 +269,8 @@
     own_part = partial_update(0, got, arrived)
     codebook, counts, sums, rounded = merge(own_part, other_part, ema_counts, ema_sums)
     far = lax.ppermute(rounded, ("zh", "zl"), [(z, 15 - z) for z in range(16)])
-    near_other = swap_cores(rounded)
-    best = nearest_codes((rounded, near_other), plane_queries)
+    near = lax.all_gather(rounded, "core", axis=0, tiled=True)
+    best = nearest_codes((near,), plane_queries)
     far, best = lax.optimization_barrier((far, best))
     far_other = swap_cores(far)
     best = nearest_codes((far,), plane_queries, best)

time: 166 us -> 166 us (level)
  Pallas kernels: 13.6 us -> 18 us
  blocking collectives: 12.8 us -> 15.2 us
  starting transfers between devices: 48.1 us -> 45.8 us
  waiting for transfers between devices: 72.5 us -> 70.2 us
  local copies, waits for them, and re-layouts: 3 us -> 1.33 us
    pallas_call x1, Pallas kernels: 5.77 us -> 10.1 us  [build(): pl.pallas_call(build_kernel, out_shape=(jax.ShapeDtypeStruct((256 * 18, 1...]
    all_gather x1, waiting for transfers between devices: 49.8 us -> 53.5 us  [body(): plane_queries = lax.all_gather(mine, ('x', 'y'), axis=0, tiled=True)]
    all_to_all x1, waiting for transfers between devices: 3.73 us -> 0.07 us  [body(): lax.all_to_all(rows.reshape(256, 9, 2, 128), ('zh', 'x', 'y', 'zl'), 0, 0...]
    all_gather x0 -> x1, blocking collectives: none -> 2.29 us  [body(): near = lax.all_gather(rounded, 'core', axis=0, tiled=True)]
    ppermute x1, waiting for transfers between devices: 9.15 us -> 6.87 us  [body(): far = lax.ppermute(rounded, ('zh', 'zl'), [(z, 15 - z) for z in range(16)])]
    ppermute x3 -> x2, starting transfers between devices: 12.7 us -> 10.4 us  [swap_cores(): return lax.ppermute(x, 'core', [(0, 1), (1, 0)])]
    dynamic_slice x1 -> x0, local copies, waits for them, and re-layouts: 1.67 us -> none  [body(): mine = lax.dynamic_slice_in_dim(queries, core * half, half, 0)]
  transfers between devices with their start and end apart: 7 -> 6, of which waited for: 5 -> 5; matrix products, arithmetic and copies ran while one was open for 1% -> 1% of each run, Pallas kernels for 6% -> 3%
where the time goes in v5:
time: 166 us; the launch traced here: 165 us
  waiting for transfers between devices  70.2 us (42%)
  starting transfers between devices  45.8 us (28%)
  Pallas kernels  18 us (11%)
  blocking collectives  15.2 us (9%)
  between operations  14.2 us (9%)
    all_gather x1, waiting for transfers between devices, body(): plane_queries = lax.all_gather(mine, ('x', 'y'), axis=0, tiled=True)  53.5 us
    all_to_all x1, starting transfers between devices, body(): lax.all_to_all(rows.reshape(256, 9, 2, 128), ('zh', 'x', 'y', 'zl'), 0, 0...  25.5 us
    all_to_all x1, blocking collectives, body(): found = jnp.min(lax.all_to_all(best, ('x', 'y'), 0, 0, tiled=True), axis=0)  12.9 us
    ppermute x2, starting transfers between devices, swap_cores(): return lax.ppermute(x, 'core', [(0, 1), (1, 0)])  10.4 us
    pallas_call x1, Pallas kernels, build(): pl.pallas_call(build_kernel, out_shape=(jax.ShapeDtypeStruct((256 * 18, 1...  10.1 us
    all_to_all x1, waiting for transfers between devices, body(): found = lax.all_to_all(found, ('zl', 'core'), 0, 0, tiled=True)  9.62 us
    ppermute x1, waiting for transfers between devices, body(): far = lax.ppermute(rounded, ('zh', 'zl'), [(z, 15 - z) for z in range(16)])  6.87 us
    pallas_call x3, Pallas kernels, nearest_codes(): pl.pallas_call(functools.partial(nearest_kernel, len(codes)), out_shape=j...  5 us
  transfers between devices with their start and end apart: 6, of which 5 were waited for; matrix products, arithmetic and copies ran while one was open for 1% of the time, Pallas kernels for 3%

profile of v5, /device:TPU:1, one launch (start us, length us, event | category | flops | bytes accessed | tf_op | source)
XLA Modules:
  0.0 165.5 jit_solution(14096766850610357960)
XLA Ops:
  7.2 0.0 all-gather.2.cloned.1.call-start
  7.2 10.1 %build.1 = (bf16[4608,128]{1,0:T(8,128)(2,1)}, bf16[512,256]{1,0:T(8,128)(2,1)}) custom-call(s32[1]{0:T(128)} %bitcast.core_ref, bf16[1024,256]{1,0:T(8,128)(2,1)} %latents_hbm.1, s32[1,1024]{1,0:T(1,128)} %order_hbm.1, s32[1,1024]{1,0:T(1,128)} %bitcast.15, s32[1,1024]{1,0:T(1,128)} %bitcast.16, bf16[1024,256]{1,0:T(8,128)(2,1)} %queries_hbm.1), custom_call_target="tpu_custom_call" | custom-call | flops 3221225472 | bytes 2097152 | tf_op jit(solution)/shard_map/build/pallas_call | solution.py:111
  17.3 0.0 all-gather.2.cloned.1.call-update
  17.4 0.0 copy-start.1
  17.4 0.0 copy-start.2
  17.4 25.5 %all-to-all-start = ((bf16[256,9,2,128]{3,2,1,0:T(2,128)(2,1)}), bf16[256,9,2,128]{3,2,1,0:T(2,128)(2,1)S(1)}, u32[]{:S(2)}, u32[]{:S(2)}) async-start(bf16[256,9,2,128]{3,2,1,0:T(2,128)(2,1)} %bitcast.12), calls=%async_computation | async-start | bytes 2359296 | tf_op jit(solution)/shard_map/all_to_all | solution.py:265
  42.9 53.5 %all-gather.2.cloned.1.call-done.refs_1_ = bf16[8192,256]{1,0:T(8,128)(2,1)} async-done(((bf16[512,256]{1,0:T(8,128)(2,1)}), bf16[8192,256]{1,0:T(8,128)(2,1)}) %all-gather.2.cloned.1.call-update) | async-done | bytes 4194320 | tf_op jit(solution)/shard_map/all_gather | solution.py:264
  96.4 0.7 slice.4.queries_ref
  97.1 0.1 all-to-all-done
  97.1 0.0 copy-start
  97.1 1.0 partial.3
  98.1 7.8 %collective-permute-start = (f32[264,256]{1,0:T(8,128)S(1)}, f32[264,256]{1,0:T(8,128)S(1)}, u32[]{:S(2)}, u32[]{:S(2)}) collective-permute-start(f32[264,256]{1,0:T(8,128)S(1)} %partial.3), channel_id=1, source_target_pairs={{0,1},{1,0},{2,3},{3,2},{4,5},{5,4},{6,7},{7,6},{8,9},{9,8},{10,11... | collective-permute-start | bytes 811016 | tf_op jit(solution)/shard_map/ppermute | solution.py:250
  106.0 1.0 partial.2.own_ref
  107.0 0.1 collective-permute-done.other_ref
  107.2 0.0 copy-done.1
  107.2 0.0 copy-done.2
  107.2 0.9 merge.1
  108.0 5.0 %collective-permute-start.1 = (bf16[256,256]{1,0:T(8,128)(2,1)S(1)}, bf16[256,256]{1,0:T(8,128)(2,1)S(1)}, u32[]{:S(2)}, u32[]{:S(2)}) collective-permute-start(bf16[256,256]{1,0:T(8,128)(2,1)S(1)} %get-tuple-element.17), channel_id=1, source_target_pairs={{0,270},{2,268},{4,266},{6,264},{8,262},{10,260},{12,258},{14,256}... | collective-permute-start | bytes 393224 | tf_op jit(solution)/shard_map/ppermute | solution.py:271
  113.0 2.3 %all_gather.7.refs_0_ = bf16[512,256]{1,0:T(8,128)(2,1)S(1)} all-gather(bf16[256,256]{1,0:T(8,128)(2,1)S(1)} %get-tuple-element.17), channel_id=1, replica_groups=mesh['zh'=2,'x'=4,'y'=4,'zl'=8,'core'=2] {'core'}, dimensions={0}, use_global_device_ids=true | all-gather | bytes 393216 | tf_op jit(solution)/shard_map/all_gather | solution.py:272
  115.3 0.0 copy-done
  115.3 2.4 %nearest.3.refs_2_ = f32[16,8,512]{2,1,0:T(8,128)S(1)} custom-call(bf16[512,256]{1,0:T(8,128)(2,1)S(1)} %all_gather.7.refs_0_, bf16[8192,256]{1,0:T(8,128)(2,1)S(1)} %copy-done), custom_call_target="tpu_custom_call" | custom-call | flops 1073741824 | bytes 5242880 | tf_op jit(solution)/shard_map/nearest/pallas_call | solution.py:238
  117.7 6.9 %collective-permute-done.1.refs_0_ = bf16[256,256]{1,0:T(8,128)(2,1)S(1)} collective-permute-done((bf16[256,256]{1,0:T(8,128)(2,1)S(1)}, bf16[256,256]{1,0:T(8,128)(2,1)S(1)}, u32[]{:S(2)}, u32[]{:S(2)}) %collective-permute-start.1) | collective-permute-done | bytes 131104 | tf_op jit(solution)/shard_map/ppermute | solution.py:271
  124.6 2.6 %collective-permute-start.2 = (bf16[256,256]{1,0:T(8,128)(2,1)S(1)}, bf16[256,256]{1,0:T(8,128)(2,1)S(1)}, u32[]{:S(2)}, u32[]{:S(2)}) collective-permute-start(bf16[256,256]{1,0:T(8,128)(2,1)S(1)} %collective-permute-done.1.refs_0_), channel_id=1, source_target_pairs={{0,1},{1,0},{2,3},{3,2},{4,5},{5,4},{6,7},{7,6},{8,9},{9,8},{10,11... | collective-permute-start | bytes 393224 | tf_op jit(solution)/shard_map/ppermute | solution.py:250
  127.1 1.3 nearest.4.refs_2_
  128.4 0.0 copy-start.3
  128.5 0.0 collective-permute-done.2.refs_0_
  128.5 1.3 nearest.5
  129.8 12.9 %all_to_all.15 = f32[16,4,128]{2,1,0:T(4,128)S(1)} all-to-all(f32[16,4,128]{2,1,0:T(4,128)S(1)} %nearest.5), channel_id=1, replica_groups=mesh['zh'=2,'x'=4,'y'=4,'zl'=8,'core'=2] {'x','y'}, dimensions={0} | all-to-all | bytes 65536 | tf_op jit(solution)/shard_map/all_to_all | solution.py:278
  142.7 0.6 broadcast_in_dim.2
  143.3 4.9 %all-to-all-start.2 = ((f32[16,4,128]{2,1,0:T(4,128)}), f32[16,4,128]{2,1,0:T(4,128)S(1)}, u32[]{:S(2)}, u32[]{:S(2)}) async-start(f32[16,4,128]{2,1,0:T(4,128)} %broadcast_in_dim.2), calls=%async_computation.2 | async-start | bytes 65536 | tf_op jit(solution)/shard_map/all_to_all | solution.py:280
  148.2 0.0 copy-done.3
  148.2 0.2 multiply_reduce_fusion
  148.4 9.6 %all-to-all-done.2 = f32[16,4,128]{2,1,0:T(4,128)S(1)} async-done(((f32[16,4,128]{2,1,0:T(4,128)}), f32[16,4,128]{2,1,0:T(4,128)S(1)}, u32[]{:S(2)}, u32[]{:S(2)}) %all-to-all-start.2) | async-done | bytes 32800 | tf_op jit(solution)/shard_map/all_to_all | solution.py:280
  158.0 0.6 add_multiply_fusion
  (2 shorter events, 0.0 us)
Async XLA Ops:
  7.2 89.2 %all-gather.2.cloned.1.call-start = ((), (), s32[]{:S(2)}) async-start(), calls=%async_computation.3 | async-start | bytes 4456448 | tf_op jit(solution)/shard_map/all_gather | solution.py:264
  17.4 89.8 %copy-start.1 = (f32[256,256]{1,0:T(8,128)S(1)}, f32[256,256]{1,0:T(8,128)}, u32[]{:S(2)}) copy-start(f32[256,256]{1,0:T(8,128)} %sums_ref.1) | copy-start | bytes 786436
  17.4 89.8 %copy-start.2 = (f32[256]{0:T(256)S(1)}, f32[256]{0:T(256)}, u32[]{:S(2)}) copy-start(f32[256]{0:T(256)} %param.11) | copy-start | bytes 3076
  17.4 79.8 %all-to-all-start = ((bf16[256,9,2,128]{3,2,1,0:T(2,128)(2,1)}), bf16[256,9,2,128]{3,2,1,0:T(2,128)(2,1)S(1)}, u32[]{:S(2)}, u32[]{:S(2)}) async-start(bf16[256,9,2,128]{3,2,1,0:T(2,128)(2,1)} %bitcast.12), calls=%async_computation | async-start | bytes 2359296 | tf_op jit(solution)/shard_map/all_to_all | solution.py:265
  97.1 18.2 %copy-start = (bf16[8192,256]{1,0:T(8,128)(2,1)S(1)}, bf16[8192,256]{1,0:T(8,128)(2,1)}, u32[]{:S(2)}) copy-start(bf16[8192,256]{1,0:T(8,128)(2,1)} %all-gather.2.cloned.1.call-done.refs_1_) | copy-start | bytes 12582916
  98.1 9.0 %collective-permute-start = (f32[264,256]{1,0:T(8,128)S(1)}, f32[264,256]{1,0:T(8,128)S(1)}, u32[]{:S(2)}, u32[]{:S(2)}) collective-permute-start(f32[264,256]{1,0:T(8,128)S(1)} %partial.3), channel_id=1, source_target_pairs={{0,1},{1,0},{2,3},{3,2},{4,5},{5,4},{6,7},{7,6},{8,9},{9,8},{10,11... | collective-permute-start | bytes 811016 | tf_op jit(solution)/shard_map/ppermute | solution.py:250
  108.0 16.6 %collective-permute-start.1 = (bf16[256,256]{1,0:T(8,128)(2,1)S(1)}, bf16[256,256]{1,0:T(8,128)(2,1)S(1)}, u32[]{:S(2)}, u32[]{:S(2)}) collective-permute-start(bf16[256,256]{1,0:T(8,128)(2,1)S(1)} %get-tuple-element.17), channel_id=1, source_target_pairs={{0,270},{2,268},{4,266},{6,264},{8,262},{10,260},{12,258},{14,256}... | collective-permute-start | bytes 393224 | tf_op jit(solution)/shard_map/ppermute | solution.py:271
  124.6 3.9 %collective-permute-start.2 = (bf16[256,256]{1,0:T(8,128)(2,1)S(1)}, bf16[256,256]{1,0:T(8,128)(2,1)S(1)}, u32[]{:S(2)}, u32[]{:S(2)}) collective-permute-start(bf16[256,256]{1,0:T(8,128)(2,1)S(1)} %collective-permute-done.1.refs_0_), channel_id=1, source_target_pairs={{0,1},{1,0},{2,3},{3,2},{4,5},{5,4},{6,7},{7,6},{8,9},{9,8},{10,11... | collective-permute-start | bytes 393224 | tf_op jit(solution)/shard_map/ppermute | solution.py:250
  128.4 19.7 %copy-start.3 = (bf16[1024,256]{1,0:T(8,128)(2,1)S(1)}, bf16[1024,256]{1,0:T(8,128)(2,1)}, u32[]{:S(2)}) copy-start(bf16[1024,256]{1,0:T(8,128)(2,1)} %queries_hbm.1) | copy-start | bytes 1572868
  143.3 14.7 %all-to-all-start.2 = ((f32[16,4,128]{2,1,0:T(4,128)}), f32[16,4,128]{2,1,0:T(4,128)S(1)}, u32[]{:S(2)}, u32[]{:S(2)}) async-start(f32[16,4,128]{2,1,0:T(4,128)} %broadcast_in_dim.2), calls=%async_computation.2 | async-start | bytes 65536 | tf_op jit(solution)/shard_map/all_to_all | solution.py:280
Sparse Core Ops, SparseCore 0:
  17.5 78.8 all-gather.1

commit v6 on v5

--- a/solution.py
+++ b/solution.py
@@ -32,7 +32,8 @@
 
 
 def build_kernel(core_ref, latents_hbm, order_hbm, block_hbm, offset_hbm, queries_hbm,
-                 rows_ref, half_hbm, latents_ref, order_ref, block_ref, offset_ref, sems):
+                 rows_ref, half_hbm, half_ref, latents_ref, order_ref,
+                 block_ref, offset_ref, sems):
     tokens = latents_ref.shape[0]
     step = tokens // STEPS
     copies = [
@@ -45,8 +46,8 @@
         copy.start()
     half = half_hbm.shape[0]
     side = pl.multiple_of(core_ref[0] * half, half)
-    half_copy = pltpu.make_async_copy(queries_hbm.at[pl.ds(side, half)], half_hbm, sems.at[4])
-    half_copy.start()
+    half_in = pltpu.make_async_copy(queries_hbm.at[pl.ds(side, half)], half_ref, sems.at[4])
+    half_in.start()
     copies[0].wait()
     block = block_ref[...] ^ core_ref[0]
     earlier = one_hot(iota((step, step), 0) < iota((step, step), 1))
@@ -66,6 +67,9 @@
     labels = lax.dot_general(named, lanes, NT, preferred_element_type=f32)
     labels = jnp.where((iota((512, 128), 0) & 1) == 1, pltpu.roll(labels, 4, 1), labels)
     labels = labels.reshape(64, 8, 128)
+    half_in.wait()
+    half_out = pltpu.make_async_copy(half_ref, half_hbm, sems.at[5])
+    half_out.start()
     digits = jnp.where(iota((8, tokens), 0) == 0, place >> 6, place & 63).astype(f32).astype(bf16)
     copies[2].wait()
     stored = one_hot(iota((tokens, tokens), 0) == order_ref[...])
@@ -104,7 +108,7 @@
         rows_ref[c * count : (c + 1) * count] = (
             jnp.stack(tiles, axis=1).reshape(count, 128).astype(bf16)
         )
-    half_copy.wait()
+    half_out.wait()
 
 
 def build(core, latents, order, block, offset, queries):
@@ -120,11 +124,12 @@
             pl.BlockSpec(memory_space=pltpu.HBM),
         ),
         scratch_shapes=[
+            pltpu.VMEM((512, E), bf16),
             pltpu.VMEM((1024, E), bf16),
             pltpu.VMEM((1, 1024), i32),
             pltpu.VMEM((1, 1024), i32),
             pltpu.VMEM((1, 1024), i32),
-            pltpu.SemaphoreType.DMA((5,)),
+            pltpu.SemaphoreType.DMA((6,)),
         ],
         compiler_params=pltpu.CompilerParams(vmem_limit_bytes=60 << 20),
         cost_estimate=pl.CostEstimate(flops=3 << 30, bytes_accessed=2 << 20, transcendentals=0),

time: 166 us -> 162 us (0.976)
  Pallas kernels: 18 us -> 13.6 us
    pallas_call x1, Pallas kernels: 10.1 us -> 5.8 us  [build(): pl.pallas_call(build_kernel, out_shape=(jax.ShapeDtypeStruct((256 * 18, 1...]
  transfers between devices with their start and end apart: 6 -> 6, of which waited for: 5 -> 4; matrix products, arithmetic and copies ran while one was open for 1% -> 1% of each run, Pallas kernels for 3% -> 3%
where the time goes in v6:
time: 162 us; the launch traced here: 161 us
  waiting for transfers between devices  70.4 us (43%)
  starting transfers between devices  45.6 us (28%)
  blocking collectives  15.2 us (9%)
  between operations  14.2 us (9%)
  Pallas kernels  13.6 us (8%)
    all_gather x1, waiting for transfers between devices, body(): plane_queries = lax.all_gather(mine, ('x', 'y'), axis=0, tiled=True)  53.8 us
    all_to_all x1, starting transfers between devices, body(): lax.all_to_all(rows.reshape(256, 9, 2, 128), ('zh', 'x', 'y', 'zl'), 0, 0...  25.5 us
    all_to_all x1, blocking collectives, body(): found = jnp.min(lax.all_to_all(best, ('x', 'y'), 0, 0, tiled=True), axis=0)  12.9 us
    ppermute x2, starting transfers between devices, swap_cores(): return lax.ppermute(x, 'core', [(0, 1), (1, 0)])  10.2 us
    all_to_all x1, waiting for transfers between devices, body(): found = lax.all_to_all(found, ('zl', 'core'), 0, 0, tiled=True)  9.62 us
    ppermute x1, waiting for transfers between devices, body(): far = lax.ppermute(rounded, ('zh', 'zl'), [(z, 15 - z) for z in range(16)])  6.87 us
    pallas_call x1, Pallas kernels, build(): pl.pallas_call(build_kernel, out_shape=(jax.ShapeDtypeStruct((256 * 18, 1...  5.8 us
    pallas_call x3, Pallas kernels, nearest_codes(): pl.pallas_call(functools.partial(nearest_kernel, len(codes)), out_shape=j...  4.99 us
  transfers between devices with their start and end apart: 6, of which 4 were waited for; matrix products, arithmetic and copies ran while one was open for 1% of the time, Pallas kernels for 3%

profile of v6, /device:TPU:1, one launch (start us, length us, event | category | flops | bytes accessed | tf_op | source)
XLA Modules:
  0.0 161.2 jit_solution(4744662372462157846)
XLA Ops:
  7.2 0.0 all-gather.2.cloned.1.call-start
  7.2 5.8 %build.1 = (bf16[4608,128]{1,0:T(8,128)(2,1)}, bf16[512,256]{1,0:T(8,128)(2,1)}) custom-call(s32[1]{0:T(128)} %bitcast.core_ref, bf16[1024,256]{1,0:T(8,128)(2,1)} %latents_hbm.1, s32[1,1024]{1,0:T(1,128)} %order_hbm.1, s32[1,1024]{1,0:T(1,128)} %bitcast.15, s32[1,1024]{1,0:T(1,128)} %bitcast.16, bf16[1024,256]{1,0:T(8,128)(2,1)} %queries_hbm.1), custom_call_target="tpu_custom_call" | custom-call | flops 3221225472 | bytes 2097152 | tf_op jit(solution)/shard_map/build/pallas_call | solution.py:115
  13.0 0.0 all-gather.2.cloned.1.call-update
  13.0 0.0 copy-start.1
  13.1 0.0 copy-start.2
  13.1 25.5 %all-to-all-start = ((bf16[256,9,2,128]{3,2,1,0:T(2,128)(2,1)}), bf16[256,9,2,128]{3,2,1,0:T(2,128)(2,1)S(1)}, u32[]{:S(2)}, u32[]{:S(2)}) async-start(bf16[256,9,2,128]{3,2,1,0:T(2,128)(2,1)} %bitcast.12), calls=%async_computation | async-start | bytes 2359296 | tf_op jit(solution)/shard_map/all_to_all | solution.py:270
  38.6 53.8 %all-gather.2.cloned.1.call-done.refs_1_ = bf16[8192,256]{1,0:T(8,128)(2,1)} async-done(((bf16[512,256]{1,0:T(8,128)(2,1)}), bf16[8192,256]{1,0:T(8,128)(2,1)}) %all-gather.2.cloned.1.call-update) | async-done | bytes 4194320 | tf_op jit(solution)/shard_map/all_gather | solution.py:269
  92.3 0.7 slice.4.queries_ref
  93.0 0.0 all-to-all-done
  93.0 0.0 copy-start
  93.0 1.0 partial.3
  94.0 7.7 %collective-permute-start = (f32[264,256]{1,0:T(8,128)S(1)}, f32[264,256]{1,0:T(8,128)S(1)}, u32[]{:S(2)}, u32[]{:S(2)}) collective-permute-start(f32[264,256]{1,0:T(8,128)S(1)} %partial.3), channel_id=1, source_target_pairs={{0,1},{1,0},{2,3},{3,2},{4,5},{5,4},{6,7},{7,6},{8,9},{9,8},{10,11... | collective-permute-start | bytes 811016 | tf_op jit(solution)/shard_map/ppermute | solution.py:255
  101.7 1.0 partial.2.own_ref
  102.7 0.1 collective-permute-done.other_ref
  102.9 0.0 copy-done.1
  102.9 0.0 copy-done.2
  102.9 0.9 merge.1
  103.7 5.0 %collective-permute-start.1 = (bf16[256,256]{1,0:T(8,128)(2,1)S(1)}, bf16[256,256]{1,0:T(8,128)(2,1)S(1)}, u32[]{:S(2)}, u32[]{:S(2)}) collective-permute-start(bf16[256,256]{1,0:T(8,128)(2,1)S(1)} %get-tuple-element.17), channel_id=1, source_target_pairs={{0,270},{2,268},{4,266},{6,264},{8,262},{10,260},{12,258},{14,256}... | collective-permute-start | bytes 393224 | tf_op jit(solution)/shard_map/ppermute | solution.py:276
  108.7 2.3 %all_gather.7.refs_0_ = bf16[512,256]{1,0:T(8,128)(2,1)S(1)} all-gather(bf16[256,256]{1,0:T(8,128)(2,1)S(1)} %get-tuple-element.17), channel_id=1, replica_groups=mesh['zh'=2,'x'=4,'y'=4,'zl'=8,'core'=2] {'core'}, dimensions={0}, use_global_device_ids=true | all-gather | bytes 393216 | tf_op jit(solution)/shard_map/all_gather | solution.py:277
  111.0 0.0 copy-done
  111.0 2.4 %nearest.3.refs_2_ = f32[16,8,512]{2,1,0:T(8,128)S(1)} custom-call(bf16[512,256]{1,0:T(8,128)(2,1)S(1)} %all_gather.7.refs_0_, bf16[8192,256]{1,0:T(8,128)(2,1)S(1)} %copy-done), custom_call_target="tpu_custom_call" | custom-call | flops 1073741824 | bytes 5242880 | tf_op jit(solution)/shard_map/nearest/pallas_call | solution.py:243
  113.4 6.9 %collective-permute-done.1.refs_0_ = bf16[256,256]{1,0:T(8,128)(2,1)S(1)} collective-permute-done((bf16[256,256]{1,0:T(8,128)(2,1)S(1)}, bf16[256,256]{1,0:T(8,128)(2,1)S(1)}, u32[]{:S(2)}, u32[]{:S(2)}) %collective-permute-start.1) | collective-permute-done | bytes 131104 | tf_op jit(solution)/shard_map/ppermute | solution.py:276
  120.3 2.6 %collective-permute-start.2 = (bf16[256,256]{1,0:T(8,128)(2,1)S(1)}, bf16[256,256]{1,0:T(8,128)(2,1)S(1)}, u32[]{:S(2)}, u32[]{:S(2)}) collective-permute-start(bf16[256,256]{1,0:T(8,128)(2,1)S(1)} %collective-permute-done.1.refs_0_), channel_id=1, source_target_pairs={{0,1},{1,0},{2,3},{3,2},{4,5},{5,4},{6,7},{7,6},{8,9},{9,8},{10,11... | collective-permute-start | bytes 393224 | tf_op jit(solution)/shard_map/ppermute | solution.py:255
  122.8 1.3 nearest.4.refs_2_
  124.1 0.0 copy-start.3
  124.1 0.0 collective-permute-done.2.refs_0_
  124.2 1.3 nearest.5
  125.5 12.9 %all_to_all.15 = f32[16,4,128]{2,1,0:T(4,128)S(1)} all-to-all(f32[16,4,128]{2,1,0:T(4,128)S(1)} %nearest.5), channel_id=1, replica_groups=mesh['zh'=2,'x'=4,'y'=4,'zl'=8,'core'=2] {'x','y'}, dimensions={0} | all-to-all | bytes 65536 | tf_op jit(solution)/shard_map/all_to_all | solution.py:283
  138.4 0.6 broadcast_in_dim.2
  139.0 4.9 %all-to-all-start.2 = ((f32[16,4,128]{2,1,0:T(4,128)}), f32[16,4,128]{2,1,0:T(4,128)S(1)}, u32[]{:S(2)}, u32[]{:S(2)}) async-start(f32[16,4,128]{2,1,0:T(4,128)} %broadcast_in_dim.2), calls=%async_computation.2 | async-start | bytes 65536 | tf_op jit(solution)/shard_map/all_to_all | solution.py:285
  143.9 0.0 copy-done.3
  143.9 0.2 multiply_reduce_fusion
  144.1 9.6 %all-to-all-done.2 = f32[16,4,128]{2,1,0:T(4,128)S(1)} async-done(((f32[16,4,128]{2,1,0:T(4,128)}), f32[16,4,128]{2,1,0:T(4,128)S(1)}, u32[]{:S(2)}, u32[]{:S(2)}) %all-to-all-start.2) | async-done | bytes 32800 | tf_op jit(solution)/shard_map/all_to_all | solution.py:285
  153.7 0.6 add_multiply_fusion
  (2 shorter events, 0.0 us)
Async XLA Ops:
  7.2 85.2 %all-gather.2.cloned.1.call-start = ((), (), s32[]{:S(2)}) async-start(), calls=%async_computation.3 | async-start | bytes 4456448 | tf_op jit(solution)/shard_map/all_gather | solution.py:269
  13.0 89.8 %copy-start.1 = (f32[256,256]{1,0:T(8,128)S(1)}, f32[256,256]{1,0:T(8,128)}, u32[]{:S(2)}) copy-start(f32[256,256]{1,0:T(8,128)} %sums_ref.1) | copy-start | bytes 786436
  13.1 89.8 %copy-start.2 = (f32[256]{0:T(256)S(1)}, f32[256]{0:T(256)}, u32[]{:S(2)}) copy-start(f32[256]{0:T(256)} %param.11) | copy-start | bytes 3076
  13.1 80.0 %all-to-all-start = ((bf16[256,9,2,128]{3,2,1,0:T(2,128)(2,1)}), bf16[256,9,2,128]{3,2,1,0:T(2,128)(2,1)S(1)}, u32[]{:S(2)}, u32[]{:S(2)}) async-start(bf16[256,9,2,128]{3,2,1,0:T(2,128)(2,1)} %bitcast.12), calls=%async_computation | async-start | bytes 2359296 | tf_op jit(solution)/shard_map/all_to_all | solution.py:270
  93.0 18.0 %copy-start = (bf16[8192,256]{1,0:T(8,128)(2,1)S(1)}, bf16[8192,256]{1,0:T(8,128)(2,1)}, u32[]{:S(2)}) copy-start(bf16[8192,256]{1,0:T(8,128)(2,1)} %all-gather.2.cloned.1.call-done.refs_1_) | copy-start | bytes 12582916
  94.0 8.8 %collective-permute-start = (f32[264,256]{1,0:T(8,128)S(1)}, f32[264,256]{1,0:T(8,128)S(1)}, u32[]{:S(2)}, u32[]{:S(2)}) collective-permute-start(f32[264,256]{1,0:T(8,128)S(1)} %partial.3), channel_id=1, source_target_pairs={{0,1},{1,0},{2,3},{3,2},{4,5},{5,4},{6,7},{7,6},{8,9},{9,8},{10,11... | collective-permute-start | bytes 811016 | tf_op jit(solution)/shard_map/ppermute | solution.py:255
  103.7 16.6 %collective-permute-start.1 = (bf16[256,256]{1,0:T(8,128)(2,1)S(1)}, bf16[256,256]{1,0:T(8,128)(2,1)S(1)}, u32[]{:S(2)}, u32[]{:S(2)}) collective-permute-start(bf16[256,256]{1,0:T(8,128)(2,1)S(1)} %get-tuple-element.17), channel_id=1, source_target_pairs={{0,270},{2,268},{4,266},{6,264},{8,262},{10,260},{12,258},{14,256}... | collective-permute-start | bytes 393224 | tf_op jit(solution)/shard_map/ppermute | solution.py:276
  120.3 3.9 %collective-permute-start.2 = (bf16[256,256]{1,0:T(8,128)(2,1)S(1)}, bf16[256,256]{1,0:T(8,128)(2,1)S(1)}, u32[]{:S(2)}, u32[]{:S(2)}) collective-permute-start(bf16[256,256]{1,0:T(8,128)(2,1)S(1)} %collective-permute-done.1.refs_0_), channel_id=1, source_target_pairs={{0,1},{1,0},{2,3},{3,2},{4,5},{5,4},{6,7},{7,6},{8,9},{9,8},{10,11... | collective-permute-start | bytes 393224 | tf_op jit(solution)/shard_map/ppermute | solution.py:255
  124.1 19.7 %copy-start.3 = (bf16[1024,256]{1,0:T(8,128)(2,1)S(1)}, bf16[1024,256]{1,0:T(8,128)(2,1)}, u32[]{:S(2)}) copy-start(bf16[1024,256]{1,0:T(8,128)(2,1)} %queries_hbm.1) | copy-start | bytes 1572868
  139.0 14.7 %all-to-all-start.2 = ((f32[16,4,128]{2,1,0:T(4,128)}), f32[16,4,128]{2,1,0:T(4,128)S(1)}, u32[]{:S(2)}, u32[]{:S(2)}) async-start(f32[16,4,128]{2,1,0:T(4,128)} %broadcast_in_dim.2), calls=%async_computation.2 | async-start | bytes 65536 | tf_op jit(solution)/shard_map/all_to_all | solution.py:285
Sparse Core Ops, SparseCore 0:
  13.2 79.1 all-gather.1

commit v7 on v6

--- a/solution.py
+++ b/solution.py
@@ -14,8 +14,8 @@
 SLOTS = STEPS * CAP
 ema_decay = 0.9
 
-AXES = ("zh", "x", "y", "zl", "core")
-SIZES = (2, 4, 4, 8, 2)
+AXES = ("zh", "xa", "xb", "y", "zl", "core")
+SIZES = (2, 2, 2, 4, 8, 2)
 NT = (((1,), (1,)), ((), ()))
 
 f32 = jnp.float32
@@ -213,22 +213,42 @@
     )(own, other, counts.reshape(1, CPD), sums)
 
 
-def nearest_kernel(codes, *refs):
-    groups, width = 16, 512
-    codes_refs, queries_ref, rest = refs[:codes], refs[codes], refs[codes + 1 :]
-    out_ref = rest[-1]
+PIECES = (176, 176, 160)
+
+
+def stage_kernel(*refs):
+    out_ref = refs[-1]
+    at = 0
+    for ref, rows in zip(refs[:-1], PIECES):
+        for g in range(8):
+            out_ref[g * 512 + at : g * 512 + at + rows] = ref[g * rows : (g + 1) * rows]
+        at += rows
+
+
+def stage(pieces):
+    return pl.pallas_call(
+        stage_kernel,
+        out_shape=jax.ShapeDtypeStruct((8 * 512, E), bf16),
+        compiler_params=pltpu.CompilerParams(vmem_limit_bytes=32 << 20),
+        name="stage",
+    )(*pieces)
+
+
+def nearest_kernel(codes_ref, queries_ref, *refs):
+    groups, width = 8, 512
+    out_ref = refs[-1]
     last = out_ref.shape == (groups, 4, 128)
     scaled, norms = [], []
-    for codes_ref in codes_refs:
-        part = codes_ref[...].astype(f32)
+    for c in range(codes_ref.shape[0] // CPD):
+        part = codes_ref[c * CPD : (c + 1) * CPD].astype(f32)
         norms.append(jnp.sum(part * part, axis=1, keepdims=True))
         scaled.append((-2.0 * part).astype(bf16))
     for g in range(groups):
         part = queries_ref[g * width : (g + 1) * width]
-        best = rest[0][g] if len(rest) > 1 else None
+        best = refs[0][g] if len(refs) > 1 else None
         for m, n in zip(scaled, norms):
             value = lax.dot_general(m, part, NT, preferred_element_type=f32) + n
-            value = jnp.min(value.reshape(-1, 8, width), axis=0)
+            value = jnp.min(value.reshape(CPD // 8, 8, width), axis=0)
             best = value if best is None else jnp.minimum(best, value)
         if last:
             line = jnp.min(best, axis=0, keepdims=True)
@@ -237,16 +257,14 @@
             out_ref[g] = best
 
 
-def nearest_codes(codes, queries, best=None, last=False):
-    shape = (16, 4, 128) if last else (16, 8, 512)
-    operands = (*codes, queries) if best is None else (*codes, queries, best)
-    return pl.pallas_call(
-        functools.partial(nearest_kernel, len(codes)),
+def nearest_codes(codes, queries, best=None):
+    shape = (8, 8, 512) if best is None else (8, 4, 128)
+    operands = (codes, queries) if best is None else (codes, queries, best)
+    return pl.pallas_call(
+        nearest_kernel,
         out_shape=jax.ShapeDtypeStruct(shape, f32),
         compiler_params=pltpu.CompilerParams(vmem_limit_bytes=32 << 20),
-        cost_estimate=pl.CostEstimate(
-            flops=len(codes) << 30, bytes_accessed=5 << 20, transcendentals=0
-        ),
+        cost_estimate=pl.CostEstimate(flops=2 << 30, bytes_accessed=4 << 20, transcendentals=0),
         name="nearest",
     )(*operands)
 
@@ -266,21 +284,23 @@
         code_offset.reshape(1, -1),
         queries,
     )
-    plane_queries = lax.all_gather(mine, ("x", "y"), axis=0, tiled=True)
-    got = lax.all_to_all(rows.reshape(256, 9, 2, 128), ("zh", "x", "y", "zl"), 0, 0, tiled=True)
+    pieces, at = [], 0
+    for count in PIECES:
+        pieces.append(lax.all_gather(mine[at : at + count], ("xa", "y"), axis=0, tiled=True))
+        at += count
+    plane_queries = stage(pieces)
+    got = lax.all_to_all(rows.reshape(256, 9, 2, 128), ("zh", "xa", "xb", "y", "zl"), 0, 0, tiled=True)
     got = got.reshape(256 * 18, 128)
     arrived = plane_queries[:16]
     other_part = swap_cores(partial_update(1, got, arrived))
     own_part = partial_update(0, got, arrived)
     codebook, counts, sums, rounded = merge(own_part, other_part, ema_counts, ema_sums)
     far = lax.ppermute(rounded, ("zh", "zl"), [(z, 15 - z) for z in range(16)])
-    near = lax.all_gather(rounded, "core", axis=0, tiled=True)
-    best = nearest_codes((near,), plane_queries)
-    far, best = lax.optimization_barrier((far, best))
-    far_other = swap_cores(far)
-    best = nearest_codes((far,), plane_queries, best)
-    best = nearest_codes((far_other,), plane_queries, best, last=True)
-    found = jnp.min(lax.all_to_all(best, ("x", "y"), 0, 0, tiled=True), axis=0)
+    near = lax.all_gather(rounded, ("xb", "core"), axis=0, tiled=True)
+    best = nearest_codes(near, plane_queries)
+    far = lax.all_gather(far, ("xb", "core"), axis=0, tiled=True)
+    best = nearest_codes(far, plane_queries, best)
+    found = jnp.min(lax.all_to_all(best, ("xa", "y"), 0, 0, tiled=True), axis=0)
     found = jnp.broadcast_to(found[None], (16, 4, 128))
     found = lax.all_to_all(found, ("zl", "core"), 0, 0, tiled=True)
     found = jnp.min(found.reshape(8, 2, 4, 128), axis=0).reshape(-1)
@@ -297,12 +317,12 @@
         P(AXES),
         P(AXES),
         P(AXES, None),
-        P(("zh", "x", "y"), None),
+        P(("zh", "xa", "xb", "y"), None),
     )
     return jax.shard_map(
         body,
         mesh=fine,
         in_specs=placed,
-        out_specs=(P(AXES, None), P(AXES), P(AXES, None), P(("zh", "x", "y"))),
+        out_specs=(P(AXES, None), P(AXES), P(AXES, None), P(("zh", "xa", "xb", "y"))),
         check_vma=False,
     )

time: 162 us -> 207 us (1.28)
  blocking collectives: 15.2 us -> 120 us
  waiting for transfers between devices: 70.4 us -> 11.9 us
  starting transfers between devices: 45.6 us -> 59.1 us
  between operations: 14.2 us -> 0.79 us
    all_gather x1 -> x5, blocking collectives: 2.29 us -> 107 us  [the longest x3 92.5 us: body(): lax.all_gather(mine[at:at + count], ('xa', 'y'), axis=0, tiled=True)]
    all_gather x1 -> x0, waiting for transfers between devices: 53.8 us -> none  [body(): plane_queries = lax.all_gather(mine, ('x', 'y'), axis=0, tiled=True)]
    ppermute x2 -> x1, starting transfers between devices: 10.2 us -> 17.8 us  [swap_cores(): return lax.ppermute(x, 'core', [(0, 1), (1, 0)])]
    all_to_all x1, starting transfers between devices: 4.89 us -> 10.9 us  [body(): found = lax.all_to_all(found, ('zl', 'core'), 0, 0, tiled=True)]
    ppermute x1, waiting for transfers between devices: 6.87 us -> 2.09 us  [body(): far = lax.ppermute(rounded, ('zh', 'zl'), [(z, 15 - z) for z in range(16)])]
  transfers between devices with their start and end apart: 6 -> 4, of which waited for: 4 -> 3; matrix products, arithmetic and copies ran while one was open for 1% -> 0% of each run, Pallas kernels for 3% -> 2%
where the time goes in v7:
time: 207 us; the launch traced here: 206 us
  blocking collectives  120 us (58%)
  starting transfers between devices  59.1 us (29%)
  Pallas kernels  13.6 us (7%)
  waiting for transfers between devices  11.9 us (6%)
    all_gather x3, blocking collectives, body(): lax.all_gather(mine[at:at + count], ('xa', 'y'), axis=0, tiled=True)  92.5 us
    all_to_all x1, starting transfers between devices, body(): lax.all_to_all(rows.reshape(256, 9, 2, 128), ('zh', 'xa', 'xb', 'y', 'zl'...  25.5 us
    ppermute x1, starting transfers between devices, swap_cores(): return lax.ppermute(x, 'core', [(0, 1), (1, 0)])  17.8 us
    all_to_all x1, blocking collectives, body(): found = jnp.min(lax.all_to_all(best, ('xa', 'y'), 0, 0, tiled=True), axis=0)  12.4 us
    all_to_all x1, starting transfers between devices, body(): found = lax.all_to_all(found, ('zl', 'core'), 0, 0, tiled=True)  10.9 us
    all_to_all x1, waiting for transfers between devices, body(): found = lax.all_to_all(found, ('zl', 'core'), 0, 0, tiled=True)  9.62 us
    all_gather x1, blocking collectives, body(): near = lax.all_gather(rounded, ('xb', 'core'), axis=0, tiled=True)  7.47 us
    all_gather x1, blocking collectives, body(): far = lax.all_gather(far, ('xb', 'core'), axis=0, tiled=True)  7.28 us
  transfers between devices with their start and end apart: 4, of which 3 were waited for; matrix products, arithmetic and copies ran while one was open for 0% of the time, Pallas kernels for 2%

profile of v7, /device:TPU:1, one launch (start us, length us, event | category | flops | bytes accessed | tf_op | source)
XLA Modules:
  0.0 206.5 jit_solution(5375047552083098818)
XLA Ops:
  0.6 5.8 %build.1 = (bf16[4608,128]{1,0:T(8,128)(2,1)}, bf16[512,256]{1,0:T(8,128)(2,1)}) custom-call(s32[1]{0:T(128)} %bitcast.core_ref, bf16[1024,256]{1,0:T(8,128)(2,1)} %latents_hbm.1, s32[1,1024]{1,0:T(1,128)} %order_hbm.1, s32[1,1024]{1,0:T(1,128)} %bitcast.15, s32[1,1024]{1,0:T(1,128)} %bitcast.16, bf16[1024,256]{1,0:T(8,128)(2,1)} %queries_hbm.1), custom_call_target="tpu_custom_call" | custom-call | flops 3221225472 | bytes 2097152 | tf_op jit(solution)/shard_map/build/pallas_call | solution.py:115
  6.5 0.0 copy-start.3
  6.5 25.5 %all-to-all-start = ((bf16[256,9,2,128]{3,2,1,0:T(2,128)(2,1)}), bf16[256,9,2,128]{3,2,1,0:T(2,128)(2,1)S(1)}, u32[]{:S(2)}, u32[]{:S(2)}) async-start(bf16[256,9,2,128]{3,2,1,0:T(2,128)(2,1)} %bitcast.12), calls=%async_computation | async-start | bytes 2359296 | tf_op jit(solution)/shard_map/all_to_all | solution.py:292
  31.9 0.0 copy-done.3
  32.0 31.3 %all_gather.17.refs_2_ = bf16[1280,256]{1,0:T(8,128)(2,1)S(1)} all-gather(bf16[160,256]{1,0:T(8,128)(2,1)S(1)} %slice.14), channel_id=1, replica_groups=mesh['zh'=2,'xa'=2,'xb'=2,'y'=4,'zl'=8,'core'=2] {'xa','y'}, dimensions={0}, use_global_device_ids=true | all-gather | bytes 737280 | tf_op jit(solution)/shard_map/all_gather | solution.py:289
  63.3 31.7 %all_gather.15.refs_0_ = bf16[1408,256]{1,0:T(8,128)(2,1)S(1)} all-gather(bf16[176,256]{1,0:T(8,128)(2,1)S(1)} %get-tuple-element.17), channel_id=1, replica_groups=mesh['zh'=2,'xa'=2,'xb'=2,'y'=4,'zl'=8,'core'=2] {'xa','y'}, dimensions={0}, use_global_device_ids=true | all-gather | bytes 811008 | tf_op jit(solution)/shard_map/all_gather | solution.py:289
  95.1 29.4 %all_gather.16.refs_1_ = bf16[1408,256]{1,0:T(8,128)(2,1)S(1)} all-gather(bf16[176,256]{1,0:T(8,128)(2,1)S(1)} %get-tuple-element.16), channel_id=1, replica_groups=mesh['zh'=2,'xa'=2,'xb'=2,'y'=4,'zl'=8,'core'=2] {'xa','y'}, dimensions={0}, use_global_device_ids=true | all-gather | bytes 811008 | tf_op jit(solution)/shard_map/all_gather | solution.py:289
  124.5 0.1 stage.1.queries_ref
  124.7 0.0 all-to-all-done
  124.7 1.0 partial.3
  125.7 0.0 copy-start
  125.7 0.0 copy-start.1
  125.7 17.8 %collective-permute-start = (f32[264,256]{1,0:T(8,128)S(1)}, f32[264,256]{1,0:T(8,128)S(1)}, u32[]{:S(2)}, u32[]{:S(2)}) collective-permute-start(f32[264,256]{1,0:T(8,128)S(1)} %partial.3), channel_id=1, source_target_pairs={{0,1},{1,0},{2,3},{3,2},{4,5},{5,4},{6,7},{7,6},{8,9},{9,8},{10,11... | collective-permute-start | bytes 811016 | tf_op jit(solution)/shard_map/ppermute | solution.py:273
  143.5 1.0 partial.2.own_ref
  144.5 0.2 collective-permute-done.other_ref
  144.6 0.0 copy-done
  144.6 0.0 copy-done.1
  144.7 0.9 merge.1
  145.5 4.9 %collective-permute-start.1 = (bf16[256,256]{1,0:T(8,128)(2,1)S(1)}, bf16[256,256]{1,0:T(8,128)(2,1)S(1)}, u32[]{:S(2)}, u32[]{:S(2)}) collective-permute-start(bf16[256,256]{1,0:T(8,128)(2,1)S(1)} %get-tuple-element.15), channel_id=1, source_target_pairs={{0,270},{2,268},{4,266},{6,264},{8,262},{10,260},{12,258},{14,256}... | collective-permute-start | bytes 393224 | tf_op jit(solution)/shard_map/ppermute | solution.py:298
  150.4 7.5 %all_gather.19.codes_ref = bf16[1024,256]{1,0:T(8,128)(2,1)S(1)} all-gather(bf16[256,256]{1,0:T(8,128)(2,1)S(1)} %get-tuple-element.15), channel_id=1, replica_groups=mesh['zh'=2,'xa'=2,'xb'=2,'y'=4,'zl'=8,'core'=2] {'xb','core'}, dimensions={0}, use_global_device_ids=true | all-gather | bytes 655360 | tf_op jit(solution)/shard_map/all_gather | solution.py:299
  157.9 2.4 %nearest.2.refs_0_ = f32[8,8,512]{2,1,0:T(8,128)S(1)} custom-call(bf16[1024,256]{1,0:T(8,128)(2,1)S(1)} %all_gather.19.codes_ref, bf16[4096,256]{1,0:T(8,128)(2,1)S(1)} %stage.1.queries_ref), custom_call_target="tpu_custom_call" | custom-call | flops 2147483648 | bytes 4194304 | tf_op jit(solution)/shard_map/nearest/pallas_call | solution.py:263
  160.3 2.1 %collective-permute-done.1 = bf16[256,256]{1,0:T(8,128)(2,1)S(1)} collective-permute-done((bf16[256,256]{1,0:T(8,128)(2,1)S(1)}, bf16[256,256]{1,0:T(8,128)(2,1)S(1)}, u32[]{:S(2)}, u32[]{:S(2)}) %collective-permute-start.1) | collective-permute-done | bytes 131104 | tf_op jit(solution)/shard_map/ppermute | solution.py:298
  162.4 7.3 %all_gather.18.codes_ref = bf16[1024,256]{1,0:T(8,128)(2,1)S(1)} all-gather(bf16[256,256]{1,0:T(8,128)(2,1)S(1)} %collective-permute-done.1), channel_id=1, replica_groups=mesh['zh'=2,'xa'=2,'xb'=2,'y'=4,'zl'=8,'core'=2] {'xb','core'}, dimensions={0}, use_global_device_ids=true | all-gather | bytes 655360 | tf_op jit(solution)/shard_map/all_gather | solution.py:301
  169.7 0.0 copy-start.2
  169.7 2.4 %nearest.3 = f32[8,4,128]{2,1,0:T(4,128)S(1)} custom-call(bf16[1024,256]{1,0:T(8,128)(2,1)S(1)} %all_gather.18.codes_ref, bf16[4096,256]{1,0:T(8,128)(2,1)S(1)} %stage.1.queries_ref, f32[8,8,512]{2,1,0:T(8,128)S(1)} %nearest.2.refs_0_), custom_call_target="tpu_custom_call" | custom-call | flops 2147483648 | bytes 4194304 | tf_op jit(solution)/shard_map/nearest/pallas_call | solution.py:263
  172.1 12.4 %all_to_all.15 = f32[8,4,128]{2,1,0:T(4,128)S(1)} all-to-all(f32[8,4,128]{2,1,0:T(4,128)S(1)} %nearest.3), channel_id=1, replica_groups=mesh['zh'=2,'xa'=2,'xb'=2,'y'=4,'zl'=8,'core'=2] {'xa','y'}, dimensions={0} | all-to-all | bytes 32768 | tf_op jit(solution)/shard_map/all_to_all | solution.py:303
  184.5 0.6 broadcast_in_dim.2
  185.1 10.9 %all-to-all-start.2 = ((f32[16,4,128]{2,1,0:T(4,128)}), f32[16,4,128]{2,1,0:T(4,128)S(1)}, u32[]{:S(2)}, u32[]{:S(2)}) async-start(f32[16,4,128]{2,1,0:T(4,128)} %broadcast_in_dim.2), calls=%async_computation.2 | async-start | bytes 65536 | tf_op jit(solution)/shard_map/all_to_all | solution.py:305
  196.0 0.0 copy-done.2
  196.0 0.2 multiply_reduce_fusion
  196.3 9.6 %all-to-all-done.2 = f32[16,4,128]{2,1,0:T(4,128)S(1)} async-done(((f32[16,4,128]{2,1,0:T(4,128)}), f32[16,4,128]{2,1,0:T(4,128)S(1)}, u32[]{:S(2)}, u32[]{:S(2)}) %all-to-all-start.2) | async-done | bytes 32800 | tf_op jit(solution)/shard_map/all_to_all | solution.py:305
  205.9 0.6 add_multiply_fusion
  (5 shorter events, 0.1 us)
Async XLA Ops:
  6.5 25.5 %copy-start.3 = (bf16[512,256]{1,0:T(8,128)(2,1)S(1)}, bf16[512,256]{1,0:T(8,128)(2,1)}, u32[]{:S(2)}) copy-start(bf16[512,256]{1,0:T(8,128)(2,1)} %get-tuple-element.11) | copy-start | bytes 786436
  6.5 118.2 %all-to-all-start = ((bf16[256,9,2,128]{3,2,1,0:T(2,128)(2,1)}), bf16[256,9,2,128]{3,2,1,0:T(2,128)(2,1)S(1)}, u32[]{:S(2)}, u32[]{:S(2)}) async-start(bf16[256,9,2,128]{3,2,1,0:T(2,128)(2,1)} %bitcast.12), calls=%async_computation | async-start | bytes 2359296 | tf_op jit(solution)/shard_map/all_to_all | solution.py:292
  125.7 19.0 %copy-start = (f32[256,256]{1,0:T(8,128)S(1)}, f32[256,256]{1,0:T(8,128)}, u32[]{:S(2)}) copy-start(f32[256,256]{1,0:T(8,128)} %sums_ref.1) | copy-start | bytes 786436
  125.7 19.0 %copy-start.1 = (f32[256]{0:T(256)S(1)}, f32[256]{0:T(256)}, u32[]{:S(2)}) copy-start(f32[256]{0:T(256)} %param.11) | copy-start | bytes 3076
  125.7 19.0 %collective-permute-start = (f32[264,256]{1,0:T(8,128)S(1)}, f32[264,256]{1,0:T(8,128)S(1)}, u32[]{:S(2)}, u32[]{:S(2)}) collective-permute-start(f32[264,256]{1,0:T(8,128)S(1)} %partial.3), channel_id=1, source_target_pairs={{0,1},{1,0},{2,3},{3,2},{4,5},{5,4},{6,7},{7,6},{8,9},{9,8},{10,11... | collective-permute-start | bytes 811016 | tf_op jit(solution)/shard_map/ppermute | solution.py:273
  145.5 16.9 %collective-permute-start.1 = (bf16[256,256]{1,0:T(8,128)(2,1)S(1)}, bf16[256,256]{1,0:T(8,128)(2,1)S(1)}, u32[]{:S(2)}, u32[]{:S(2)}) collective-permute-start(bf16[256,256]{1,0:T(8,128)(2,1)S(1)} %get-tuple-element.15), channel_id=1, source_target_pairs={{0,270},{2,268},{4,266},{6,264},{8,262},{10,260},{12,258},{14,256}... | collective-permute-start | bytes 393224 | tf_op jit(solution)/shard_map/ppermute | solution.py:298
  169.7 26.4 %copy-start.2 = (bf16[1024,256]{1,0:T(8,128)(2,1)S(1)}, bf16[1024,256]{1,0:T(8,128)(2,1)}, u32[]{:S(2)}) copy-start(bf16[1024,256]{1,0:T(8,128)(2,1)} %queries_hbm.1) | copy-start | bytes 1572868
  185.1 20.8 %all-to-all-start.2 = ((f32[16,4,128]{2,1,0:T(4,128)}), f32[16,4,128]{2,1,0:T(4,128)S(1)}, u32[]{:S(2)}, u32[]{:S(2)}) async-start(f32[16,4,128]{2,1,0:T(4,128)} %broadcast_in_dim.2), calls=%async_computation.2 | async-start | bytes 65536 | tf_op jit(solution)/shard_map/all_to_all | solution.py:305

commit v8 on v6

--- a/solution.py
+++ b/solution.py
@@ -213,40 +213,42 @@
     )(own, other, counts.reshape(1, CPD), sums)
 
 
-def nearest_kernel(codes, *refs):
-    groups, width = 16, 512
-    codes_refs, queries_ref, rest = refs[:codes], refs[codes], refs[codes + 1 :]
-    out_ref = rest[-1]
-    last = out_ref.shape == (groups, 4, 128)
+def nearest_kernel(codes_ref, low_ref, high_ref, *refs):
+    out_ref = refs[-1]
+    last = out_ref.shape == (32, 4, 128)
     scaled, norms = [], []
-    for codes_ref in codes_refs:
-        part = codes_ref[...].astype(f32)
+    for c in range(codes_ref.shape[0] // CPD):
+        part = codes_ref[c * CPD : (c + 1) * CPD].astype(f32)
         norms.append(jnp.sum(part * part, axis=1, keepdims=True))
         scaled.append((-2.0 * part).astype(bf16))
-    for g in range(groups):
-        part = queries_ref[g * width : (g + 1) * width]
-        best = rest[0][g] if len(rest) > 1 else None
-        for m, n in zip(scaled, norms):
-            value = lax.dot_general(m, part, NT, preferred_element_type=f32) + n
-            value = jnp.min(value.reshape(-1, 8, width), axis=0)
-            best = value if best is None else jnp.minimum(best, value)
+    for y in range(4):
+        lines = []
+        for h, queries_ref in enumerate((low_ref, high_ref)):
+            part = queries_ref[y * 256 : (y + 1) * 256]
+            best = refs[0][2 * y + h] if len(refs) > 1 else None
+            for m, n in zip(scaled, norms):
+                value = lax.dot_general(m, part, NT, preferred_element_type=f32) + n
+                value = jnp.min(value.reshape(CPD // 8, 8, 256), axis=0)
+                best = value if best is None else jnp.minimum(best, value)
+            if last:
+                line = jnp.min(best, axis=0, keepdims=True)
+                lines += [line[:, :128], line[:, 128:]]
+            else:
+                out_ref[2 * y + h] = best
         if last:
-            line = jnp.min(best, axis=0, keepdims=True)
-            out_ref[g] = jnp.concatenate([line[:, j * 128 : (j + 1) * 128] for j in range(4)], axis=0)
-        else:
-            out_ref[g] = best
+            lines = jnp.concatenate(lines, axis=0)
+            for z in range(8):
+                out_ref[y * 8 + z] = lines
 
 
 def nearest_codes(codes, queries, best=None, last=False):
-    shape = (16, 4, 128) if last else (16, 8, 512)
-    operands = (*codes, queries) if best is None else (*codes, queries, best)
+    shape = (32, 4, 128) if last else (8, 8, 256)
+    operands = (codes, *queries) if best is None else (codes, *queries, best)
     return pl.pallas_call(
-        functools.partial(nearest_kernel, len(codes)),
+        nearest_kernel,
         out_shape=jax.ShapeDtypeStruct(shape, f32),
         compiler_params=pltpu.CompilerParams(vmem_limit_bytes=32 << 20),
-        cost_estimate=pl.CostEstimate(
-            flops=len(codes) << 30, bytes_accessed=5 << 20, transcendentals=0
-        ),
+        cost_estimate=pl.CostEstimate(flops=1 << 30, bytes_accessed=2 << 20, transcendentals=0),
         name="nearest",
     )(*operands)
 
@@ -266,24 +268,26 @@
         code_offset.reshape(1, -1),
         queries,
     )
-    plane_queries = lax.all_gather(mine, ("x", "y"), axis=0, tiled=True)
+    row_queries = [
+        lax.all_gather(part, "y", axis=0, tiled=True) for part in (mine[:256], mine[256:])
+    ]
     got = lax.all_to_all(rows.reshape(256, 9, 2, 128), ("zh", "x", "y", "zl"), 0, 0, tiled=True)
     got = got.reshape(256 * 18, 128)
-    arrived = plane_queries[:16]
+    arrived = row_queries[0][:16] + row_queries[1][:16]
     other_part = swap_cores(partial_update(1, got, arrived))
     own_part = partial_update(0, got, arrived)
     codebook, counts, sums, rounded = merge(own_part, other_part, ema_counts, ema_sums)
     far = lax.ppermute(rounded, ("zh", "zl"), [(z, 15 - z) for z in range(16)])
-    near = lax.all_gather(rounded, "core", axis=0, tiled=True)
-    best = nearest_codes((near,), plane_queries)
-    far, best = lax.optimization_barrier((far, best))
+    near = lax.all_gather(rounded, "x", axis=0, tiled=True)
+    near_other = swap_cores(near)
+    best = nearest_codes(near, row_queries)
+    best = nearest_codes(near_other, row_queries, best)
+    far = lax.all_gather(far, "x", axis=0, tiled=True)
     far_other = swap_cores(far)
-    best = nearest_codes((far,), plane_queries, best)
-    best = nearest_codes((far_other,), plane_queries, best, last=True)
-    found = jnp.min(lax.all_to_all(best, ("x", "y"), 0, 0, tiled=True), axis=0)
-    found = jnp.broadcast_to(found[None], (16, 4, 128))
-    found = lax.all_to_all(found, ("zl", "core"), 0, 0, tiled=True)
-    found = jnp.min(found.reshape(8, 2, 4, 128), axis=0).reshape(-1)
+    best = nearest_codes(far, row_queries, best)
+    best = nearest_codes(far_other, row_queries, best, last=True)
+    found = jnp.min(lax.all_to_all(best, ("y", "zl"), 0, 0, tiled=True), axis=0)
+    found = lax.all_gather(found, "core", axis=0, tiled=True).reshape(-1)
     nearest = (own + found) / E
     return (codebook, counts.reshape(-1), sums, nearest)
 

time: 162 us -> 161 us (level)
  blocking collectives: 15.2 us -> 46 us
  waiting for transfers between devices: 70.4 us -> 42.8 us
  between operations: 14.2 us -> 0.82 us
  starting transfers between devices: 45.6 us -> 55.6 us
    all_gather x1 -> x0, waiting for transfers between devices: 53.8 us -> none  [body(): plane_queries = lax.all_gather(mine, ('x', 'y'), axis=0, tiled=True)]
    all_gather x1 -> x5, blocking collectives: 2.29 us -> 46 us  [the longest x2 22.8 us: body(): lax.all_gather(part, 'y', axis=0, tiled=True)]
    all_to_all x1, waiting for transfers between devices: 0.01 us -> 31.3 us  [body(): lax.all_to_all(rows.reshape(256, 9, 2, 128), ('zh', 'x', 'y', 'zl'), 0, 0...]
    all_to_all x1 -> x0, blocking collectives: 12.9 us -> none  [body(): found = jnp.min(lax.all_to_all(best, ('x', 'y'), 0, 0, tiled=True), axis=0)]
    ppermute x2 -> x3, starting transfers between devices: 10.2 us -> 19.2 us  [swap_cores(): return lax.ppermute(x, 'core', [(0, 1), (1, 0)])]
    ppermute x1, waiting for transfers between devices: 6.87 us -> 0.01 us  [body(): far = lax.ppermute(rounded, ('zh', 'zl'), [(z, 15 - z) for z in range(16)])]
    all_to_all x1, waiting for transfers between devices: 9.62 us -> 11.4 us  [body(): found = jnp.min(lax.all_to_all(best, ('y', 'zl'), 0, 0, tiled=True), axis=0)]
    pallas_call x3 -> x4, Pallas kernels: 4.99 us -> 5.9 us  [nearest_codes(): pl.pallas_call(nearest_kernel, out_shape=jax.ShapeDtypeStruct(shape, f32)...]
  transfers between devices with their start and end apart: 6 -> 6, of which waited for: 4 -> 3; matrix products, arithmetic and copies ran while one was open for 1% -> 0% of each run, Pallas kernels for 3% -> 3%
where the time goes in v8:
time: 161 us
  starting transfers between devices  55.6 us (35%)
  blocking collectives  46 us (29%)
  waiting for transfers between devices  42.8 us (27%)
  Pallas kernels  14.5 us (9%)
    all_to_all x1, waiting for transfers between devices, body(): lax.all_to_all(rows.reshape(256, 9, 2, 128), ('zh', 'x', 'y', 'zl'), 0, 0...  31.3 us
    all_to_all x1, starting transfers between devices, body(): lax.all_to_all(rows.reshape(256, 9, 2, 128), ('zh', 'x', 'y', 'zl'), 0, 0...  25.5 us
    all_gather x2, blocking collectives, body(): lax.all_gather(part, 'y', axis=0, tiled=True)  22.8 us
    ppermute x3, starting transfers between devices, swap_cores(): return lax.ppermute(x, 'core', [(0, 1), (1, 0)])  19.2 us
    all_to_all x1, waiting for transfers between devices, body(): found = jnp.min(lax.all_to_all(best, ('y', 'zl'), 0, 0, tiled=True), axis=0)  11.4 us
    all_gather x1, blocking collectives, body(): far = lax.all_gather(far, 'x', axis=0, tiled=True)  10.5 us
    all_gather x1, blocking collectives, body(): near = lax.all_gather(rounded, 'x', axis=0, tiled=True)  9.9 us
    all_to_all x1, starting transfers between devices, body(): found = jnp.min(lax.all_to_all(best, ('y', 'zl'), 0, 0, tiled=True), axis=0)  5.97 us
  transfers between devices with their start and end apart: 6, of which 3 were waited for; matrix products, arithmetic and copies ran while one was open for 0% of the time, Pallas kernels for 3%

profile of v8, /device:TPU:1, one launch (start us, length us, event | category | flops | bytes accessed | tf_op | source)
XLA Modules:
  0.0 160.6 jit_solution(1974749371323143104)
XLA Ops:
  0.6 5.8 %build.1 = (bf16[4608,128]{1,0:T(8,128)(2,1)}, bf16[512,256]{1,0:T(8,128)(2,1)}) custom-call(s32[1]{0:T(128)} %bitcast.core_ref, bf16[1024,256]{1,0:T(8,128)(2,1)} %latents_hbm.1, s32[1,1024]{1,0:T(1,128)} %order_hbm.1, s32[1,1024]{1,0:T(1,128)} %bitcast.15, s32[1,1024]{1,0:T(1,128)} %bitcast.16, bf16[1024,256]{1,0:T(8,128)(2,1)} %queries_hbm.1), custom_call_target="tpu_custom_call" | custom-call | flops 3221225472 | bytes 2097152 | tf_op jit(solution)/shard_map/build/pallas_call | solution.py:115
  6.5 0.0 copy-start.3
  6.5 25.5 %all-to-all-start = ((bf16[256,9,2,128]{3,2,1,0:T(2,128)(2,1)}), bf16[256,9,2,128]{3,2,1,0:T(2,128)(2,1)S(1)}, u32[]{:S(2)}, u32[]{:S(2)}) async-start(bf16[256,9,2,128]{3,2,1,0:T(2,128)(2,1)} %bitcast.12), calls=%async_computation | async-start | bytes 2359296 | tf_op jit(solution)/shard_map/all_to_all | solution.py:274
  32.0 0.0 copy-done.3
  32.0 11.5 %all_gather.15.low_ref = bf16[1024,256]{1,0:T(8,128)(2,1)S(1)} all-gather(bf16[256,256]{1,0:T(8,128)(2,1)S(1)} %get-tuple-element.16), channel_id=1, replica_groups=mesh['zh'=2,'x'=4,'y'=4,'zl'=8,'core'=2] {'y'}, dimensions={0}, use_global_device_ids=true | all-gather | bytes 655360 | tf_op jit(solution)/shard_map/all_gather | solution.py:272
  43.5 11.3 %all_gather.16.high_ref = bf16[1024,256]{1,0:T(8,128)(2,1)S(1)} all-gather(bf16[256,256]{1,0:T(8,128)(2,1)S(1)} %get-tuple-element.17), channel_id=1, replica_groups=mesh['zh'=2,'x'=4,'y'=4,'zl'=8,'core'=2] {'y'}, dimensions={0}, use_global_device_ids=true | all-gather | bytes 655360 | tf_op jit(solution)/shard_map/all_gather | solution.py:272
  54.8 31.3 %all-to-all-done = bf16[256,9,2,128]{3,2,1,0:T(2,128)(2,1)S(1)} async-done(((bf16[256,9,2,128]{3,2,1,0:T(2,128)(2,1)}), bf16[256,9,2,128]{3,2,1,0:T(2,128)(2,1)S(1)}, u32[]{:S(2)}, u32[]{:S(2)}) %all-to-all-start) | async-done | bytes 1179680 | tf_op jit(solution)/shard_map/all_to_all | solution.py:274
  86.1 1.0 partial.3
  87.1 0.0 copy-start
  87.1 0.0 copy-start.1
  87.1 8.0 %collective-permute-start = (f32[264,256]{1,0:T(8,128)S(1)}, f32[264,256]{1,0:T(8,128)S(1)}, u32[]{:S(2)}, u32[]{:S(2)}) collective-permute-start(f32[264,256]{1,0:T(8,128)S(1)} %partial.3), channel_id=1, source_target_pairs={{0,1},{1,0},{2,3},{3,2},{4,5},{5,4},{6,7},{7,6},{8,9},{9,8},{10,11... | collective-permute-start | bytes 811016 | tf_op jit(solution)/shard_map/ppermute | solution.py:257
  95.1 1.0 partial.2.own_ref
  96.1 0.2 collective-permute-done.other_ref
  96.3 0.0 copy-done
  96.3 0.0 copy-done.1
  96.3 0.8 merge.1
  97.1 5.0 %collective-permute-start.1 = (bf16[256,256]{1,0:T(8,128)(2,1)S(1)}, bf16[256,256]{1,0:T(8,128)(2,1)S(1)}, u32[]{:S(2)}, u32[]{:S(2)}) collective-permute-start(bf16[256,256]{1,0:T(8,128)(2,1)S(1)} %get-tuple-element.15), channel_id=1, source_target_pairs={{0,270},{2,268},{4,266},{6,264},{8,262},{10,260},{12,258},{14,256}... | collective-permute-start | bytes 393224 | tf_op jit(solution)/shard_map/ppermute | solution.py:280
  102.1 9.9 %all_gather.18.codes_ref = bf16[1024,256]{1,0:T(8,128)(2,1)S(1)} all-gather(bf16[256,256]{1,0:T(8,128)(2,1)S(1)} %get-tuple-element.15), channel_id=1, replica_groups=mesh['zh'=2,'x'=4,'y'=4,'zl'=8,'core'=2] {'x'}, dimensions={0}, use_global_device_ids=true | all-gather | bytes 655360 | tf_op jit(solution)/shard_map/all_gather | solution.py:281
  112.0 6.0 %collective-permute-start.3 = (bf16[1024,256]{1,0:T(8,128)(2,1)S(1)}, bf16[1024,256]{1,0:T(8,128)(2,1)S(1)}, u32[]{:S(2)}, u32[]{:S(2)}) collective-permute-start(bf16[1024,256]{1,0:T(8,128)(2,1)S(1)} %all_gather.18.codes_ref), channel_id=1, source_target_pairs={{0,1},{1,0},{2,3},{3,2},{4,5},{5,4},{6,7},{7,6},{8,9},{9,8},{10,11... | collective-permute-start | bytes 1572872 | tf_op jit(solution)/shard_map/ppermute | solution.py:257
  118.0 0.0 collective-permute-done.1
  118.0 10.5 %all_gather.17.codes_ref = bf16[1024,256]{1,0:T(8,128)(2,1)S(1)} all-gather(bf16[256,256]{1,0:T(8,128)(2,1)S(1)} %collective-permute-done.1), channel_id=1, replica_groups=mesh['zh'=2,'x'=4,'y'=4,'zl'=8,'core'=2] {'x'}, dimensions={0}, use_global_device_ids=true | all-gather | bytes 655360 | tf_op jit(solution)/shard_map/all_gather | solution.py:285
  128.5 5.1 %collective-permute-start.2 = (bf16[1024,256]{1,0:T(8,128)(2,1)S(1)}, bf16[1024,256]{1,0:T(8,128)(2,1)S(1)}, u32[]{:S(2)}, u32[]{:S(2)}) collective-permute-start(bf16[1024,256]{1,0:T(8,128)(2,1)S(1)} %all_gather.17.codes_ref), channel_id=1, source_target_pairs={{0,1},{1,0},{2,3},{3,2},{4,5},{5,4},{6,7},{7,6},{8,9},{9,8},{10,11... | collective-permute-start | bytes 1572872 | tf_op jit(solution)/shard_map/ppermute | solution.py:257
  133.7 1.3 nearest.4.refs_0_
  135.0 0.0 collective-permute-done.3.codes_ref
  135.0 1.3 nearest.5.refs_0_
  136.3 1.3 nearest.6.refs_0_
  137.6 0.0 copy-start.2
  137.7 0.0 collective-permute-done.2.codes_ref
  137.7 1.9 %nearest.7 = f32[32,4,128]{2,1,0:T(4,128)} custom-call(bf16[1024,256]{1,0:T(8,128)(2,1)S(1)} %collective-permute-done.2.codes_ref, bf16[1024,256]{1,0:T(8,128)(2,1)S(1)} %all_gather.15.low_ref, bf16[1024,256]{1,0:T(8,128)(2,1)S(1)} %all_gather.16.high_ref, f32[8,8,256]{2,1,0:T(8,128)S(1)} %nearest.6.refs_0_), custom_call_target="tpu_custom_call" | custom-call | flops 1073741824 | bytes 2097152 | tf_op jit(solution)/shard_map/nearest/pallas_call | solution.py:247
  139.6 6.0 %all-to-all-start.1 = ((f32[32,4,128]{2,1,0:T(4,128)}), f32[32,4,128]{2,1,0:T(4,128)S(1)}, u32[]{:S(2)}, u32[]{:S(2)}) async-start(f32[32,4,128]{2,1,0:T(4,128)} %nearest.7), calls=%async_computation.1 | async-start | bytes 131072 | tf_op jit(solution)/shard_map/all_to_all | solution.py:289
  145.6 0.0 copy-done.2
  145.6 0.2 multiply_reduce_fusion
  145.8 11.4 %all-to-all-done.1 = f32[32,4,128]{2,1,0:T(4,128)S(1)} async-done(((f32[32,4,128]{2,1,0:T(4,128)}), f32[32,4,128]{2,1,0:T(4,128)S(1)}, u32[]{:S(2)}, u32[]{:S(2)}) %all-to-all-start.1) | async-done | bytes 65568 | tf_op jit(solution)/shard_map/all_to_all | solution.py:289
  157.2 2.8 %all-gather = f32[2,4,128]{2,1,0:T(4,128)S(1)} all-gather(f32[1,4,128]{2,1,0:T(4,128)S(1)} %bitcast.14), channel_id=1, replica_groups=mesh['zh'=2,'x'=4,'y'=4,'zl'=8,'core'=2] {'core'}, dimensions={0}, use_global_device_ids=true | all-gather | bytes 6144 | tf_op jit(solution)/shard_map/all_gather | solution.py:290
  160.0 0.6 add_multiply_fusion
  (3 shorter events, 0.1 us)
Async XLA Ops:
  6.5 25.5 %copy-start.3 = (bf16[512,256]{1,0:T(8,128)(2,1)S(1)}, bf16[512,256]{1,0:T(8,128)(2,1)}, u32[]{:S(2)}) copy-start(bf16[512,256]{1,0:T(8,128)(2,1)} %get-tuple-element.11) | copy-start | bytes 786436
  6.5 79.6 %all-to-all-start = ((bf16[256,9,2,128]{3,2,1,0:T(2,128)(2,1)}), bf16[256,9,2,128]{3,2,1,0:T(2,128)(2,1)S(1)}, u32[]{:S(2)}, u32[]{:S(2)}) async-start(bf16[256,9,2,128]{3,2,1,0:T(2,128)(2,1)} %bitcast.12), calls=%async_computation | async-start | bytes 2359296 | tf_op jit(solution)/shard_map/all_to_all | solution.py:274
  87.1 9.2 %copy-start = (f32[256,256]{1,0:T(8,128)S(1)}, f32[256,256]{1,0:T(8,128)}, u32[]{:S(2)}) copy-start(f32[256,256]{1,0:T(8,128)} %sums_ref.1) | copy-start | bytes 786436
  87.1 9.2 %copy-start.1 = (f32[256]{0:T(256)S(1)}, f32[256]{0:T(256)}, u32[]{:S(2)}) copy-start(f32[256]{0:T(256)} %param.11) | copy-start | bytes 3076
  87.1 9.2 %collective-permute-start = (f32[264,256]{1,0:T(8,128)S(1)}, f32[264,256]{1,0:T(8,128)S(1)}, u32[]{:S(2)}, u32[]{:S(2)}) collective-permute-start(f32[264,256]{1,0:T(8,128)S(1)} %partial.3), channel_id=1, source_target_pairs={{0,1},{1,0},{2,3},{3,2},{4,5},{5,4},{6,7},{7,6},{8,9},{9,8},{10,11... | collective-permute-start | bytes 811016 | tf_op jit(solution)/shard_map/ppermute | solution.py:257
  97.1 20.9 %collective-permute-start.1 = (bf16[256,256]{1,0:T(8,128)(2,1)S(1)}, bf16[256,256]{1,0:T(8,128)(2,1)S(1)}, u32[]{:S(2)}, u32[]{:S(2)}) collective-permute-start(bf16[256,256]{1,0:T(8,128)(2,1)S(1)} %get-tuple-element.15), channel_id=1, source_target_pairs={{0,270},{2,268},{4,266},{6,264},{8,262},{10,260},{12,258},{14,256}... | collective-permute-start | bytes 393224 | tf_op jit(solution)/shard_map/ppermute | solution.py:280
  112.0 23.0 %collective-permute-start.3 = (bf16[1024,256]{1,0:T(8,128)(2,1)S(1)}, bf16[1024,256]{1,0:T(8,128)(2,1)S(1)}, u32[]{:S(2)}, u32[]{:S(2)}) collective-permute-start(bf16[1024,256]{1,0:T(8,128)(2,1)S(1)} %all_gather.18.codes_ref), channel_id=1, source_target_pairs={{0,1},{1,0},{2,3},{3,2},{4,5},{5,4},{6,7},{7,6},{8,9},{9,8},{10,11... | collective-permute-start | bytes 1572872 | tf_op jit(solution)/shard_map/ppermute | solution.py:257
  128.5 9.1 %collective-permute-start.2 = (bf16[1024,256]{1,0:T(8,128)(2,1)S(1)}, bf16[1024,256]{1,0:T(8,128)(2,1)S(1)}, u32[]{:S(2)}, u32[]{:S(2)}) collective-permute-start(bf16[1024,256]{1,0:T(8,128)(2,1)S(1)} %all_gather.17.codes_ref), channel_id=1, source_target_pairs={{0,1},{1,0},{2,3},{3,2},{4,5},{5,4},{6,7},{7,6},{8,9},{9,8},{10,11... | collective-permute-start | bytes 1572872 | tf_op jit(solution)/shard_map/ppermute | solution.py:257
  137.6 7.9 %copy-start.2 = (bf16[1024,256]{1,0:T(8,128)(2,1)S(1)}, bf16[1024,256]{1,0:T(8,128)(2,1)}, u32[]{:S(2)}) copy-start(bf16[1024,256]{1,0:T(8,128)(2,1)} %queries_hbm.1) | copy-start | bytes 1572868
  139.6 17.6 %all-to-all-start.1 = ((f32[32,4,128]{2,1,0:T(4,128)}), f32[32,4,128]{2,1,0:T(4,128)S(1)}, u32[]{:S(2)}, u32[]{:S(2)}) async-start(f32[32,4,128]{2,1,0:T(4,128)} %nearest.7), calls=%async_computation.1 | async-start | bytes 131072 | tf_op jit(solution)/shard_map/all_to_all | solution.py:289

commit v9 on v8

--- a/solution.py
+++ b/solution.py
@@ -14,8 +14,8 @@
 SLOTS = STEPS * CAP
 ema_decay = 0.9
 
-AXES = ("zh", "x", "y", "zl", "core")
-SIZES = (2, 4, 4, 8, 2)
+AXES = ("zh", "xa", "xb", "y", "zl", "core")
+SIZES = (2, 2, 2, 4, 8, 2)
 NT = (((1,), (1,)), ((), ()))
 
 f32 = jnp.float32
@@ -213,19 +213,20 @@
     )(own, other, counts.reshape(1, CPD), sums)
 
 
-def nearest_kernel(codes_ref, low_ref, high_ref, *refs):
-    out_ref = refs[-1]
-    last = out_ref.shape == (32, 4, 128)
+def nearest_kernel(side_ref, codes_ref, *refs):
+    queries_refs, out_ref = refs[:4], refs[-1]
+    last = out_ref.shape == (64, 4, 128)
     scaled, norms = [], []
     for c in range(codes_ref.shape[0] // CPD):
         part = codes_ref[c * CPD : (c + 1) * CPD].astype(f32)
         norms.append(jnp.sum(part * part, axis=1, keepdims=True))
         scaled.append((-2.0 * part).astype(bf16))
-    for y in range(4):
+    for g in range(8):
+        other, y = g // 4, g % 4
         lines = []
-        for h, queries_ref in enumerate((low_ref, high_ref)):
-            part = queries_ref[y * 256 : (y + 1) * 256]
-            best = refs[0][2 * y + h] if len(refs) > 1 else None
+        for h in range(2):
+            part = queries_refs[2 * other + h][y * 256 : (y + 1) * 256]
+            best = refs[4][2 * g + h] if last else None
             for m, n in zip(scaled, norms):
                 value = lax.dot_general(m, part, NT, preferred_element_type=f32) + n
                 value = jnp.min(value.reshape(CPD // 8, 8, 256), axis=0)
@@ -234,21 +235,25 @@
                 line = jnp.min(best, axis=0, keepdims=True)
                 lines += [line[:, :128], line[:, 128:]]
             else:
-                out_ref[2 * y + h] = best
+                out_ref[2 * g + h] = best
         if last:
             lines = jnp.concatenate(lines, axis=0)
+            at = (side_ref[0] ^ other) * 32 + y * 8
             for z in range(8):
-                out_ref[y * 8 + z] = lines
-
-
-def nearest_codes(codes, queries, best=None, last=False):
-    shape = (32, 4, 128) if last else (8, 8, 256)
-    operands = (codes, *queries) if best is None else (codes, *queries, best)
+                out_ref[at + z] = lines
+
+
+def nearest_codes(side, codes, queries, best=None):
+    shape = (16, 8, 256) if best is None else (64, 4, 128)
+    operands = (side, codes, *queries) if best is None else (side, codes, *queries, best)
+    vmem = pl.BlockSpec(memory_space=pltpu.VMEM)
     return pl.pallas_call(
         nearest_kernel,
         out_shape=jax.ShapeDtypeStruct(shape, f32),
+        in_specs=[pl.BlockSpec(memory_space=pltpu.SMEM)] + [vmem] * (len(operands) - 1),
+        out_specs=vmem,
         compiler_params=pltpu.CompilerParams(vmem_limit_bytes=32 << 20),
-        cost_estimate=pl.CostEstimate(flops=1 << 30, bytes_accessed=2 << 20, transcendentals=0),
+        cost_estimate=pl.CostEstimate(flops=2 << 30, bytes_accessed=4 << 20, transcendentals=0),
         name="nearest",
     )(*operands)
 
@@ -268,25 +273,24 @@
         code_offset.reshape(1, -1),
         queries,
     )
+    across = lax.ppermute(mine, "xa", [(0, 1), (1, 0)])
     row_queries = [
-        lax.all_gather(part, "y", axis=0, tiled=True) for part in (mine[:256], mine[256:])
+        lax.all_gather(part, "y", axis=0, tiled=True)
+        for part in (mine[:256], mine[256:], across[:256], across[256:])
     ]
-    got = lax.all_to_all(rows.reshape(256, 9, 2, 128), ("zh", "x", "y", "zl"), 0, 0, tiled=True)
+    side = lax.axis_index("xa").astype(i32).reshape(1)
+    got = lax.all_to_all(rows.reshape(256, 9, 2, 128), ("zh", "xa", "xb", "y", "zl"), 0, 0, tiled=True)
     got = got.reshape(256 * 18, 128)
-    arrived = row_queries[0][:16] + row_queries[1][:16]
+    arrived = (row_queries[0][:16] + row_queries[1][:16]) + (row_queries[2][:16] + row_queries[3][:16])
     other_part = swap_cores(partial_update(1, got, arrived))
     own_part = partial_update(0, got, arrived)
     codebook, counts, sums, rounded = merge(own_part, other_part, ema_counts, ema_sums)
     far = lax.ppermute(rounded, ("zh", "zl"), [(z, 15 - z) for z in range(16)])
-    near = lax.all_gather(rounded, "x", axis=0, tiled=True)
-    near_other = swap_cores(near)
-    best = nearest_codes(near, row_queries)
-    best = nearest_codes(near_other, row_queries, best)
-    far = lax.all_gather(far, "x", axis=0, tiled=True)
-    far_other = swap_cores(far)
-    best = nearest_codes(far, row_queries, best)
-    best = nearest_codes(far_other, row_queries, best, last=True)
-    found = jnp.min(lax.all_to_all(best, ("y", "zl"), 0, 0, tiled=True), axis=0)
+    near = lax.all_gather(rounded, ("xb", "core"), axis=0, tiled=True)
+    best = nearest_codes(side, near, row_queries)
+    far = lax.all_gather(far, ("xb", "core"), axis=0, tiled=True)
+    best = nearest_codes(side, far, row_queries, best)
+    found = jnp.min(lax.all_to_all(best, ("xa", "y", "zl"), 0, 0, tiled=True), axis=0)
     found = lax.all_gather(found, "core", axis=0, tiled=True).reshape(-1)
     nearest = (own + found) / E
     return (codebook, counts.reshape(-1), sums, nearest)
@@ -301,12 +305,12 @@
         P(AXES),
         P(AXES),
         P(AXES, None),
-        P(("zh", "x", "y"), None),
+        P(("zh", "xa", "xb", "y"), None),
     )
     return jax.shard_map(
         body,
         mesh=fine,
         in_specs=placed,
-        out_specs=(P(AXES, None), P(AXES), P(AXES, None), P(("zh", "x", "y"))),
+        out_specs=(P(AXES, None), P(AXES), P(AXES, None), P(("zh", "xa", "xb", "y"))),
         check_vma=False,
     )

time: 161 us -> 158 us (0.981)
  waiting for transfers between devices: 42.8 us -> 17.1 us
  blocking collectives: 46 us -> 67 us
    all_to_all x2, waiting for transfers between devices: 42.6 us -> 15.9 us  [the longest x1 12.7 us: body(): lax.all_to_all(best, ('xa', 'y', 'zl'), 0, 0, tiled=True)]
    all_gather x2 -> x4, blocking collectives: 22.8 us -> 47.5 us  [body(): lax.all_gather(part, 'y', axis=0, tiled=True)]
    ppermute x3 -> x1, starting transfers between devices: 19.2 us -> 7.87 us  [swap_cores(): return lax.ppermute(x, 'core', [(0, 1), (1, 0)])]
    all_to_all x2, starting transfers between devices: 31.5 us -> 39.5 us  [the longest x1 25.5 us: body(): lax.all_to_all(rows.reshape(256, 9, 2, 128), ('zh', 'xa', 'xb', 'y', 'zl'...]
    all_gather x2, blocking collectives: 20.4 us -> 15.1 us  [the longest x1 7.68 us: body(): far = lax.all_gather(far, ('xb', 'core'), axis=0, tiled=True)]
    ppermute x0 -> x1, starting transfers between devices: none -> 3.43 us  [body(): across = lax.ppermute(mine, 'xa', [(0, 1), (1, 0)])]
    pallas_call x4 -> x2, Pallas kernels: 5.9 us -> 5.48 us  [nearest_codes(): pl.pallas_call(nearest_kernel, out_shape=jax.ShapeDtypeStruct(shape, f32)...]
  transfers between devices with their start and end apart: 6 -> 5, of which waited for: 3 -> 4; matrix products, arithmetic and copies ran while one was open for 0% -> 1% of each run, Pallas kernels for 3% -> 2%
where the time goes in v9:
time: 158 us
  blocking collectives  67 us (42%)
  starting transfers between devices  56.2 us (36%)
  waiting for transfers between devices  17.1 us (11%)
  Pallas kernels  14.8 us (9%)
  other arithmetic  1.93 us (1%)
    all_gather x4, blocking collectives, body(): lax.all_gather(part, 'y', axis=0, tiled=True)  47.5 us
    all_to_all x1, starting transfers between devices, body(): lax.all_to_all(rows.reshape(256, 9, 2, 128), ('zh', 'xa', 'xb', 'y', 'zl'...  25.5 us
    all_to_all x1, starting transfers between devices, body(): lax.all_to_all(best, ('xa', 'y', 'zl'), 0, 0, tiled=True)  14 us
    all_to_all x1, waiting for transfers between devices, body(): lax.all_to_all(best, ('xa', 'y', 'zl'), 0, 0, tiled=True)  12.7 us
    ppermute x1, starting transfers between devices, swap_cores(): return lax.ppermute(x, 'core', [(0, 1), (1, 0)])  7.87 us
    all_gather x1, blocking collectives, body(): far = lax.all_gather(far, ('xb', 'core'), axis=0, tiled=True)  7.68 us
    all_gather x1, blocking collectives, body(): near = lax.all_gather(rounded, ('xb', 'core'), axis=0, tiled=True)  7.47 us
    pallas_call x1, Pallas kernels, build(): pl.pallas_call(build_kernel, out_shape=(jax.ShapeDtypeStruct((256 * 18, 1...  5.83 us
  transfers between devices with their start and end apart: 5, of which 4 were waited for; matrix products, arithmetic and copies ran while one was open for 1% of the time, Pallas kernels for 2%

profile of v9, /device:TPU:1, one launch (start us, length us, event | category | flops | bytes accessed | tf_op | source)
XLA Modules:
  0.0 157.8 jit_solution(13078933841912268883)
XLA Ops:
  0.6 5.8 %build.1 = (bf16[4608,128]{1,0:T(8,128)(2,1)}, bf16[512,256]{1,0:T(8,128)(2,1)}) custom-call(s32[1]{0:T(128)} %bitcast.core_ref, bf16[1024,256]{1,0:T(8,128)(2,1)} %latents_hbm.1, s32[1,1024]{1,0:T(1,128)} %order_hbm.1, s32[1,1024]{1,0:T(1,128)} %bitcast.16, s32[1,1024]{1,0:T(1,128)} %bitcast.17, bf16[1024,256]{1,0:T(8,128)(2,1)} %queries_hbm.1), custom_call_target="tpu_custom_call" | custom-call | flops 3221225472 | bytes 2097152 | tf_op jit(solution)/shard_map/build/pallas_call | solution.py:115
  6.5 0.0 copy-start.2
  6.5 25.5 %all-to-all-start = ((bf16[256,9,2,128]{3,2,1,0:T(2,128)(2,1)}), bf16[256,9,2,128]{3,2,1,0:T(2,128)(2,1)S(1)}, u32[]{:S(2)}, u32[]{:S(2)}) async-start(bf16[256,9,2,128]{3,2,1,0:T(2,128)(2,1)} %bitcast.13), calls=%async_computation | async-start | bytes 2359296 | tf_op jit(solution)/shard_map/all_to_all | solution.py:282
  32.0 0.0 copy-done.2
  32.0 3.4 %collective-permute-start = (bf16[512,256]{1,0:T(8,128)(2,1)S(1)}, bf16[512,256]{1,0:T(8,128)(2,1)S(1)}, u32[]{:S(2)}, u32[]{:S(2)}) collective-permute-start(bf16[512,256]{1,0:T(8,128)(2,1)S(1)} %copy-done.2), channel_id=1, source_target_pairs={{0,128},{128,0},{1,129},{129,1},{2,130},{130,2},{3,131},{131,3},{4... | collective-permute-start | bytes 786440 | tf_op jit(solution)/shard_map/ppermute | solution.py:276
  35.4 12.6 %all_gather.22.refs_1_ = bf16[1024,256]{1,0:T(8,128)(2,1)S(1)} all-gather(bf16[256,256]{1,0:T(8,128)(2,1)S(1)} %get-tuple-element.17), channel_id=1, replica_groups=mesh['zh'=2,'xa'=2,'xb'=2,'y'=4,'zl'=8,'core'=2] {'y'}, dimensions={0}, use_global_device_ids=true | all-gather | bytes 655360 | tf_op jit(solution)/shard_map/all_gather | solution.py:278
  48.0 11.3 %all_gather.21.refs_0_ = bf16[1024,256]{1,0:T(8,128)(2,1)S(1)} all-gather(bf16[256,256]{1,0:T(8,128)(2,1)S(1)} %get-tuple-element.16), channel_id=1, replica_groups=mesh['zh'=2,'xa'=2,'xb'=2,'y'=4,'zl'=8,'core'=2] {'y'}, dimensions={0}, use_global_device_ids=true | all-gather | bytes 655360 | tf_op jit(solution)/shard_map/all_gather | solution.py:278
  59.4 0.0 collective-permute-done
  59.4 12.0 %all_gather.24.refs_3_ = bf16[1024,256]{1,0:T(8,128)(2,1)S(1)} all-gather(bf16[256,256]{1,0:T(8,128)(2,1)S(1)} %get-tuple-element.19), channel_id=1, replica_groups=mesh['zh'=2,'xa'=2,'xb'=2,'y'=4,'zl'=8,'core'=2] {'y'}, dimensions={0}, use_global_device_ids=true | all-gather | bytes 655360 | tf_op jit(solution)/shard_map/all_gather | solution.py:278
  71.4 11.5 %all_gather.23.refs_2_ = bf16[1024,256]{1,0:T(8,128)(2,1)S(1)} all-gather(bf16[256,256]{1,0:T(8,128)(2,1)S(1)} %get-tuple-element.18), channel_id=1, replica_groups=mesh['zh'=2,'xa'=2,'xb'=2,'y'=4,'zl'=8,'core'=2] {'y'}, dimensions={0}, use_global_device_ids=true | all-gather | bytes 655360 | tf_op jit(solution)/shard_map/all_gather | solution.py:278
  82.9 3.2 %all-to-all-done = bf16[256,9,2,128]{3,2,1,0:T(2,128)(2,1)S(1)} async-done(((bf16[256,9,2,128]{3,2,1,0:T(2,128)(2,1)}), bf16[256,9,2,128]{3,2,1,0:T(2,128)(2,1)S(1)}, u32[]{:S(2)}, u32[]{:S(2)}) %all-to-all-start) | async-done | bytes 1179680 | tf_op jit(solution)/shard_map/all_to_all | solution.py:282
  86.1 1.7 %partial.3 = f32[264,256]{1,0:T(8,128)} custom-call(bf16[4608,128]{1,0:T(8,128)(2,1)S(1)} %bitcast.10, bf16[16,256]{1,0:T(8,128)(2,1)S(1)} %fusion.queries_ref), custom_call_target="tpu_custom_call" | custom-call | flops 536870912 | bytes 2097152 | tf_op jit(solution)/shard_map/partial/pallas_call | solution.py:178
  87.8 7.9 %collective-permute-start.1 = (f32[264,256]{1,0:T(8,128)}, f32[264,256]{1,0:T(8,128)S(1)}, u32[]{:S(2)}, u32[]{:S(2)}) collective-permute-start(f32[264,256]{1,0:T(8,128)} %partial.3), channel_id=1, source_target_pairs={{0,1},{1,0},{2,3},{3,2},{4,5},{5,4},{6,7},{7,6},{8,9},{9,8},{10,11... | collective-permute-start | bytes 811016 | tf_op jit(solution)/shard_map/ppermute | solution.py:262
  95.7 0.0 copy-start
  95.7 0.0 copy-start.1
  95.7 1.0 partial.2.own_ref
  96.7 0.3 collective-permute-done.1.other_ref
  97.0 0.0 copy-done
  97.0 0.0 copy-done.1
  97.0 0.9 merge.1
  97.9 5.4 %collective-permute-start.2 = (bf16[256,256]{1,0:T(8,128)(2,1)S(1)}, bf16[256,256]{1,0:T(8,128)(2,1)S(1)}, u32[]{:S(2)}, u32[]{:S(2)}) collective-permute-start(bf16[256,256]{1,0:T(8,128)(2,1)S(1)} %get-tuple-element.15), channel_id=1, source_target_pairs={{0,270},{2,268},{4,266},{6,264},{8,262},{10,260},{12,258},{14,256}... | collective-permute-start | bytes 393224 | tf_op jit(solution)/shard_map/ppermute | solution.py:288
  103.3 7.5 %all_gather.26.codes_ref = bf16[1024,256]{1,0:T(8,128)(2,1)S(1)} all-gather(bf16[256,256]{1,0:T(8,128)(2,1)S(1)} %get-tuple-element.15), channel_id=1, replica_groups=mesh['zh'=2,'xa'=2,'xb'=2,'y'=4,'zl'=8,'core'=2] {'xb','core'}, dimensions={0}, use_global_device_ids=true | all-gather | bytes 655360 | tf_op jit(solution)/shard_map/all_gather | solution.py:289
  110.8 2.4 %nearest.2.refs_4_ = f32[16,8,256]{2,1,0:T(8,128)S(1)} custom-call(s32[1]{0:T(128)} %bitcast.7.side_ref, bf16[1024,256]{1,0:T(8,128)(2,1)S(1)} %all_gather.26.codes_ref, bf16[1024,256]{1,0:T(8,128)(2,1)S(1)} %all_gather.21.refs_0_, bf16[1024,256]{1,0:T(8,128)(2,1)S(1)} %all_gather.22.refs_1_, bf16[1024,256]{1,0:T(8,128)(2,1)S(1)} %all_gather.23.refs_2_, ...), custom_call_target="tpu_custom_call" | custom-call | flops 2147483648 | bytes 4194304 | tf_op jit(solution)/shard_map/nearest/pallas_call | solution.py:250
  113.2 0.9 collective-permute-done.2
  114.1 7.7 %all_gather.25.codes_ref = bf16[1024,256]{1,0:T(8,128)(2,1)S(1)} all-gather(bf16[256,256]{1,0:T(8,128)(2,1)S(1)} %collective-permute-done.2), channel_id=1, replica_groups=mesh['zh'=2,'xa'=2,'xb'=2,'y'=4,'zl'=8,'core'=2] {'xb','core'}, dimensions={0}, use_global_device_ids=true | all-gather | bytes 655360 | tf_op jit(solution)/shard_map/all_gather | solution.py:291
  121.7 3.1 %nearest.3 = f32[64,4,128]{2,1,0:T(4,128)} custom-call(s32[1]{0:T(128)} %bitcast.7.side_ref, bf16[1024,256]{1,0:T(8,128)(2,1)S(1)} %all_gather.25.codes_ref, bf16[1024,256]{1,0:T(8,128)(2,1)S(1)} %all_gather.21.refs_0_, bf16[1024,256]{1,0:T(8,128)(2,1)S(1)} %all_gather.22.refs_1_, bf16[1024,256]{1,0:T(8,128)(2,1)S(1)} %all_gather.23.refs_2_, ...), custom_call_target="tpu_custom_call" | custom-call | flops 2147483648 | bytes 4194304 | tf_op jit(solution)/shard_map/nearest/pallas_call | solution.py:250
  124.8 14.0 %all-to-all-start.1 = ((f32[64,4,128]{2,1,0:T(4,128)}), f32[64,4,128]{2,1,0:T(4,128)S(1)}, u32[]{:S(2)}, u32[]{:S(2)}) async-start(f32[64,4,128]{2,1,0:T(4,128)} %nearest.3), calls=%async_computation.1 | async-start | bytes 262144 | tf_op jit(solution)/shard_map/all_to_all | solution.py:293
  138.8 1.3 multiply_reduce_fusion
  140.1 12.7 %all-to-all-done.1 = f32[64,4,128]{2,1,0:T(4,128)S(1)} async-done(((f32[64,4,128]{2,1,0:T(4,128)}), f32[64,4,128]{2,1,0:T(4,128)S(1)}, u32[]{:S(2)}, u32[]{:S(2)}) %all-to-all-start.1) | async-done | bytes 131104 | tf_op jit(solution)/shard_map/all_to_all | solution.py:293
  152.8 0.1 reduce_min.9
  152.8 4.4 %all-gather = f32[2,4,128]{2,1,0:T(4,128)S(1)} all-gather(f32[1,4,128]{2,1,0:T(4,128)S(1)} %bitcast.15), channel_id=1, replica_groups=mesh['zh'=2,'xa'=2,'xb'=2,'y'=4,'zl'=8,'core'=2] {'core'}, dimensions={0}, use_global_device_ids=true | all-gather | bytes 6144 | tf_op jit(solution)/shard_map/all_gather | solution.py:294
  157.2 0.6 add_multiply_fusion
  (3 shorter events, 0.0 us)
Async XLA Ops:
  6.5 25.5 %copy-start.2 = (bf16[512,256]{1,0:T(8,128)(2,1)S(1)}, bf16[512,256]{1,0:T(8,128)(2,1)}, u32[]{:S(2)}) copy-start(bf16[512,256]{1,0:T(8,128)(2,1)} %get-tuple-element.11) | copy-start | bytes 786436
  6.5 79.6 %all-to-all-start = ((bf16[256,9,2,128]{3,2,1,0:T(2,128)(2,1)}), bf16[256,9,2,128]{3,2,1,0:T(2,128)(2,1)S(1)}, u32[]{:S(2)}, u32[]{:S(2)}) async-start(bf16[256,9,2,128]{3,2,1,0:T(2,128)(2,1)} %bitcast.13), calls=%async_computation | async-start | bytes 2359296 | tf_op jit(solution)/shard_map/all_to_all | solution.py:282
  32.0 27.4 %collective-permute-start = (bf16[512,256]{1,0:T(8,128)(2,1)S(1)}, bf16[512,256]{1,0:T(8,128)(2,1)S(1)}, u32[]{:S(2)}, u32[]{:S(2)}) collective-permute-start(bf16[512,256]{1,0:T(8,128)(2,1)S(1)} %copy-done.2), channel_id=1, source_target_pairs={{0,128},{128,0},{1,129},{129,1},{2,130},{130,2},{3,131},{131,3},{4... | collective-permute-start | bytes 786440 | tf_op jit(solution)/shard_map/ppermute | solution.py:276
  87.8 9.2 %collective-permute-start.1 = (f32[264,256]{1,0:T(8,128)}, f32[264,256]{1,0:T(8,128)S(1)}, u32[]{:S(2)}, u32[]{:S(2)}) collective-permute-start(f32[264,256]{1,0:T(8,128)} %partial.3), channel_id=1, source_target_pairs={{0,1},{1,0},{2,3},{3,2},{4,5},{5,4},{6,7},{7,6},{8,9},{9,8},{10,11... | collective-permute-start | bytes 811016 | tf_op jit(solution)/shard_map/ppermute | solution.py:262
  95.7 1.4 copy-start
  95.7 1.4 copy-start.1
  97.9 16.2 %collective-permute-start.2 = (bf16[256,256]{1,0:T(8,128)(2,1)S(1)}, bf16[256,256]{1,0:T(8,128)(2,1)S(1)}, u32[]{:S(2)}, u32[]{:S(2)}) collective-permute-start(bf16[256,256]{1,0:T(8,128)(2,1)S(1)} %get-tuple-element.15), channel_id=1, source_target_pairs={{0,270},{2,268},{4,266},{6,264},{8,262},{10,260},{12,258},{14,256}... | collective-permute-start | bytes 393224 | tf_op jit(solution)/shard_map/ppermute | solution.py:288
  124.8 28.0 %all-to-all-start.1 = ((f32[64,4,128]{2,1,0:T(4,128)}), f32[64,4,128]{2,1,0:T(4,128)S(1)}, u32[]{:S(2)}, u32[]{:S(2)}) async-start(f32[64,4,128]{2,1,0:T(4,128)} %nearest.3), calls=%async_computation.1 | async-start | bytes 262144 | tf_op jit(solution)/shard_map/all_to_all | solution.py:293

commit v10 on v8

--- a/solution.py
+++ b/solution.py
@@ -14,8 +14,8 @@
 SLOTS = STEPS * CAP
 ema_decay = 0.9
 
-AXES = ("zh", "x", "y", "zl", "core")
-SIZES = (2, 4, 4, 8, 2)
+AXES = ("zh", "xa", "xb", "y", "zl", "core")
+SIZES = (2, 2, 2, 4, 8, 2)
 NT = (((1,), (1,)), ((), ()))
 
 f32 = jnp.float32
@@ -215,7 +215,7 @@
 
 def nearest_kernel(codes_ref, low_ref, high_ref, *refs):
     out_ref = refs[-1]
-    last = out_ref.shape == (32, 4, 128)
+    last = out_ref.shape == (4, 4, 128)
     scaled, norms = [], []
     for c in range(codes_ref.shape[0] // CPD):
         part = codes_ref[c * CPD : (c + 1) * CPD].astype(f32)
@@ -236,13 +236,11 @@
             else:
                 out_ref[2 * y + h] = best
         if last:
-            lines = jnp.concatenate(lines, axis=0)
-            for z in range(8):
-                out_ref[y * 8 + z] = lines
+            out_ref[y] = jnp.concatenate(lines, axis=0)
 
 
 def nearest_codes(codes, queries, best=None, last=False):
-    shape = (32, 4, 128) if last else (8, 8, 256)
+    shape = (4, 4, 128) if last else (8, 8, 256)
     operands = (codes, *queries) if best is None else (codes, *queries, best)
     return pl.pallas_call(
         nearest_kernel,
@@ -268,24 +266,27 @@
         code_offset.reshape(1, -1),
         queries,
     )
+    across = lax.ppermute(mine, "xa", [(0, 1), (1, 0)])
     row_queries = [
-        lax.all_gather(part, "y", axis=0, tiled=True) for part in (mine[:256], mine[256:])
+        lax.all_gather(part, "y", axis=0, tiled=True)
+        for part in (mine[:256], mine[256:], across[:256], across[256:])
     ]
-    got = lax.all_to_all(rows.reshape(256, 9, 2, 128), ("zh", "x", "y", "zl"), 0, 0, tiled=True)
+    got = lax.all_to_all(rows.reshape(256, 9, 2, 128), ("zh", "xa", "xb", "y", "zl"), 0, 0, tiled=True)
     got = got.reshape(256 * 18, 128)
-    arrived = row_queries[0][:16] + row_queries[1][:16]
+    arrived = (row_queries[0][:16] + row_queries[1][:16]) + (row_queries[2][:16] + row_queries[3][:16])
     other_part = swap_cores(partial_update(1, got, arrived))
     own_part = partial_update(0, got, arrived)
     codebook, counts, sums, rounded = merge(own_part, other_part, ema_counts, ema_sums)
     far = lax.ppermute(rounded, ("zh", "zl"), [(z, 15 - z) for z in range(16)])
-    near = lax.all_gather(rounded, "x", axis=0, tiled=True)
-    near_other = swap_cores(near)
-    best = nearest_codes(near, row_queries)
-    best = nearest_codes(near_other, row_queries, best)
-    far = lax.all_gather(far, "x", axis=0, tiled=True)
-    far_other = swap_cores(far)
-    best = nearest_codes(far, row_queries, best)
-    best = nearest_codes(far_other, row_queries, best, last=True)
+    near = lax.all_gather(rounded, ("xb", "core"), axis=0, tiled=True)
+    own_best = nearest_codes(near, row_queries[:2])
+    across_best = nearest_codes(near, row_queries[2:])
+    far = lax.all_gather(far, ("xb", "core"), axis=0, tiled=True)
+    across_best = nearest_codes(far, row_queries[2:], across_best, last=True)
+    returned = lax.ppermute(across_best, "xa", [(0, 1), (1, 0)])
+    own_best = nearest_codes(far, row_queries[:2], own_best, last=True)
+    best = jnp.minimum(own_best, returned)
+    best = jnp.broadcast_to(best[:, None], (4, 8, 4, 128)).reshape(32, 4, 128)
     found = jnp.min(lax.all_to_all(best, ("y", "zl"), 0, 0, tiled=True), axis=0)
     found = lax.all_gather(found, "core", axis=0, tiled=True).reshape(-1)
     nearest = (own + found) / E
@@ -301,12 +302,12 @@
         P(AXES),
         P(AXES),
         P(AXES, None),
-        P(("zh", "x", "y"), None),
+        P(("zh", "xa", "xb", "y"), None),
     )
     return jax.shard_map(
         body,
         mesh=fine,
         in_specs=placed,
-        out_specs=(P(AXES, None), P(AXES), P(AXES, None), P(("zh", "x", "y"))),
+        out_specs=(P(AXES, None), P(AXES), P(AXES, None), P(("zh", "xa", "xb", "y"))),
         check_vma=False,
     )

time: 161 us -> 159 us (0.988)
  waiting for transfers between devices: 42.8 us -> 15.3 us
  blocking collectives: 46 us -> 66.8 us
  starting transfers between devices: 55.6 us -> 60 us
    all_to_all x1, waiting for transfers between devices: 31.3 us -> 3.21 us  [body(): lax.all_to_all(rows.reshape(256, 9, 2, 128), ('zh', 'xa', 'xb', 'y', 'zl'...]
    all_gather x2 -> x4, blocking collectives: 22.8 us -> 47.4 us  [body(): lax.all_gather(part, 'y', axis=0, tiled=True)]
    ppermute x3 -> x1, starting transfers between devices: 19.2 us -> 8.01 us  [swap_cores(): return lax.ppermute(x, 'core', [(0, 1), (1, 0)])]
    ppermute x0 -> x2, starting transfers between devices: none -> 10.1 us  [the longest x1 6.63 us: body(): returned = lax.ppermute(across_best, 'xa', [(0, 1), (1, 0)])]
    all_gather x2, blocking collectives: 20.4 us -> 15.1 us  [the longest x1 7.68 us: body(): far = lax.all_gather(far, ('xb', 'core'), axis=0, tiled=True)]
    all_to_all x1, starting transfers between devices: 5.97 us -> 11 us  [body(): found = jnp.min(lax.all_to_all(best, ('y', 'zl'), 0, 0, tiled=True), axis=0)]
  transfers between devices with their start and end apart: 6 -> 6, of which waited for: 3 -> 4; matrix products, arithmetic and copies ran while one was open for 0% -> 0% of each run, Pallas kernels for 3% -> 3%
where the time goes in v10:
time: 159 us; the launch traced here: 158 us
  blocking collectives  66.8 us (42%)
  starting transfers between devices  60 us (38%)
  waiting for transfers between devices  15.3 us (10%)
  Pallas kernels  13.9 us (9%)
    all_gather x4, blocking collectives, body(): lax.all_gather(part, 'y', axis=0, tiled=True)  47.4 us
    all_to_all x1, starting transfers between devices, body(): lax.all_to_all(rows.reshape(256, 9, 2, 128), ('zh', 'xa', 'xb', 'y', 'zl'...  25.5 us
    all_to_all x1, waiting for transfers between devices, body(): found = jnp.min(lax.all_to_all(best, ('y', 'zl'), 0, 0, tiled=True), axis=0)  11.3 us
    all_to_all x1, starting transfers between devices, body(): found = jnp.min(lax.all_to_all(best, ('y', 'zl'), 0, 0, tiled=True), axis=0)  11 us
    ppermute x1, starting transfers between devices, swap_cores(): return lax.ppermute(x, 'core', [(0, 1), (1, 0)])  8.01 us
    all_gather x1, blocking collectives, body(): far = lax.all_gather(far, ('xb', 'core'), axis=0, tiled=True)  7.68 us
    all_gather x1, blocking collectives, body(): near = lax.all_gather(rounded, ('xb', 'core'), axis=0, tiled=True)  7.47 us
    ppermute x1, starting transfers between devices, body(): returned = lax.ppermute(across_best, 'xa', [(0, 1), (1, 0)])  6.63 us
  transfers between devices with their start and end apart: 6, of which 4 were waited for; matrix products, arithmetic and copies ran while one was open for 0% of the time, Pallas kernels for 3%

profile of v10, /device:TPU:1, one launch (start us, length us, event | category | flops | bytes accessed | tf_op | source)
XLA Modules:
  0.0 158.3 jit_solution(10050956991727226362)
XLA Ops:
  0.6 5.8 %build.1 = (bf16[4608,128]{1,0:T(8,128)(2,1)}, bf16[512,256]{1,0:T(8,128)(2,1)}) custom-call(s32[1]{0:T(128)} %bitcast.core_ref, bf16[1024,256]{1,0:T(8,128)(2,1)} %latents_hbm.1, s32[1,1024]{1,0:T(1,128)} %order_hbm.1, s32[1,1024]{1,0:T(1,128)} %bitcast.16, s32[1,1024]{1,0:T(1,128)} %bitcast.17, bf16[1024,256]{1,0:T(8,128)(2,1)} %queries_hbm.1), custom_call_target="tpu_custom_call" | custom-call | flops 3221225472 | bytes 2097152 | tf_op jit(solution)/shard_map/build/pallas_call | solution.py:115
  6.5 0.0 copy-start.3
  6.5 25.5 %all-to-all-start = ((bf16[256,9,2,128]{3,2,1,0:T(2,128)(2,1)}), bf16[256,9,2,128]{3,2,1,0:T(2,128)(2,1)S(1)}, u32[]{:S(2)}, u32[]{:S(2)}) async-start(bf16[256,9,2,128]{3,2,1,0:T(2,128)(2,1)} %bitcast.13), calls=%async_computation | async-start | bytes 2359296 | tf_op jit(solution)/shard_map/all_to_all | solution.py:274
  32.0 0.0 copy-done.3
  32.0 3.4 %collective-permute-start = (bf16[512,256]{1,0:T(8,128)(2,1)S(1)}, bf16[512,256]{1,0:T(8,128)(2,1)S(1)}, u32[]{:S(2)}, u32[]{:S(2)}) collective-permute-start(bf16[512,256]{1,0:T(8,128)(2,1)S(1)} %copy-done.3), channel_id=1, source_target_pairs={{0,128},{128,0},{1,129},{129,1},{2,130},{130,2},{3,131},{131,3},{4... | collective-permute-start | bytes 786440 | tf_op jit(solution)/shard_map/ppermute | solution.py:269
  35.4 12.6 %all_gather.22.high_ref = bf16[1024,256]{1,0:T(8,128)(2,1)S(1)} all-gather(bf16[256,256]{1,0:T(8,128)(2,1)S(1)} %get-tuple-element.17), channel_id=1, replica_groups=mesh['zh'=2,'xa'=2,'xb'=2,'y'=4,'zl'=8,'core'=2] {'y'}, dimensions={0}, use_global_device_ids=true | all-gather | bytes 655360 | tf_op jit(solution)/shard_map/all_gather | solution.py:271
  48.0 11.3 %all_gather.21.low_ref = bf16[1024,256]{1,0:T(8,128)(2,1)S(1)} all-gather(bf16[256,256]{1,0:T(8,128)(2,1)S(1)} %get-tuple-element.16), channel_id=1, replica_groups=mesh['zh'=2,'xa'=2,'xb'=2,'y'=4,'zl'=8,'core'=2] {'y'}, dimensions={0}, use_global_device_ids=true | all-gather | bytes 655360 | tf_op jit(solution)/shard_map/all_gather | solution.py:271
  59.3 0.0 collective-permute-done
  59.3 12.0 %all_gather.24.high_ref = bf16[1024,256]{1,0:T(8,128)(2,1)S(1)} all-gather(bf16[256,256]{1,0:T(8,128)(2,1)S(1)} %get-tuple-element.19), channel_id=1, replica_groups=mesh['zh'=2,'xa'=2,'xb'=2,'y'=4,'zl'=8,'core'=2] {'y'}, dimensions={0}, use_global_device_ids=true | all-gather | bytes 655360 | tf_op jit(solution)/shard_map/all_gather | solution.py:271
  71.4 11.5 %all_gather.23.low_ref = bf16[1024,256]{1,0:T(8,128)(2,1)S(1)} all-gather(bf16[256,256]{1,0:T(8,128)(2,1)S(1)} %get-tuple-element.18), channel_id=1, replica_groups=mesh['zh'=2,'xa'=2,'xb'=2,'y'=4,'zl'=8,'core'=2] {'y'}, dimensions={0}, use_global_device_ids=true | all-gather | bytes 655360 | tf_op jit(solution)/shard_map/all_gather | solution.py:271
  82.9 3.2 %all-to-all-done = bf16[256,9,2,128]{3,2,1,0:T(2,128)(2,1)S(1)} async-done(((bf16[256,9,2,128]{3,2,1,0:T(2,128)(2,1)}), bf16[256,9,2,128]{3,2,1,0:T(2,128)(2,1)S(1)}, u32[]{:S(2)}, u32[]{:S(2)}) %all-to-all-start) | async-done | bytes 1179680 | tf_op jit(solution)/shard_map/all_to_all | solution.py:274
  86.1 1.0 partial.3
  87.1 0.0 copy-start
  87.1 0.0 copy-start.1
  87.1 8.0 %collective-permute-start.1 = (f32[264,256]{1,0:T(8,128)S(1)}, f32[264,256]{1,0:T(8,128)S(1)}, u32[]{:S(2)}, u32[]{:S(2)}) collective-permute-start(f32[264,256]{1,0:T(8,128)S(1)} %partial.3), channel_id=1, source_target_pairs={{0,1},{1,0},{2,3},{3,2},{4,5},{5,4},{6,7},{7,6},{8,9},{9,8},{10,11... | collective-permute-start | bytes 811016 | tf_op jit(solution)/shard_map/ppermute | solution.py:255
  95.1 1.0 partial.2.own_ref
  96.1 0.2 collective-permute-done.1.other_ref
  96.3 0.0 copy-done
  96.3 0.0 copy-done.1
  96.3 0.9 merge.1
  97.1 5.4 %collective-permute-start.2 = (bf16[256,256]{1,0:T(8,128)(2,1)S(1)}, bf16[256,256]{1,0:T(8,128)(2,1)S(1)}, u32[]{:S(2)}, u32[]{:S(2)}) collective-permute-start(bf16[256,256]{1,0:T(8,128)(2,1)S(1)} %get-tuple-element.15), channel_id=1, source_target_pairs={{0,270},{2,268},{4,266},{6,264},{8,262},{10,260},{12,258},{14,256}... | collective-permute-start | bytes 393224 | tf_op jit(solution)/shard_map/ppermute | solution.py:280
  102.5 7.5 %all_gather.26.codes_ref = bf16[1024,256]{1,0:T(8,128)(2,1)S(1)} all-gather(bf16[256,256]{1,0:T(8,128)(2,1)S(1)} %get-tuple-element.15), channel_id=1, replica_groups=mesh['zh'=2,'xa'=2,'xb'=2,'y'=4,'zl'=8,'core'=2] {'xb','core'}, dimensions={0}, use_global_device_ids=true | all-gather | bytes 655360 | tf_op jit(solution)/shard_map/all_gather | solution.py:281
  110.0 1.3 nearest.4.refs_0_
  111.3 1.3 nearest.6.refs_0_
  112.7 0.7 collective-permute-done.2
  113.3 7.7 %all_gather.25.codes_ref = bf16[1024,256]{1,0:T(8,128)(2,1)S(1)} all-gather(bf16[256,256]{1,0:T(8,128)(2,1)S(1)} %collective-permute-done.2), channel_id=1, replica_groups=mesh['zh'=2,'xa'=2,'xb'=2,'y'=4,'zl'=8,'core'=2] {'xb','core'}, dimensions={0}, use_global_device_ids=true | all-gather | bytes 655360 | tf_op jit(solution)/shard_map/all_gather | solution.py:284
  121.0 1.3 nearest.7
  122.3 0.0 copy-start.2
  122.3 6.6 %collective-permute-start.3 = (f32[4,4,128]{2,1,0:T(4,128)S(1)}, f32[4,4,128]{2,1,0:T(4,128)S(1)}, u32[]{:S(2)}, u32[]{:S(2)}) collective-permute-start(f32[4,4,128]{2,1,0:T(4,128)S(1)} %nearest.7), channel_id=1, source_target_pairs={{0,128},{128,0},{1,129},{129,1},{2,130},{130,2},{3,131},{131,3},{4... | collective-permute-start | bytes 24584 | tf_op jit(solution)/shard_map/ppermute | solution.py:286
  129.0 1.3 nearest.5
  130.3 0.0 collective-permute-done.3
  130.3 0.6 broadcast_in_dim.2
  131.0 11.0 %all-to-all-start.1 = ((f32[32,4,128]{2,1,0:T(4,128)}), f32[32,4,128]{2,1,0:T(4,128)S(1)}, u32[]{:S(2)}, u32[]{:S(2)}) async-start(f32[32,4,128]{2,1,0:T(4,128)} %bitcast.7), calls=%async_computation.1 | async-start | bytes 131072 | tf_op jit(solution)/shard_map/all_to_all | solution.py:290
  142.0 0.0 copy-done.2
  142.0 0.2 multiply_reduce_fusion
  142.2 11.3 %all-to-all-done.1 = f32[32,4,128]{2,1,0:T(4,128)S(1)} async-done(((f32[32,4,128]{2,1,0:T(4,128)}), f32[32,4,128]{2,1,0:T(4,128)S(1)}, u32[]{:S(2)}, u32[]{:S(2)}) %all-to-all-start.1) | async-done | bytes 65568 | tf_op jit(solution)/shard_map/all_to_all | solution.py:290
  153.5 4.2 %all-gather = f32[2,4,128]{2,1,0:T(4,128)S(1)} all-gather(f32[1,4,128]{2,1,0:T(4,128)S(1)} %bitcast.15), channel_id=1, replica_groups=mesh['zh'=2,'xa'=2,'xb'=2,'y'=4,'zl'=8,'core'=2] {'core'}, dimensions={0}, use_global_device_ids=true | all-gather | bytes 6144 | tf_op jit(solution)/shard_map/all_gather | solution.py:291
  157.8 0.6 add_multiply_fusion
  (5 shorter events, 0.1 us)
Async XLA Ops:
  6.5 25.5 %copy-start.3 = (bf16[512,256]{1,0:T(8,128)(2,1)S(1)}, bf16[512,256]{1,0:T(8,128)(2,1)}, u32[]{:S(2)}) copy-start(bf16[512,256]{1,0:T(8,128)(2,1)} %get-tuple-element.11) | copy-start | bytes 786436
  6.5 79.6 %all-to-all-start = ((bf16[256,9,2,128]{3,2,1,0:T(2,128)(2,1)}), bf16[256,9,2,128]{3,2,1,0:T(2,128)(2,1)S(1)}, u32[]{:S(2)}, u32[]{:S(2)}) async-start(bf16[256,9,2,128]{3,2,1,0:T(2,128)(2,1)} %bitcast.13), calls=%async_computation | async-start | bytes 2359296 | tf_op jit(solution)/shard_map/all_to_all | solution.py:274
  32.0 27.4 %collective-permute-start = (bf16[512,256]{1,0:T(8,128)(2,1)S(1)}, bf16[512,256]{1,0:T(8,128)(2,1)S(1)}, u32[]{:S(2)}, u32[]{:S(2)}) collective-permute-start(bf16[512,256]{1,0:T(8,128)(2,1)S(1)} %copy-done.3), channel_id=1, source_target_pairs={{0,128},{128,0},{1,129},{129,1},{2,130},{130,2},{3,131},{131,3},{4... | collective-permute-start | bytes 786440 | tf_op jit(solution)/shard_map/ppermute | solution.py:269
  87.1 9.2 %copy-start = (f32[256,256]{1,0:T(8,128)S(1)}, f32[256,256]{1,0:T(8,128)}, u32[]{:S(2)}) copy-start(f32[256,256]{1,0:T(8,128)} %sums_ref.1) | copy-start | bytes 786436
  87.1 9.2 %copy-start.1 = (f32[256]{0:T(256)S(1)}, f32[256]{0:T(256)}, u32[]{:S(2)}) copy-start(f32[256]{0:T(256)} %param.11) | copy-start | bytes 3076
  87.1 9.2 %collective-permute-start.1 = (f32[264,256]{1,0:T(8,128)S(1)}, f32[264,256]{1,0:T(8,128)S(1)}, u32[]{:S(2)}, u32[]{:S(2)}) collective-permute-start(f32[264,256]{1,0:T(8,128)S(1)} %partial.3), channel_id=1, source_target_pairs={{0,1},{1,0},{2,3},{3,2},{4,5},{5,4},{6,7},{7,6},{8,9},{9,8},{10,11... | collective-permute-start | bytes 811016 | tf_op jit(solution)/shard_map/ppermute | solution.py:255
  97.1 16.2 %collective-permute-start.2 = (bf16[256,256]{1,0:T(8,128)(2,1)S(1)}, bf16[256,256]{1,0:T(8,128)(2,1)S(1)}, u32[]{:S(2)}, u32[]{:S(2)}) collective-permute-start(bf16[256,256]{1,0:T(8,128)(2,1)S(1)} %get-tuple-element.15), channel_id=1, source_target_pairs={{0,270},{2,268},{4,266},{6,264},{8,262},{10,260},{12,258},{14,256}... | collective-permute-start | bytes 393224 | tf_op jit(solution)/shard_map/ppermute | solution.py:280
  122.3 19.7 %copy-start.2 = (bf16[1024,256]{1,0:T(8,128)(2,1)S(1)}, bf16[1024,256]{1,0:T(8,128)(2,1)}, u32[]{:S(2)}) copy-start(bf16[1024,256]{1,0:T(8,128)(2,1)} %queries_hbm.1) | copy-start | bytes 1572868
  122.3 8.0 %collective-permute-start.3 = (f32[4,4,128]{2,1,0:T(4,128)S(1)}, f32[4,4,128]{2,1,0:T(4,128)S(1)}, u32[]{:S(2)}, u32[]{:S(2)}) collective-permute-start(f32[4,4,128]{2,1,0:T(4,128)S(1)} %nearest.7), channel_id=1, source_target_pairs={{0,128},{128,0},{1,129},{129,1},{2,130},{130,2},{3,131},{131,3},{4... | collective-permute-start | bytes 24584 | tf_op jit(solution)/shard_map/ppermute | solution.py:286
  131.0 22.5 %all-to-all-start.1 = ((f32[32,4,128]{2,1,0:T(4,128)}), f32[32,4,128]{2,1,0:T(4,128)S(1)}, u32[]{:S(2)}, u32[]{:S(2)}) async-start(f32[32,4,128]{2,1,0:T(4,128)} %bitcast.7), calls=%async_computation.1 | async-start | bytes 131072 | tf_op jit(solution)/shard_map/all_to_all | solution.py:290
